TPU v7x, 128 devices: a whole 4x4x4 slice. The times are simulated.
128 devices in a mesh: dp: 8 (over y, x_lo), seq: 16 (over z, x_hi, core).
Axes of the slice: x: 4 (x_hi: 2, x_lo: 2; x = x_hi * 2 + x_lo), y: 4, z: 4, core: 2. Of those that a mesh axis runs over, the one named last changes fastest.
Arguments:
- tokens: bfloat16 [16384, 1024], P(('dp', 'seq')), may hold values from -6 to 6
- segment_ids: int32 [8, 2048], P('dp', 'seq'), may hold values from 0 to 7, never falling along the last dimension, each value on 1 to 1024 neighbouring positions
- attn_gain: bfloat16 [1024], P('dp'), may hold values from 0.5 to 1.5
- w_query: bfloat16 [1024, 1024], P('dp'), may hold values from -0.1875 to 0.1875
- w_key: bfloat16 [1024, 512], P('dp'), may hold values from -0.1875 to 0.1875
- w_value: bfloat16 [1024, 512], P('dp'), may hold values from -0.1875 to 0.1875
- w_out: bfloat16 [1024, 1024], P('dp'), may hold values from -1 to 1
- ffn_gain: bfloat16 [1024], P('dp'), may hold values from 0.5 to 1.5
- w_gate: bfloat16 [1024, 4608], P('dp'), may hold values from -0.1875 to 0.1875
- w_up: bfloat16 [1024, 4608], P('dp'), may hold values from -0.1875 to 0.1875
- w_down: bfloat16 [4608, 1024], P('dp'), may hold values from -0.09375 to 0.09375
- query_gain: bfloat16 [64], replicated, may hold values from 0.25 to 1.75
- key_gain: bfloat16 [64], replicated, may hold values from 0.25 to 1.75
- cotangent: bfloat16 [16384, 1024], P(('dp', 'seq')), may hold values from -6 to 6
Outputs:
- block_out: bfloat16 [16384, 1024], P(('dp', 'seq'))
- input_grad: bfloat16 [16384, 1024], P(('dp', 'seq'))
- grad_attn_gain: float32 [1024], P('dp')
- grad_w_query: float32 [1024, 1024], P('dp')
- grad_w_key: float32 [1024, 512], P('dp')
- grad_w_value: float32 [1024, 512], P('dp')
- grad_w_out: float32 [1024, 1024], P('dp')
- grad_ffn_gain: float32 [1024], P('dp')
- grad_w_gate: float32 [1024, 4608], P('dp')
- grad_w_up: float32 [1024, 4608], P('dp')
- grad_w_down: float32 [4608, 1024], P('dp')
- grad_query_gain: float32 [64], replicated
- grad_key_gain: float32 [64], replicated
Inputs may be any that keep to these rules, and one draw needn't show every extreme that they name: `segment_ids`: in each sequence the document numbers never fall along the tokens; each of the 8 documents has 1 to 1024 tokens and one has exactly 1024.
All inputs are finite; a program needn't handle non-finite values.
Results may differ from a plain program's by a relative error of at most 0.025.
Values may be sent and summed in bfloat16 or wider, within the bound.
A program may use at most 192 MiB of HBM per device.

v0:
```python
import jax
import jax.numpy as jnp
from jax import lax
from jax.sharding import PartitionSpec as P

HEADS = 16
KVH = 8
HD = 64


EPSILON = 1e-05
ROPE_BASE = 1000000.0


def norm_rows(values, gain_vec):
    factor = lax.rsqrt(jnp.mean(values * values, axis=-1, keepdims=True) + EPSILON)
    return (values * factor * gain_vec, factor)


def norm_back(grad_in, values, factor, gain_vec):
    weighted = grad_in * gain_vec
    return factor * weighted - values * (factor * factor * factor) * jnp.mean(
        weighted * values, axis=-1, keepdims=True
    )


def rotate(values, cosine_table, sine_table):
    half_size = values.shape[-1] // 2
    first_half = values[..., :half_size]
    second_half = values[..., half_size:]
    return jnp.concatenate(
        [
            first_half * cosine_table - second_half * sine_table,
            second_half * cosine_table + first_half * sine_table,
        ],
        axis=-1,
    )


def unrotate(grads_in, cosine_table, sine_table):
    half_size = grads_in.shape[-1] // 2
    first_half = grads_in[..., :half_size]
    second_half = grads_in[..., half_size:]
    return jnp.concatenate(
        [
            first_half * cosine_table + second_half * sine_table,
            second_half * cosine_table - first_half * sine_table,
        ],
        axis=-1,
    )


def rope_tables(positions, head_size):
    half_size = head_size // 2
    inverse = ROPE_BASE ** (-(jnp.arange(half_size).astype(jnp.float32) * 2.0 / head_size))
    angles = positions[:, None] * inverse[None, :]
    return (jnp.cos(angles)[:, None, :], jnp.sin(angles)[:, None, :])


def over_rows(left_side, right_side):
    return lax.dot_general(
        left_side, right_side, (((0,), (0,)), ((), ())), preferred_element_type=jnp.float32
    )


def over_cols(left_side, right_side):
    return lax.dot_general(
        left_side, right_side, (((1,), (1,)), ((), ())), preferred_element_type=jnp.float32
    )


def local(
    tokens,
    segment_ids,
    attn_gain,
    w_query,
    w_key,
    w_value,
    w_out,
    ffn_gain,
    w_gate,
    w_up,
    w_down,
    query_gain,
    key_gain,
    cotangent,
):
    tok_rows = tokens.shape[0]
    seq_devices = lax.axis_size("seq")
    local_heads = HEADS // seq_devices
    copies = seq_devices // KVH
    query_cols = local_heads * HD
    gain_one, query_full, key_full, value_full, out_full = (
        lax.all_gather(attn_gain, "dp", axis=0, tiled=True),
        lax.all_gather(w_query, "dp", axis=0, tiled=True),
        lax.all_gather(w_key, "dp", axis=0, tiled=True),
        lax.all_gather(w_value, "dp", axis=0, tiled=True),
        lax.all_gather(w_out, "dp", axis=0, tiled=True),
    )
    doc_all = lax.all_gather(segment_ids, "seq", axis=1, tiled=True)[0]
    seq_length = doc_all.shape[0]
    doc_own = segment_ids[0]
    offset = lax.axis_index("seq") * tok_rows
    begins = jnp.sum((doc_all[None, :] < doc_own[:, None]).astype(jnp.int32), axis=1)
    positions = (offset + jnp.arange(tok_rows, dtype=jnp.int32) - begins).astype(jnp.float32)
    cosine_table, sine_table = rope_tables(positions, HD)
    inputs = tokens.astype(jnp.float32)
    normed, factor_one = norm_rows(inputs, gain_one.astype(jnp.float32))
    hidden = normed.astype(jnp.bfloat16)
    queries = jnp.dot(hidden, query_full, preferred_element_type=jnp.float32).reshape(
        tok_rows, HEADS, HD
    )
    keys_raw = jnp.dot(hidden, key_full, preferred_element_type=jnp.float32).reshape(
        tok_rows, KVH, HD
    )
    values_raw = jnp.dot(hidden, value_full, preferred_element_type=jnp.float32).reshape(
        tok_rows, KVH, HD
    )
    query_normed, query_factor = norm_rows(queries, query_gain.astype(jnp.float32))
    key_normed, key_factor = norm_rows(keys_raw, key_gain.astype(jnp.float32))
    query_rot = rotate(query_normed, cosine_table, sine_table).astype(jnp.bfloat16)
    key_rot = rotate(key_normed, cosine_table, sine_table).astype(jnp.bfloat16)
    key_value = jnp.concatenate([key_rot, values_raw.astype(jnp.bfloat16)], axis=-1)
    packed = jnp.concatenate([query_rot, jnp.repeat(key_value, copies, axis=1)], axis=-1)
    arrived = lax.all_to_all(packed, "seq", split_axis=1, concat_axis=0, tiled=True)[:, 0]
    head_queries = arrived[:, :query_cols].reshape(seq_length, local_heads, HD)
    head_keys = arrived[:, query_cols : query_cols + HD]
    head_values = arrived[:, query_cols + HD :]
    block_rows = min(512, seq_length)
    block_count = seq_length // block_rows
    factor = HD ** (-0.5)
    key_index = jnp.arange(seq_length, dtype=jnp.int32)
    starts = jnp.arange(block_count, dtype=jnp.int32) * block_rows

    def masked_scores(row_start):
        query_block = lax.dynamic_slice_in_dim(head_queries, row_start, block_rows, 0)
        block_ids = lax.dynamic_slice_in_dim(doc_all, row_start, block_rows, 0)
        rows_index = row_start + jnp.arange(block_rows, dtype=jnp.int32)
        allowed = (block_ids[:, None] == doc_all[None, :]) & (
            key_index[None, :] <= rows_index[:, None]
        )
        raw_scores = (
            jnp.einsum("qhd,kd->hqk", query_block, head_keys, preferred_element_type=jnp.float32)
            * factor
        )
        return (query_block, jnp.where(allowed[None], raw_scores, -1e30))

    def forward_block(row_start):
        query_block, scores = masked_scores(row_start)
        row_max = jnp.max(scores, axis=-1, keepdims=True)
        weights = jnp.exp(scores - row_max)
        row_total = jnp.sum(weights, axis=-1, keepdims=True)
        softmax_out = (weights / row_total).astype(jnp.bfloat16)
        attended = jnp.einsum(
            "hqk,kd->qhd", softmax_out, head_values, preferred_element_type=jnp.float32
        )
        return (attended.astype(jnp.bfloat16), (row_max + jnp.log(row_total))[..., 0])

    block_outs, log_totals = lax.map(forward_block, starts)
    head_out = block_outs.reshape(seq_length, query_cols)
    attended_tok = lax.all_to_all(head_out, "seq", split_axis=0, concat_axis=1, tiled=True)
    middle = inputs + jnp.dot(attended_tok, out_full, preferred_element_type=jnp.float32)
    gain_two, gate_full, up_full, down_full = (
        lax.all_gather(ffn_gain, "dp", axis=0, tiled=True),
        lax.all_gather(w_gate, "dp", axis=0, tiled=True),
        lax.all_gather(w_up, "dp", axis=0, tiled=True),
        lax.all_gather(w_down, "dp", axis=0, tiled=True),
    )
    normed_two, factor_two = norm_rows(middle, gain_two.astype(jnp.float32))
    hidden_two = normed_two.astype(jnp.bfloat16)
    gate_pre = jnp.dot(hidden_two, gate_full, preferred_element_type=jnp.float32)
    up_pre = jnp.dot(hidden_two, up_full, preferred_element_type=jnp.float32)
    gate_sig = jax.nn.sigmoid(gate_pre)
    activation = gate_pre * gate_sig
    mixed_act = (activation * up_pre).astype(jnp.bfloat16)
    block_out = (middle + jnp.dot(mixed_act, down_full, preferred_element_type=jnp.float32)).astype(
        jnp.bfloat16
    )
    gain_two, gate_full, up_full, down_full = (
        lax.all_gather(ffn_gain, "dp", axis=0, tiled=True),
        lax.all_gather(w_gate, "dp", axis=0, tiled=True),
        lax.all_gather(w_up, "dp", axis=0, tiled=True),
        lax.all_gather(w_down, "dp", axis=0, tiled=True),
    )
    upstream = cotangent.astype(jnp.float32)
    grad_down = over_rows(mixed_act, cotangent)
    grad_mixed = over_cols(cotangent, down_full)
    grad_gate_pre = (grad_mixed * up_pre * gate_sig * (1.0 + gate_pre * (1.0 - gate_sig))).astype(
        jnp.bfloat16
    )
    grad_up_pre = (grad_mixed * activation).astype(jnp.bfloat16)
    grad_gate = over_rows(hidden_two, grad_gate_pre)
    grad_up = over_rows(hidden_two, grad_up_pre)
    grad_hidden_two = over_cols(grad_gate_pre, gate_full) + over_cols(grad_up_pre, up_full)
    grad_gain_two = jnp.sum(grad_hidden_two * middle * factor_two, axis=0)
    grad_middle = upstream + norm_back(
        grad_hidden_two, middle, factor_two, gain_two.astype(jnp.float32)
    )
    grad_branch = grad_middle.astype(jnp.bfloat16)
    grad_out = over_rows(attended_tok, grad_branch)
    gain_one, query_full, key_full, value_full, out_full = (
        lax.all_gather(attn_gain, "dp", axis=0, tiled=True),
        lax.all_gather(w_query, "dp", axis=0, tiled=True),
        lax.all_gather(w_key, "dp", axis=0, tiled=True),
        lax.all_gather(w_value, "dp", axis=0, tiled=True),
        lax.all_gather(w_out, "dp", axis=0, tiled=True),
    )
    grad_attended = over_cols(grad_branch, out_full).astype(jnp.bfloat16)
    grad_heads = lax.all_to_all(
        grad_attended.reshape(tok_rows, seq_devices, query_cols),
        "seq",
        split_axis=1,
        concat_axis=0,
        tiled=True,
    )[:, 0].reshape(seq_length, local_heads, HD)

    def backward_block(carried, scan_item):
        row_start, log_block = scan_item
        query_block, scores = masked_scores(row_start)
        softmax_f = jnp.exp(scores - log_block[..., None])
        softmax_out = softmax_f.astype(jnp.bfloat16)
        grad_block = lax.dynamic_slice_in_dim(grad_heads, row_start, block_rows, 0)
        grad_probs = jnp.einsum(
            "qhd,kd->hqk", grad_block, head_values, preferred_element_type=jnp.float32
        )
        row_dot = jnp.sum(grad_probs * softmax_f, axis=-1, keepdims=True)
        grad_scores = (softmax_f * (grad_probs - row_dot)).astype(jnp.bfloat16)
        grad_query_block = (
            jnp.einsum("hqk,kd->qhd", grad_scores, head_keys, preferred_element_type=jnp.float32)
            * factor
        )
        grad_keys = (
            carried[0]
            + jnp.einsum(
                "hqk,qhd->kd", grad_scores, query_block, preferred_element_type=jnp.float32
            )
            * factor
        )
        grad_values = carried[1] + jnp.einsum(
            "hqk,qhd->kd", softmax_out, grad_block, preferred_element_type=jnp.float32
        )
        return ((grad_keys, grad_values), grad_query_block.astype(jnp.bfloat16))

    zero_keys = jnp.zeros((seq_length, HD), jnp.float32)
    (grad_keys, grad_values), grad_query_blocks = lax.scan(
        backward_block, (zero_keys, zero_keys), (starts, log_totals)
    )
    back_pack = jnp.concatenate(
        [
            grad_query_blocks.reshape(seq_length, query_cols),
            grad_keys.astype(jnp.bfloat16),
            grad_values.astype(jnp.bfloat16),
        ],
        axis=-1,
    )
    returned = lax.all_to_all(back_pack, "seq", split_axis=0, concat_axis=1, tiled=True).reshape(
        tok_rows, seq_devices, query_cols + 2 * HD
    )
    grad_query_rot = returned[..., :query_cols].astype(jnp.float32)
    grad_pair = (
        returned[..., query_cols:]
        .astype(jnp.float32)
        .reshape(tok_rows, KVH, copies, 2 * HD)
        .sum(axis=2)
    )
    grad_query_norm = unrotate(grad_query_rot, cosine_table, sine_table)
    grad_key_norm = unrotate(grad_pair[..., :HD], cosine_table, sine_table)
    grad_query_gain = jnp.sum(grad_query_norm * queries * query_factor, axis=(0, 1))
    grad_key_gain = jnp.sum(grad_key_norm * keys_raw * key_factor, axis=(0, 1))
    grad_queries = (
        norm_back(grad_query_norm, queries, query_factor, query_gain.astype(jnp.float32))
        .astype(jnp.bfloat16)
        .reshape(tok_rows, HEADS * HD)
    )
    grad_keys_raw = (
        norm_back(grad_key_norm, keys_raw, key_factor, key_gain.astype(jnp.float32))
        .astype(jnp.bfloat16)
        .reshape(tok_rows, KVH * HD)
    )
    grad_values_raw = grad_pair[..., HD:].astype(jnp.bfloat16).reshape(tok_rows, KVH * HD)
    grad_query = over_rows(hidden, grad_queries)
    grad_key = over_rows(hidden, grad_keys_raw)
    grad_value = over_rows(hidden, grad_values_raw)
    grad_hidden = (
        over_cols(grad_queries, query_full)
        + over_cols(grad_keys_raw, key_full)
        + over_cols(grad_values_raw, value_full)
    )
    grad_gain_one = jnp.sum(grad_hidden * inputs * factor_one, axis=0)
    input_grad = (
        grad_middle + norm_back(grad_hidden, inputs, factor_one, gain_one.astype(jnp.float32))
    ).astype(jnp.bfloat16)
    gradients = (
        grad_gain_one,
        grad_query,
        grad_key,
        grad_value,
        grad_out,
        grad_gain_two,
        grad_gate,
        grad_up,
        grad_down,
    )
    shards = (
        lax.psum_scatter(
            gradients[0].astype(jnp.bfloat16), "dp", scatter_dimension=0, tiled=True
        ).astype(jnp.float32),
        lax.psum_scatter(
            gradients[1].astype(jnp.bfloat16), "dp", scatter_dimension=0, tiled=True
        ).astype(jnp.float32),
        lax.psum_scatter(
            gradients[2].astype(jnp.bfloat16), "dp", scatter_dimension=0, tiled=True
        ).astype(jnp.float32),
        lax.psum_scatter(
            gradients[3].astype(jnp.bfloat16), "dp", scatter_dimension=0, tiled=True
        ).astype(jnp.float32),
        lax.psum_scatter(
            gradients[4].astype(jnp.bfloat16), "dp", scatter_dimension=0, tiled=True
        ).astype(jnp.float32),
        lax.psum_scatter(
            gradients[5].astype(jnp.bfloat16), "dp", scatter_dimension=0, tiled=True
        ).astype(jnp.float32),
        lax.psum_scatter(
            gradients[6].astype(jnp.bfloat16), "dp", scatter_dimension=0, tiled=True
        ).astype(jnp.float32),
        lax.psum_scatter(
            gradients[7].astype(jnp.bfloat16), "dp", scatter_dimension=0, tiled=True
        ).astype(jnp.float32),
        lax.psum_scatter(
            gradients[8].astype(jnp.bfloat16), "dp", scatter_dimension=0, tiled=True
        ).astype(jnp.float32),
    )
    shards = (
        lax.psum(shards[0].astype(jnp.bfloat16), "seq").astype(jnp.float32),
        lax.psum(shards[1].astype(jnp.bfloat16), "seq").astype(jnp.float32),
        lax.psum(shards[2].astype(jnp.bfloat16), "seq").astype(jnp.float32),
        lax.psum(shards[3].astype(jnp.bfloat16), "seq").astype(jnp.float32),
        lax.psum(shards[4].astype(jnp.bfloat16), "seq").astype(jnp.float32),
        lax.psum(shards[5].astype(jnp.bfloat16), "seq").astype(jnp.float32),
        lax.psum(shards[6].astype(jnp.bfloat16), "seq").astype(jnp.float32),
        lax.psum(shards[7].astype(jnp.bfloat16), "seq").astype(jnp.float32),
        lax.psum(shards[8].astype(jnp.bfloat16), "seq").astype(jnp.float32),
    )
    gain_sums = lax.psum((grad_query_gain, grad_key_gain), ("dp", "seq"))
    return (
        block_out,
        input_grad,
        shards[0],
        shards[1],
        shards[2],
        shards[3],
        shards[4],
        shards[5],
        shards[6],
        shards[7],
        shards[8],
        gain_sums[0],
        gain_sums[1],
    )


def solution(mesh):
    return jax.shard_map(
        local,
        mesh=mesh,
        in_specs=(
            P(("dp", "seq"), None),
            P("dp", "seq"),
            P("dp"),
            P("dp", None),
            P("dp", None),
            P("dp", None),
            P("dp", None),
            P("dp"),
            P("dp", None),
            P("dp", None),
            P("dp", None),
            P(),
            P(),
            P(("dp", "seq"), None),
        ),
        out_specs=(
            P(("dp", "seq"), None),
            P(("dp", "seq"), None),
            P("dp"),
            P("dp", None),
            P("dp", None),
            P("dp", None),
            P("dp", None),
            P("dp"),
            P("dp", None),
            P("dp", None),
            P("dp", None),
            P(),
            P(),
        ),
        check_vma=False,
    )
```

profile of v0, /device:TPU:25, one launch (start us, length us, event | category | flops | bytes accessed | tf_op | source)
XLA Modules:
  0.0 1863.1 jit_solution(2402109513291064083)
XLA Ops:
  12.0 11.6 all-gather
  23.7 29.1 %all_gather.39 = s32[1,2048]{1,0:T(1,128)S(1)} all-gather(s32[1,128]{1,0:T(1,128)S(1)} %copy-done.48), channel_id=1, replica_groups=mesh['dp'=8,'seq'=16] {'seq'}, dimensions={1}, use_global_device_ids=true | all-gather | bytes 8704 | tf_op jit(solution)/shard_map/all_gather | solution.py:100
  55.6 31.7 %all-gather.12.cloned.1.call-done = bf16[1024,512]{1,0:T(8,128)(2,1)} async-done(((bf16[128,512]{1,0:T(8,128)(2,1)}), bf16[1024,512]{1,0:T(8,128)(2,1)}) %all-gather.12.cloned.1.call-update) | async-done | bytes 1048592 | tf_op jit(solution)/shard_map/all_gather | solution.py:96
  89.3 56.1 %all-gather.10.cloned.1.call-done = bf16[1024,1024]{1,0:T(8,128)(2,1)} async-done(((bf16[128,1024]{1,0:T(8,128)(2,1)}), bf16[1024,1024]{1,0:T(8,128)(2,1)}) %all-gather.10.cloned.1.call-update) | async-done | bytes 2097168 | tf_op jit(solution)/shard_map/all_gather | solution.py:95
  145.4 2.1 fusion.66
  149.8 7.2 all-to-all-start
  157.1 22.8 %all-to-all-done = bf16[128,16,192]{0,2,1:T(8,128)(2,1)S(1)} async-done(((bf16[128,16,192]{0,2,1:T(8,128)(2,1)}), bf16[128,16,192]{0,2,1:T(8,128)(2,1)S(1)}, u32[]{:S(2)}, u32[]{:S(2)}) %all-to-all-start) | async-done | bytes 786464 | tf_op jit(solution)/shard_map/all_to_all | solution.py:125
  182.6 31.1 %while.28 = (s32[]{:T(128)}, bf16[4,512,1,64]{1,3,2,0:T(8,128)(2,1)S(1)}, f32[4,1,512]{2,1,0:T(1,128)S(1)}, s32[4]{0:T(128)S(1)}, s32[2048]{0:T(1024)S(1)}, /*in...) while((s32[]{:T(128)}, ...), condition=%wide.region_7.8_spmd.clone, body=%wide.region_4.7_spmd.clone.sunk | while | flops 280002560 | bytes 13801663 | solution.py:159
  185.9 2.7 fusion.139
  193.7 2.7 fusion.139
  201.5 2.7 fusion.139
  209.3 2.7 fusion.139
  214.9 4.3 all-to-all-start.1
  219.2 16.3 all-gather.1
  235.5 2.3 multiply_reduce_fusion.4
  237.9 162.3 %all-gather.18.cloned.1.call-done = bf16[1024,4608]{1,0:T(8,128)(2,1)} async-done(((bf16[128,4608]{1,0:T(8,128)(2,1)}), bf16[1024,4608]{1,0:T(8,128)(2,1)}) %all-gather.18.cloned.1.call-update) | async-done | bytes 9437200 | tf_op jit(solution)/shard_map/all_gather | solution.py:165
  400.1 6.5 fusion.70
  406.6 184.0 %all-gather.20.cloned.1.call-done = bf16[1024,4608]{1,0:T(8,128)(2,1)} async-done(((bf16[128,4608]{1,0:T(8,128)(2,1)}), bf16[1024,4608]{1,0:T(8,128)(2,1)}) %all-gather.20.cloned.1.call-update) | async-done | bytes 9437200 | tf_op jit(solution)/shard_map/all_gather | solution.py:166
  590.7 6.5 fusion.71
  597.2 184.2 %all-gather.22.cloned.1.call-done = bf16[4608,1024]{1,0:T(8,128)(2,1)} async-done(((bf16[576,1024]{1,0:T(8,128)(2,1)}), bf16[4608,1024]{1,0:T(8,128)(2,1)}) %all-gather.22.cloned.1.call-update) | async-done | bytes 9437200 | tf_op jit(solution)/shard_map/all_gather | solution.py:167
  781.4 9.7 multiply_convert_fusion
  791.1 7.7 fusion.72
  798.8 3.7 multiply_reduce_fusion.1
  804.4 7.5 all-to-all-start.2
  812.0 8.6 all-to-all-done.2
  822.0 71.9 %while.29 = (s32[]{:T(128)}, f32[2048,64]{0,1:T(8,128)}, f32[2048,64]{0,1:T(8,128)S(1)}, bf16[4,512,1,64]{1,3,2,0:T(8,128)(2,1)}, s32[4]{0:T(128)S(1)}, /*index=...) while((s32[]{:T(128)}, f32[2048,64]{0,1:T(8,128)}, ...), condition=%wide.region_12.13_spmd.clone, body=%wide.region_10.12_spmd.clone.sunk | while | flops 684392448 | bytes 51998984 | solution.py:245
  824.5 1.8 fusion.151
  827.0 3.3 fusion.152
  832.3 2.2 fusion.154
  834.6 2.8 convolution_add_fusion.7
  837.4 2.4 fusion.155
  844.8 3.3 fusion.152
  850.2 2.4 fusion.154
  852.6 2.8 convolution_add_fusion.7
  855.4 2.4 fusion.155
  862.9 3.3 fusion.152
  868.2 2.4 fusion.154
  870.6 2.8 convolution_add_fusion.7
  873.5 2.4 fusion.155
  880.9 3.3 fusion.152
  886.2 2.4 fusion.154
  888.6 2.8 convolution_add_fusion.7
  891.4 2.4 fusion.155
  896.6 4.5 all-to-all-start.3
  901.6 14.0 all-to-all-done.3
  918.5 2.2 convolution_convert_fusion.5
  920.9 2.0 convolution_convert_fusion.3
  928.1 2.1 convolution_convert_fusion.4
  930.3 5.2 convolution_convert_fusion.2
  936.8 5.1 convolution_convert_fusion.1
  943.2 5.1 convolution_convert_fusion
  950.0 42.3 %reduce-scatter.12.cloned.1.call-done = bf16[128,512]{1,0:T(8,128)(2,1)} async-done(((bf16[1024,512]{1,0:T(8,128)(2,1)}), bf16[128,512]{1,0:T(8,128)(2,1)}) %reduce-scatter.12.cloned.1.call-update) | async-done | bytes 131088 | tf_op jit(solution)/shard_map/reduce_scatter | solution.py:314
  992.3 59.2 %reduce-scatter.14.cloned.1.call-done = bf16[128,1024]{1,0:T(8,128)(2,1)} async-done(((bf16[1024,1024]{1,0:T(8,128)(2,1)}), bf16[128,1024]{1,0:T(8,128)(2,1)}) %reduce-scatter.14.cloned.1.call-update) | async-done | bytes 262160 | tf_op jit(solution)/shard_map/reduce_scatter | solution.py:317
  1051.5 54.7 %reduce-scatter.8.cloned.1.call-done = bf16[128,1024]{1,0:T(8,128)(2,1)} async-done(((bf16[1024,1024]{1,0:T(8,128)(2,1)}), bf16[128,1024]{1,0:T(8,128)(2,1)}) %reduce-scatter.8.cloned.1.call-update) | async-done | bytes 262160 | tf_op jit(solution)/shard_map/reduce_scatter | solution.py:308
  1106.2 192.1 %reduce-scatter.16.cloned.1.call-done = bf16[128,4608]{1,0:T(8,128)(2,1)} async-done(((bf16[1024,4608]{1,0:T(8,128)(2,1)}), bf16[128,4608]{1,0:T(8,128)(2,1)}) %reduce-scatter.16.cloned.1.call-update) | async-done | bytes 1179664 | tf_op jit(solution)/shard_map/reduce_scatter | solution.py:323
  1298.4 192.3 %reduce-scatter.18.cloned.1.call-done = bf16[128,4608]{1,0:T(8,128)(2,1)} async-done(((bf16[1024,4608]{1,0:T(8,128)(2,1)}), bf16[128,4608]{1,0:T(8,128)(2,1)}) %reduce-scatter.18.cloned.1.call-update) | async-done | bytes 1179664 | tf_op jit(solution)/shard_map/reduce_scatter | solution.py:326
  1490.7 192.2 %reduce-scatter.20.cloned.1.call-done = bf16[576,1024]{1,0:T(8,128)(2,1)} async-done(((bf16[4608,1024]{1,0:T(8,128)(2,1)}), bf16[576,1024]{1,0:T(8,128)(2,1)}) %reduce-scatter.20.cloned.1.call-update) | async-done | bytes 1179664 | tf_op jit(solution)/shard_map/reduce_scatter | solution.py:329
  1684.2 5.9 fusion.47
  1692.4 12.1 all-reduce.5
  1704.7 37.0 %all-reduce.3 = (bf16[128]{0:T(256)(128)(2,1)S(1)}, bf16[128]{0:T(256)(128)(2,1)S(1)}) all-reduce(bf16[128]{0:T(256)(128)(2,1)S(1)} %dynamic-slice.1, bf16[128]{0:T(256)(128)(2,1)S(1)} %dynamic-slice.3), channel_id=1, replica_groups=mesh['dp'=8,'seq'=16] {'seq'}, use_global_device_ids=true, to_apply=%region_19.20 | all-reduce | flops 256 | bytes 1024 | tf_op jit(solution)/shard_map/psum | solution.py:334
  1742.9 69.5 %all-reduce.2 = (f32[64]{0:T(128)}, f32[64]{0:T(128)}) all-reduce(f32[64]{0:T(128)S(1)} %reduce_sum.172, f32[64]{0:T(128)S(1)} %reduce_sum.175), channel_id=1, replica_groups=mesh['dp'=8,'seq'=16] {'dp','seq'}, use_global_device_ids=true, to_apply=%region_39.40 | all-reduce | flops 128 | bytes 1024 | tf_op jit(solution)/shard_map/psum | solution.py:344
  1813.4 30.7 %all-reduce.8.cloned.1.call-done = (bf16[128,1024]{1,0:T(8,128)(2,1)}, bf16[128,512]{1,0:T(8,128)(2,1)}, bf16[128,512]{1,0:T(8,128)(2,1)}, bf16[128,1024]{1,0:T(...) async-done(((bf16[128,1024]{1,0:T(8,128)(2,1)}, bf16[128,512]{1,0:T(8,128)(2,1)}, bf16[128,512]{1,0:T(8,128)(2,1)}, ...) | async-done | bytes 4325392 | tf_op jit(solution)/shard_map/psum | solution.py:335
  1844.1 1.9 convert_element_type.226
  1849.4 1.8 convert_element_type.232
  (312 shorter events, 79.2 us)
Async XLA Ops:
  7.2 4.8 copy-start.52
  7.2 16.4 copy-start.54
  7.2 16.4 copy-start.56
  7.2 16.5 copy-start.48
  7.2 45.9 %copy-start.2 = (bf16[128,1024]{1,0:T(8,128)(2,1)S(1)}, bf16[128,1024]{1,0:T(8,128)(2,1)}, u32[]{:S(2)}) copy-start(bf16[128,1024]{1,0:T(8,128)(2,1)} %param.18) | copy-start | bytes 786436
  7.2 46.7 %all-gather.14.cloned.1.call-start = ((), (), s32[]{:S(2)}) async-start(), calls=%async_computation.13 | async-start | bytes 1179648 | tf_op jit(solution)/shard_map/all_gather | solution.py:97
  8.0 79.3 %all-gather.12.cloned.1.call-start = ((), (), s32[]{:S(2)}) async-start(), calls=%async_computation.12 | async-start | bytes 1179648 | tf_op jit(solution)/shard_map/all_gather | solution.py:96
  8.7 136.7 %all-gather.10.cloned.1.call-start = ((), (), s32[]{:S(2)}) async-start(), calls=%async_computation.11 | async-start | bytes 2359296 | tf_op jit(solution)/shard_map/all_gather | solution.py:95
  9.5 226.0 %all-gather.16.cloned.1.call-start = ((), (), s32[]{:S(2)}) async-start(), calls=%async_computation.14 | async-start | bytes 2359296 | tf_op jit(solution)/shard_map/all_gather | solution.py:98
  10.0 390.1 %all-gather.18.cloned.1.call-start = ((), (), s32[]{:S(2)}) async-start(), calls=%async_computation.15 | async-start | bytes 10616832 | tf_op jit(solution)/shard_map/all_gather | solution.py:165
  10.6 580.1 %all-gather.20.cloned.1.call-start = ((), (), s32[]{:S(2)}) async-start(), calls=%async_computation.16 | async-start | bytes 10616832 | tf_op jit(solution)/shard_map/all_gather | solution.py:166
  11.2 770.2 %all-gather.22.cloned.1.call-start = ((), (), s32[]{:S(2)}) async-start(), calls=%async_computation.17 | async-start | bytes 10616832 | tf_op jit(solution)/shard_map/all_gather | solution.py:167
  23.6 893.3 %copy-start.36 = (f32[8,1,128]{2,1,0:T(1,128)}, f32[8,1,128]{2,1,0:T(1,128)S(1)}, u32[]{:S(2)}) copy-start(f32[8,1,128]{2,1,0:T(1,128)S(1)} %convert_element_type.241) | copy-start | bytes 12292
  23.6 65.6 %copy-start.49 = (f32[64]{0:T(128)}, f32[64]{0:T(128)S(1)}, u32[]{:S(2)}) copy-start(f32[64]{0:T(128)S(1)} %convert_element_type.205) | copy-start | bytes 772
  23.7 124.9 %copy-start.46 = (f32[64]{0:T(128)}, f32[64]{0:T(128)S(1)}, u32[]{:S(2)}) copy-start(f32[64]{0:T(128)S(1)} %convert_element_type.201) | copy-start | bytes 772
  53.8 863.1 %copy-start.41 = (f32[128]{0:T(128)}, f32[128]{0:T(128)S(1)}, u32[]{:S(2)}) copy-start(f32[128]{0:T(128)S(1)} %get-tuple-element.377) | copy-start | bytes 1540
  53.9 861.8 %copy-start.34 = (f32[128,32]{0,1:T(8,128)}, f32[128,32]{0,1:T(8,128)S(1)}, u32[]{:S(2)}) copy-start(f32[128,32]{0,1:T(8,128)S(1)} %get-tuple-element.375) | copy-start | bytes 49156
  88.9 56.5 %copy-start.24 = (f32[128,512]{1,0:T(8,128)}, f32[128,512]{1,0:T(8,128)S(1)}, u32[]{:S(2)}) copy-start(f32[128,512]{1,0:T(8,128)S(1)} %fusion.64) | copy-start | bytes 786436
  89.0 56.4 %copy-start.22 = (f32[128,512]{0,1:T(8,128)}, f32[128,512]{0,1:T(8,128)S(1)}, u32[]{:S(2)}) copy-start(f32[128,512]{0,1:T(8,128)S(1)} %copy.120) | copy-start | bytes 786436
  147.5 2.3 copy-start.18
  149.8 30.0 %all-to-all-start = ((bf16[128,16,192]{0,2,1:T(8,128)(2,1)}), bf16[128,16,192]{0,2,1:T(8,128)(2,1)S(1)}, u32[]{:S(2)}, u32[]{:S(2)}) async-start(bf16[128,16,192]{0,2,1:T(8,128)(2,1)} %pad_maximum_fusion), calls=%async_computation | async-start | bytes 1572864 | tf_op jit(solution)/shard_map/all_to_all | solution.py:125
  182.6 36.5 %copy-start.53 = (bf16[128]{0:T(256)(128)(2,1)S(1)}, bf16[128]{0:T(256)(128)(2,1)}, u32[]{:S(2)}) copy-start(bf16[128]{0:T(256)(128)(2,1)} %param.25) | copy-start | bytes 772
  214.9 20.6 %all-to-all-start.1 = ((bf16[16,128,64]{1,2,0:T(8,128)(2,1)}), bf16[16,128,64]{1,2,0:T(8,128)(2,1)S(1)}, u32[]{:S(2)}, u32[]{:S(2)}) async-start(bf16[16,128,64]{1,2,0:T(8,128)(2,1)} %copy.126), calls=%async_computation.1 | async-start | bytes 524288 | tf_op jit(solution)/shard_map/all_to_all | solution.py:161
  235.5 2.3 copy-start.26
  237.7 564.8 %copy-start.3 = (f32[128,1024]{1,0:T(8,128)}, f32[128,1024]{1,0:T(8,128)S(1)}, u32[]{:S(2)}) copy-start(f32[128,1024]{1,0:T(8,128)S(1)} %get-tuple-element.381) | copy-start | bytes 1572868
  237.9 352.8 %copy-start.6 = (bf16[128,1024]{1,0:T(8,128)(2,1)}, bf16[128,1024]{1,0:T(8,128)(2,1)S(1)}, u32[]{:S(2)}) copy-start(bf16[128,1024]{1,0:T(8,128)(2,1)S(1)} %multiply_convert_fusion.3) | copy-start | bytes 786436
  406.6 374.7 %copy-start.31 = (bf16[128,1024]{1,0:T(8,128)(2,1)S(1)}, bf16[128,1024]{1,0:T(8,128)(2,1)}, u32[]{:S(2)}) copy-start(bf16[128,1024]{1,0:T(8,128)(2,1)} %param.31) | copy-start | bytes 786436
  791.1 7.7 copy-start.16
  791.1 7.7 copy-start.14
  791.1 7.7 copy-start.1
  798.8 3.9 copy-start.9
  802.7 19.3 %copy-start.12 = (f32[128,1024]{1,0:T(8,128)}, f32[128,1024]{1,0:T(8,128)S(1)}, u32[]{:S(2)}) copy-start(f32[128,1024]{1,0:T(8,128)S(1)} %subtract_add_fusion) | copy-start | bytes 1572868
  804.4 16.1 all-to-all-start.2
  830.2 2.1 copy-start
  848.1 2.1 copy-start
  866.1 2.1 copy-start
  884.1 2.1 copy-start
  895.2 5.9 copy-start.55
  896.6 19.1 %copy-start.23 = (f32[128,512]{0,1:T(8,128)S(1)}, f32[128,512]{0,1:T(8,128)}, u32[]{:S(2)}) copy-start(f32[128,512]{0,1:T(8,128)} %copy-done.22) | copy-start | bytes 786436
  896.6 19.1 %copy-start.50 = (f32[64]{0:T(128)S(1)}, f32[64]{0:T(128)}, u32[]{:S(2)}) copy-start(f32[64]{0:T(128)} %copy-done.49) | copy-start | bytes 772
  896.6 19.0 %all-to-all-start.3 = ((bf16[16,128,192]{1,2,0:T(8,128)(2,1)}), bf16[16,128,192]{1,2,0:T(8,128)(2,1)S(1)}, u32[]{:S(2)}, u32[]{:S(2)}) async-start(bf16[16,128,192]{1,2,0:T(8,128)(2,1)} %pad_maximum_fusion.1), calls=%async_computation.3 | async-start | bytes 1572864 | tf_op jit(solution)/shard_map/all_to_all | solution.py:256
  901.1 48.9 %reduce-scatter.10.cloned.1.call-start = ((), (), s32[]{:S(2)}) async-start(), calls=%async_computation.19 | async-start | bytes 1179648 | tf_op jit(solution)/shard_map/reduce_scatter | solution.py:311
  901.4 14.8 copy-start.25
  916.9 4.0 copy-start.13
  916.9 4.0 copy-start.27
  918.4 73.8 %reduce-scatter.12.cloned.1.call-start = ((), (), s32[]{:S(2)}) async-start(), calls=%async_computation.20 | async-start | bytes 1179648 | tf_op jit(solution)/shard_map/reduce_scatter | solution.py:314
  920.8 2.2 copy-start.57
  920.8 2.9 copy-start.39
  920.8 130.7 %reduce-scatter.14.cloned.1.call-start = ((), (), s32[]{:S(2)}) async-start(), calls=%async_computation.21 | async-start | bytes 2359296 | tf_op jit(solution)/shard_map/reduce_scatter | solution.py:317
  922.9 2.1 copy-start.35
  922.9 183.3 %reduce-scatter.8.cloned.1.call-start = ((), (), s32[]{:S(2)}) async-start(), calls=%async_computation.18 | async-start | bytes 2359296 | tf_op jit(solution)/shard_map/reduce_scatter | solution.py:308
  928.1 2.2 copy-start.7
  928.1 2.2 copy-start.17
  930.3 368.1 %reduce-scatter.16.cloned.1.call-start = ((), (), s32[]{:S(2)}) async-start(), calls=%async_computation.22 | async-start | bytes 10616832 | tf_op jit(solution)/shard_map/reduce_scatter | solution.py:323
  935.6 555.1 %reduce-scatter.18.cloned.1.call-start = ((), (), s32[]{:S(2)}) async-start(), calls=%async_computation.23 | async-start | bytes 10616832 | tf_op jit(solution)/shard_map/reduce_scatter | solution.py:326
  942.0 740.9 %reduce-scatter.20.cloned.1.call-start = ((), (), s32[]{:S(2)}) async-start(), calls=%async_computation.24 | async-start | bytes 10616832 | tf_op jit(solution)/shard_map/reduce_scatter | solution.py:329
  948.4 734.5 %copy-start.58 = (u32[128]{0:T(128)S(1)}, u32[128]{0:T(128)}, u32[]{:S(2)}) copy-start(u32[128]{0:T(128)} %constant.84) | copy-start | bytes 1540
  948.4 735.8 %copy-start.4 = (f32[128,1024]{1,0:T(8,128)S(1)}, f32[128,1024]{1,0:T(8,128)}, u32[]{:S(2)}) copy-start(f32[128,1024]{1,0:T(8,128)} %copy-done.3) | copy-start | bytes 1572868
  948.4 895.7 %all-reduce.8.cloned.1.call-start = ((), (), s32[]{:S(2)}) async-start(), calls=%async_computation.25 | async-start | bytes 8650752 | tf_op jit(solution)/shard_map/psum | solution.py:335
  1684.1 5.9 copy-start.8
  1691.3 51.5 %copy-start.44 = (f32[512]{0:T(512)S(1)}, f32[512]{0:T(512)}, u32[]{:S(2)}) copy-start(f32[512]{0:T(512)} %get-tuple-element.353) | copy-start | bytes 6148
  1691.3 121.2 %copy-start.51 = (f32[128]{0:T(128)S(1)}, f32[128]{0:T(128)}, u32[]{:S(2)}) copy-start(f32[128]{0:T(128)} %get-tuple-element.376) | copy-start | bytes 1540
  1844.1 7.0 copy-start.30
  1847.6 5.2 copy-start.29
  (17 other events, 24.6 us)
Sparse Core Ops, SparseCore 0:
  9.7 36.0 all-gather.13
  47.4 39.8 all-gather.11
  89.0 56.4 all-gather.9
  146.9 59.7 all-gather.15
  208.2 191.9 all-gather.17
  401.6 188.9 all-gather.19
  592.3 188.9 all-gather.21
  918.6 31.4 reduce-scatter.9
  952.4 39.8 reduce-scatter.11
  995.1 56.3 reduce-scatter.13
  1054.4 51.7 reduce-scatter.7
  1108.5 189.8 reduce-scatter.15
  1300.8 189.8 reduce-scatter.17
  1492.9 189.8 reduce-scatter.19
  1685.8 158.2 all-reduce.7
where the time goes:
time: 1870 us; the launch traced here: 1860 us
  waiting for transfers between devices  1430 us (76%)
  blocking collectives  176 us (9%)
  matrix products  139 us (7%)
  other arithmetic  32 us (2%)
  local copies, waits for them, and re-layouts  27 us (1%)
  starting transfers between devices  24.4 us (1%)
    reduce_scatter x1, waiting for transfers between devices, local(): lax.psum_scatter(gradients[7].astype(jnp.bfloat16), 'dp', scatter_dimensi...  192 us
    reduce_scatter x1, waiting for transfers between devices, local(): lax.psum_scatter(gradients[8].astype(jnp.bfloat16), 'dp', scatter_dimensi...  192 us
    reduce_scatter x1, waiting for transfers between devices, local(): lax.psum_scatter(gradients[6].astype(jnp.bfloat16), 'dp', scatter_dimensi...  192 us
    all_gather x1, waiting for transfers between devices, local(): lax.all_gather(w_down, 'dp', axis=0, tiled=True)  184 us
    all_gather x1, waiting for transfers between devices, local(): lax.all_gather(w_up, 'dp', axis=0, tiled=True)  184 us
    all_gather x1, waiting for transfers between devices, local(): lax.all_gather(w_gate, 'dp', axis=0, tiled=True)  162 us
    psum x1, blocking collectives, local(): gain_sums = lax.psum((grad_query_gain, grad_key_gain), ('dp', 'seq'))  69.5 us
    reduce_scatter x1, waiting for transfers between devices, local(): lax.psum_scatter(gradients[4].astype(jnp.bfloat16), 'dp', scatter_dimensi...  59.2 us
  transfers between devices with their start and end apart: 19, of which 16 were waited for; matrix products, arithmetic and copies ran while one was open for 5% of the time, Pallas kernels for 0%

commit v1 on v0

v1 whole, which is shorter than its diff:
```python
import math

import jax
import jax.numpy as jnp
import numpy as np
from jax import lax
from jax.experimental import pallas as pl
from jax.experimental.pallas import tpu as pltpu
from jax.sharding import PartitionSpec as P

MESH = pl.DeviceIdType.MESH
F32 = jnp.float32
BF = jnp.bfloat16
EPS = 1e-05
ROPE_BASE = 1000000.0
NN = (((1,), (0,)), ((), ()))
NT = (((1,), (1,)), ((), ()))
TN = (((0,), (0,)), ((), ()))
SCALE = 0.125
LOG2E = math.log2(math.e)


def dot(a, b, dims=NN, precision=None):
    return lax.dot_general(a, b, dims, preferred_element_type=F32, precision=precision)


def rem(a, b):
    return lax.rem(a, b)


class Place:
    def __init__(self):
        self.dp = lax.axis_index("dp")
        self.sq = lax.axis_index("seq")
        self.y = lax.div(self.dp, 2)
        self.xl = rem(self.dp, 2)
        self.z = lax.div(self.sq, 4)
        self.g = rem(self.sq, 4)
        self.xh = lax.div(self.g, 2)
        self.c = rem(self.sq, 2)

    def zpeer(self, dz):
        return (self.dp, rem(self.z + dz + 4, 4) * 4 + self.g)

    def sib(self):
        return (self.dp, self.sq + 1 - 2 * self.c)

    def xpeer(self):
        return (self.dp, self.z * 4 + (1 - self.xh) * 2 + self.c)

    def dpeer(self, k):
        return (rem(self.dp + k + 8, 8), self.sq)

    def speer(self, k):
        return (self.dp, rem(self.sq + k + 16, 16))

    def tpeer(self, t):
        xl = self.xl if t == 0 else 1 - self.xl
        return (self.z * 2 + xl, self.y * 4 + self.g)


def seg_rows(ids):
    start = jnp.zeros_like(ids)
    for j in range(1, 8):
        below = jnp.sum(jnp.where(ids < j, 1.0, 0.0), keepdims=True)
        start = jnp.where(ids == j, below, start)
    return start


def lane_half():
    return lax.rem(lax.broadcasted_iota(jnp.int32, (1, 128), 1), 64) < 32


def swap_halves(x):
    return jnp.where(lane_half(), pltpu.roll(x, 96, 1), pltpu.roll(x, 32, 1))


def head_mean(x):
    a = lax.div(lax.broadcasted_iota(jnp.int32, (128, 128), 0), 64)
    b = lax.div(lax.broadcasted_iota(jnp.int32, (128, 128), 1), 64)
    block = jnp.where(a == b, 1.0 / 64, 0.0)
    return dot(x, block, NN, lax.Precision.HIGHEST)


def spread_heads(first, second):
    lo = lax.broadcasted_iota(jnp.int32, (1, 128), 1) < 64
    return [
        jnp.where(lo, first, 0.0),
        jnp.where(lo, pltpu.roll(first, 64, 1), 0.0),
        jnp.where(lo, 0.0, pltpu.roll(second, 64, 1)),
        jnp.where(lo, 0.0, second),
    ]


INPUTS = ["tok", "meta", "wq", "wk", "wv", "wo", "wg", "wu", "wd", "cot"]
OUTPUTS = {
    "block_out": ((128, 1024), BF),
    "input_grad": ((128, 1024), BF),
    "fF": ((16, 32, 2304), BF),
    "fD": ((16, 3, 16, 1024), BF),
    "fA": ((16, 32, 768), BF),
    "g_small": ((8, 128), F32),
}
SCRATCH = {
    "tok_all": ((4, 128, 1024), BF),
    "cot_all": ((4, 128, 1024), BF),
    "h_all": ((4, 128, 1024), BF),
    "mseq": ((16, 8, 128), F32),
    "mdp": ((8, 8, 128), F32),
    "wqkv": ((8, 128, 512), BF),
    "wo_v": ((8, 128, 1024), BF),
    "wg_v": ((8, 128, 1152), BF),
    "wu_v": ((8, 128, 1152), BF),
    "wd_v": ((18, 64, 1024), BF),
    "wg_s": ((64, 1152), BF),
    "wu_s": ((64, 1152), BF),
    "st": ((16, 128), F32),
    "qk_raw": ((4, 128, 384), F32),
    "qz": ((4, 512, 128), BF),
    "kv": ((16, 128, 256), BF),
    "kt": ((16, 128, 128), BF),
    "vt": ((16, 128, 128), BF),
    "cosr": ((4, 128, 128), F32),
    "sinr": ((4, 128, 128), F32),
    "invl": ((4, 8, 512), F32),
    "oT": ((4, 256, 128), F32),
    "acc": ((128, 512), F32),
    "lacc": ((8, 512), F32),
    "o_s": ((4, 128, 256), BF),
    "o_in": ((4, 128, 256), BF),
    "o_own": ((128, 1024), BF),
    "o_full": ((4, 128, 1024), BF),
    "mid": ((128, 1024), F32),
    "h2": ((4, 128, 1024), BF),
    "dm": ((4, 128, 1152), F32),
    "mixed": ((4, 128, 1152), BF),
    "dg": ((4, 128, 1152), BF),
    "du": ((4, 128, 1152), BF),
    "p2s": ((3, 128, 1024), BF),
    "p2r": ((3, 128, 1024), BF),
    "own": ((128, 1024), F32),
    "p3s": ((3, 128, 1024), BF),
    "p3r": ((3, 128, 1024), BF),
    "own3": ((128, 1024), F32),
    "dmid": ((128, 1024), F32),
    "da": ((128, 1024), BF),
    "da_c": ((4, 128, 256), BF),
    "dob": ((128, 1024), BF),
    "do_all": ((4, 128, 256), BF),
    "doz": ((512, 128), BF),
    "dkv": ((16, 128, 256), F32),
    "dkvb": ((4, 4, 128, 256), BF),
    "dkvr": ((3, 4, 128, 256), BF),
    "dqr": ((4, 128, 256), F32),
    "dqkv": ((4, 128, 512), BF),
    "p4s": ((3, 128, 1024), BF),
    "p4r": ((3, 128, 1024), BF),
    "gF": ((8, 128, 2304), BF),
    "gD": ((18, 64, 1024), BF),
    "gA": ((8, 128, 768), BF),
    "r1F": ((8, 64, 2304), BF),
    "r1D": ((18, 32, 1024), BF),
    "r1A": ((8, 64, 768), BF),
    "r2F": ((16, 32, 2304), BF),
    "r2D": ((16, 3, 16, 1024), BF),
    "r2A": ((16, 32, 768), BF),
    "oF": ((32, 2304), BF),
    "oD": ((3, 16, 1024), BF),
    "oA": ((32, 768), BF),
    "gsm": ((8, 8, 128), F32),
    "gs1": ((8, 8, 128), F32),
    "gs1s": ((8, 128), F32),
    "gs2": ((16, 8, 128), F32),
}
NSEM = 320


class Refs:
    pass


class Comm:
    def __init__(self, place, ssem, rsem):
        self.p, self.ssem, self.rsem = place, ssem, rsem
        self.n = 0
        self.sent = []

    def take(self, count=1):
        base = self.n
        self.n += count
        return base

    def copy(self, src, dst, i, dev):
        return pltpu.make_async_remote_copy(
            src_ref=src, dst_ref=dst, send_sem=self.ssem.at[i], recv_sem=self.rsem.at[i],
            device_id=dev, device_id_type=MESH,
        )

    def send(self, src, dst, i, dev):
        self.copy(src, dst, i, dev).start()
        self.sent.append((src, i))

    def local(self, src, dst, i):
        return pltpu.make_async_copy(src, dst, self.rsem.at[i])

    def got(self, dst, i):
        self.copy(dst, dst, i, self.p.sib()).wait_recv()

    def finish(self):
        for src, i in self.sent:
            self.copy(src, src, i, self.p.sib()).wait_send()
        self.sent = []


def kernel(*refs):
    r = Refs()
    names = INPUTS + list(OUTPUTS) + list(SCRATCH)
    for name, ref in zip(names, refs):
        setattr(r, name, ref)
    ssem, rsem = refs[len(names):]
    p = Place()
    m = Comm(p, ssem, rsem)

    def z_of(dz):
        return rem(p.z - dz + 4, 4)

    half = pl.ds(pl.multiple_of(p.c * 64, 64), 64)
    other = pl.ds(pl.multiple_of(64 - p.c * 64, 64), 64)
    zq = pl.ds(pl.multiple_of(p.z * 256, 256), 256)
    zk = pl.ds(pl.multiple_of(p.z * 128, 128), 128)
    dps = [rem(p.dp + 8 - k, 8) for k in range(8)]

    i_loc = m.take(3)
    stage = []
    for src, dst, i in ((r.wg, r.wg_s, i_loc), (r.wu, r.wu_s, i_loc + 1)):
        for t in range(9):
            cols = pl.ds(pl.multiple_of(t * 512 + p.z * 128, 128), 128)
            m.local(src.at[half, cols], dst.at[:, pl.ds(t * 128, 128)], i).start()
        stage.append((dst, i))
    parts = ((r.wq, zq, 0, 256), (r.wk, zk, 256, 128), (r.wv, zk, 384, 128))
    for w, cols, at, wid in parts:
        m.local(w.at[half, cols], r.wqkv.at[p.dp, half, pl.ds(at, wid)], i_loc + 2).start()

    bar = pltpu.get_barrier_semaphore()
    for k in range(1, 16):
        pl.semaphore_signal(bar, inc=1, device_id=p.speer(k), device_id_type=MESH)
    for k in range(1, 8):
        pl.semaphore_signal(bar, inc=1, device_id=p.dpeer(k), device_id_type=MESH)
    far = []
    for k in range(8):
        far.append((p.dpeer(k)[0], (p.z * 4 + (1 - p.xh) * 2 + p.c)))
    for k in range(1, 8):
        pl.semaphore_signal(bar, inc=1, device_id=far[k], device_id_type=MESH)
    pl.semaphore_wait(bar, 29)

    i_tok = m.take(4)
    for dz in (1, 3, 2):
        m.send(r.tok, r.tok_all.at[dz], i_tok + dz, p.zpeer(dz))
    i_w = m.take(8)
    for k in range(1, 8):
        for w, cols, at, wid in parts:
            m.copy(w.at[half, cols], r.wqkv.at[p.dp, half, pl.ds(at, wid)], i_w + k, p.dpeer(k)).start()
        m.sent.append((r.wqkv.at[0, half], i_w + k))
    i_mseq = m.take(16)
    for k in range(1, 16):
        m.send(r.meta, r.mseq.at[p.sq], i_mseq + k, p.speer(k))
    i_mdp = m.take(8)
    for k in range(1, 8):
        m.send(r.meta, r.mdp.at[p.dp], i_mdp + k, p.dpeer(k))
    r.mseq[p.sq] = r.meta[...]
    r.mdp[p.dp] = r.meta[...]

    for k in range(1, 16):
        m.got(r.mseq.at[rem(p.sq + 16 - k, 16)], i_mseq + k)
    r.st[...] = seg_rows(r.mseq[:, 2, :])
    lanesign = jnp.where(lane_half(), -1.0, 1.0)
    freq = r.meta[5:6, :]
    for dz in range(4):
        i = 4 * z_of(dz) + p.g
        row = r.st[pl.ds(i, 1), :]
        pos = (lax.broadcasted_iota(jnp.int32, (1, 128), 1) + i * 128).astype(F32) - row
        ang = jnp.transpose(jnp.broadcast_to(pos, (128, 128))) * freq
        r.cosr[dz] = jnp.cos(ang)
        r.sinr[dz] = jnp.sin(ang) * lanesign
    for k in range(1, 8):
        m.got(r.mdp.at[dps[k]], i_mdp + k)
    gain1 = jnp.concatenate([r.mdp[j, 0:1, :] for j in range(8)], axis=1)
    gain2 = jnp.concatenate([r.mdp[j, 1:2, :] for j in range(8)], axis=1)

    m.local(r.wqkv.at[0, half], r.wqkv.at[0, half], i_loc + 2).wait()
    for k in range(1, 8):
        m.got(r.wqkv.at[dps[k], half], i_w + k)
    i_share = m.take(5)
    m.send(r.wqkv.at[:, half], r.wqkv.at[:, half], i_share, p.sib())

    i_wo = m.take(8)
    m.local(r.wo.at[half], r.wo_v.at[p.dp, half], i_wo).start()
    for k in range(1, 8):
        m.send(r.wo.at[half], r.wo_v.at[p.dp, half], i_wo + k, p.dpeer(k))
    for dst, i in stage:
        m.local(dst, dst, i).wait()
    i_wd = m.take(1)
    i_wds = m.take(24)
    i_wg = m.take(8)
    i_wu = m.take(8)

    def down_pieces(d):
        out = []
        for n in range(2):
            u = rem(2 * p.z + n - d + 8, 8)
            big = 9 * d + u
            out.append((u, 2 * lax.div(big, 8) + rem(big, 2)))
        big = 9 * d + 8
        return out, (8, 2 * lax.div(big, 8) + rem(big, 2)), lax.div(d, 2) == p.z

    pieces, extra, has_extra = down_pieces(p.dp)
    c32 = p.c * 32

    def down_copy(k, n, piece):
        u, hidx = piece
        src = r.wd.at[pl.ds(pl.multiple_of(u * 64 + c32, 32), 32)]
        dst = r.wd_v.at[hidx, pl.ds(pl.multiple_of(c32, 32), 32)]
        if k == 0:
            return pltpu.make_async_copy(src, dst, rsem.at[i_wd])
        return pltpu.make_async_remote_copy(
            src_ref=src, dst_ref=dst, send_sem=ssem.at[i_wds + 3 * k + n], recv_sem=rsem.at[i_wd],
            device_id=p.dpeer(k), device_id_type=MESH,
        )

    for k in range(8):
        for n in range(2):
            down_copy(k, n, pieces[n]).start()

    @pl.when(has_extra)
    def _():
        for k in range(8):
            down_copy(k, 2, extra).start()

    for src, dst, i in ((r.wg_s, r.wg_v, i_wg), (r.wu_s, r.wu_v, i_wu)):
        for k in range(1, 8):
            m.send(src, dst.at[p.dp, half], i + k, p.dpeer(k))
        dst[p.dp, half] = src[...]
    m.got(r.wqkv.at[:, other], i_share)

    wfull = r.wqkv[...].reshape(1024, 512)
    qg = r.meta[3:4, :]
    kg = r.meta[4:5, :]
    i_kv = m.take(4)
    i_kvx = m.take(4)
    i_kvf = m.take(4)

    def project(dz, x):
        x = x.astype(F32)
        r1 = lax.rsqrt(jnp.mean(x * x, axis=1, keepdims=True) + EPS)
        h = (x * r1 * gain1).astype(BF)
        r.h_all[dz] = h
        o = dot(h, wfull)
        cs, sn = r.cosr[dz], r.sinr[dz]
        r.qk_raw[dz] = o[:, 0:384]
        rot = []
        for b, gn in ((0, qg), (1, qg), (2, kg)):
            v = o[:, b * 128:(b + 1) * 128]
            v = v * lax.rsqrt(head_mean(v * v) + EPS) * gn
            rot.append(v * cs + swap_halves(v) * sn)
        for hd, v in enumerate(spread_heads(rot[0], rot[1])):
            r.qz[dz, pl.ds(hd * 128, 128), :] = v.astype(BF)
        i = 4 * z_of(dz) + p.g
        r.kv[i, :, 0:128] = rot[2].astype(BF)
        r.kv[i, :, 128:256] = o[:, 384:512].astype(BF)
        m.send(r.kv.at[i], r.kv.at[i], i_kvx + dz, p.xpeer())
        m.send(r.kv.at[i], r.kv.at[i], i_kv + dz, p.sib())

    project(0, r.tok[...])
    for dz in (1, 3, 2):
        m.got(r.tok_all.at[dz], i_tok + dz)
        project(dz, r.tok_all[dz])
    i_cot = m.take(4)
    for dz in (1, 3, 2):
        m.send(r.cot, r.cot_all.at[dz], i_cot + dz, p.zpeer(dz))
    r.cot_all[0] = r.cot[...]
    gs = p.g + 1 - 2 * p.c
    gx = (1 - p.xh) * 2 + p.c
    gxs = (1 - p.xh) * 2 + 1 - p.c
    for dz in (0, 1, 3, 2):
        zz = 4 * z_of(dz)
        m.got(r.kv.at[zz + gx], i_kvx + dz)
        m.send(r.kv.at[zz + gx], r.kv.at[zz + gx], i_kvf + dz, p.sib())
    for dz in (0, 1, 3, 2):
        zz = 4 * z_of(dz)
        m.got(r.kv.at[zz + gs], i_kv + dz)
        m.got(r.kv.at[zz + gxs], i_kvf + dz)

    def turn(j, carry):
        r.kt[j] = jnp.transpose(r.kv[j, :, 0:128].astype(F32)).astype(BF)
        r.vt[j] = jnp.transpose(r.kv[j, :, 128:256].astype(F32)).astype(BF)
        return carry

    lax.fori_loop(0, 16, turn, 0)

    def allowed_rows(i):
        row = r.st[pl.ds(i, 1), :].astype(jnp.int32)
        qi = lax.broadcasted_iota(jnp.int32, (1, 128), 1) + i * 128
        return jnp.concatenate([row] * 4, axis=1), jnp.concatenate([qi] * 4, axis=1)

    def weights_of(kb, qv, row4, qi4):
        s = dot(r.kv[kb, :, 0:128], qv, NT)
        ki = lax.broadcasted_iota(jnp.int32, (128, 512), 0) + kb * 128
        return jnp.where((ki >= row4) & (ki <= qi4), jnp.exp2(s * (SCALE * LOG2E)), 0.0)

    def forward_chunk(j, carry):
        dz = rem(j + 1, 4)
        i = 4 * z_of(dz) + p.g
        row4, qi4 = allowed_rows(i)
        r.acc[...] = jnp.zeros_like(r.acc)
        r.lacc[...] = jnp.zeros_like(r.lacc)
        qv = r.qz[dz]

        def body(kb, inner):
            w = weights_of(kb, qv, row4, qi4)
            r.lacc[...] += jnp.sum(w.reshape(16, 8, 512), axis=0)
            r.acc[...] += dot(r.vt[kb], w.astype(BF))
            return inner

        lax.fori_loop(jnp.maximum(i - 8, 0), i + 1, body, 0)
        il = 1.0 / jnp.sum(r.lacc[...], axis=0, keepdims=True)
        r.invl[dz] = jnp.broadcast_to(il, (8, 512))
        o = r.acc[...] * il
        full = jnp.concatenate(
            [o[(h // 2) * 64:(h // 2) * 64 + 64, h * 128:(h + 1) * 128] for h in range(4)], axis=0
        )
        r.oT[dz] = full
        r.o_s[dz] = jnp.transpose(full).astype(BF)
        return carry

    i_o = m.take(4)
    for j in range(4):
        forward_chunk(j, 0)
        dz = (j + 1) % 4
        if dz:
            m.send(r.o_s.at[dz], r.o_in.at[p.z], i_o + dz, p.zpeer(-dz))
        else:
            r.o_in[p.z] = r.o_s[0]

    m.local(r.wo_v.at[0, half], r.wo_v.at[0, half], i_wo).wait()
    for k in range(1, 8):
        m.got(r.wo_v.at[dps[k], half], i_wo + k)
    m.send(r.wo_v.at[:, half], r.wo_v.at[:, half], i_share + 1, p.sib())
    for dz in range(1, 4):
        m.got(r.o_in.at[rem(p.z + dz, 4)], i_o + dz)
    for j in range(4):
        r.o_own[:, j * 256:(j + 1) * 256] = r.o_in[j]
    m.got(r.wo_v.at[:, other], i_share + 1)
    x0 = r.tok[...].astype(F32)
    middle = x0 + dot(r.o_own[...], r.wo_v[...].reshape(1024, 1024))
    r.mid[...] = middle
    r2 = lax.rsqrt(jnp.mean(middle * middle, axis=1, keepdims=True) + EPS)
    r.h2[0] = (middle * r2 * gain2).astype(BF)
    i_h2 = m.take(4)
    for dz in (2, 1, 3):
        m.send(r.h2.at[0], r.h2.at[dz], i_h2 + dz, p.zpeer(dz))

    pltpu.make_async_copy(r.wd_v.at[:, pl.ds(0, 32)], r.wd_v.at[:, pl.ds(0, 32)], rsem.at[i_wd]).wait()
    h32 = pl.ds(pl.multiple_of(c32, 32), 32)
    o32 = pl.ds(pl.multiple_of(32 - c32, 32), 32)
    m.send(r.wd_v.at[:, h32], r.wd_v.at[:, h32], i_share + 2, p.sib())
    for n, (dst, i) in enumerate(((r.wg_v, i_wg), (r.wu_v, i_wu))):
        for k in range(1, 8):
            m.got(dst.at[dps[k], half], i + k)
        m.send(dst.at[:, half], dst.at[:, half], i_share + 3 + n, p.sib())
    for dz in range(1, 4):
        m.got(r.cot_all.at[dz], i_cot + dz)
    m.got(r.wd_v.at[:, o32], i_share + 2)
    wd = r.wd_v[...].reshape(1152, 1024)
    cots = r.cot_all[...].reshape(512, 1024)

    def cols384(t):
        return pl.ds(pl.multiple_of(t * 384, 128), 384)

    def dm_tile(t, carry):
        w = r.wd_v[pl.ds(t * 6, 6)].reshape(384, 1024)
        r.dm[:, :, cols384(t)] = dot(cots, w, NT).reshape(4, 128, 384)
        return carry

    lax.fori_loop(0, 3, dm_tile, 0)
    m.got(r.wg_v.at[:, other], i_share + 3)
    m.got(r.wu_v.at[:, other], i_share + 4)

    i_p2 = m.take(4)
    for pair in range(2):
        two = slice(2 * pair, 2 * pair + 2)
        for dz in ((1,), (2, 3))[pair]:
            m.got(r.h2.at[dz], i_h2 + dz)
        hh = r.h2[two].reshape(256, 1024)

        def ffn_tile(t, carry):
            cols = cols384(t)
            gate = dot(hh, r.wg_v[:, :, cols].reshape(1024, 384))
            up = dot(hh, r.wu_v[:, :, cols].reshape(1024, 384))
            sig = 1.0 / (1.0 + jnp.exp(-gate))
            act = gate * sig
            dmt = r.dm[two, :, cols].reshape(256, 384)
            r.mixed[two, :, cols] = (act * up).astype(BF).reshape(2, 128, 384)
            r.dg[two, :, cols] = (dmt * up * sig * (1.0 + gate * (1.0 - sig))).astype(BF).reshape(2, 128, 384)
            r.du[two, :, cols] = (dmt * act).astype(BF).reshape(2, 128, 384)
            return carry

        lax.fori_loop(0, 3, ffn_tile, 0)
        part = dot(r.dg[two].reshape(256, 1152), r.wg_v[...].reshape(1024, 1152), NT)
        part += dot(r.du[two].reshape(256, 1152), r.wu_v[...].reshape(1024, 1152), NT)
        if pair == 0:
            r.own[...] = part[0:128]
            r.p2s[0] = part[128:256].astype(BF)
            m.send(r.p2s.at[0], r.p2r.at[0], i_p2 + 1, p.zpeer(-1))
        else:
            r.p2s[1] = part[0:128].astype(BF)
            m.send(r.p2s.at[1], r.p2r.at[1], i_p2 + 2, p.zpeer(-2))
            r.p2s[2] = part[128:256].astype(BF)
            m.send(r.p2s.at[2], r.p2r.at[2], i_p2 + 3, p.zpeer(-3))

    i_r1 = m.take(3)
    h2t = r.h2[...].reshape(512, 1024)

    def gate_up_tile(t, carry):
        cols = cols384(t)
        r.gF[:, :, cols] = dot(h2t, r.dg[:, :, cols].reshape(512, 384), TN).astype(BF).reshape(8, 128, 384)
        r.gF[:, :, cols384(t + 3)] = dot(h2t, r.du[:, :, cols].reshape(512, 384), TN).astype(BF).reshape(8, 128, 384)
        return carry

    lax.fori_loop(0, 3, gate_up_tile, 0)
    m.send(r.gF.at[:, other], r.r1F, i_r1, p.sib())

    def down_tile(t, carry):
        w = r.mixed[:, :, cols384(t)].reshape(512, 384)
        r.gD[pl.ds(t * 6, 6)] = dot(w, cots, TN).astype(BF).reshape(6, 64, 1024)
        return carry

    lax.fori_loop(0, 3, down_tile, 0)
    m.send(r.gD.at[:, o32], r.r1D, i_r1 + 1, p.sib())
    r.own3[...] = dot(r.mixed[0], wd)

    def out_chunk(dz, carry):
        r.p3s[dz - 1] = dot(r.mixed[dz], wd).astype(BF)
        return carry

    lax.fori_loop(1, 4, out_chunk, 0)

    for dz in range(1, 4):
        m.got(r.p2r.at[dz - 1], i_p2 + dz)
    dh2 = r.own[...] + r.p2r[0].astype(F32) + r.p2r[1].astype(F32) + r.p2r[2].astype(F32)
    middle = r.mid[...]
    r2 = lax.rsqrt(jnp.mean(middle * middle, axis=1, keepdims=True) + EPS)
    small2 = jnp.sum(dh2 * middle * r2, axis=0, keepdims=True)
    wdh = dh2 * gain2
    dmid = r.cot[...].astype(F32) + r2 * wdh - middle * (r2 * r2 * r2) * jnp.mean(wdh * middle, axis=1, keepdims=True)
    r.dmid[...] = dmid
    r.da[...] = dmid.astype(BF)
    r.dob[...] = dot(r.da[...], r.wo_v[...].reshape(1024, 1024), NT).astype(BF)
    i_do = m.take(4)

    def zcols(z):
        return pl.ds(pl.multiple_of(z * 256, 256), 256)

    for dz in (2, 1, 3):
        m.send(r.dob.at[:, zcols(rem(p.z + dz, 4))], r.do_all.at[dz], i_do + dz, p.zpeer(dz))
    r.do_all[0] = r.dob[:, zq]
    i_p3 = m.take(4)
    i_of = m.take(4)
    i_dc = m.take(4)
    for dz in (2, 1, 3):
        m.send(r.o_own, r.o_full.at[dz], i_of + dz, p.zpeer(dz))
        m.send(r.da.at[:, zcols(rem(p.z + dz, 4))], r.da_c.at[dz], i_dc + dz, p.zpeer(dz))
    for dz in (2, 1, 3):
        m.send(r.p3s.at[dz - 1], r.p3r.at[dz - 1], i_p3 + dz, p.zpeer(-dz))
    r.o_full[0] = r.o_own[...]
    r.da_c[0] = r.da[:, zq]

    m.got(r.r1F, i_r1)
    m.got(r.r1D, i_r1 + 1)

    def add_core(d, carry):
        r.r1F[d] = (r.r1F[d].astype(F32) + r.gF[d, half].astype(F32)).astype(BF)
        return carry

    lax.fori_loop(0, 8, add_core, 0)

    def add_core_down(d, carry):
        r.r1D[d] = (r.r1D[d].astype(F32) + r.gD[d, h32].astype(F32)).astype(BF)
        return carry

    lax.fori_loop(0, 18, add_core_down, 0)
    i_r2 = m.take(16)
    i_r2d = m.take(16)
    i_r2e = m.take(16)

    def slots():
        for t in range(2):
            for k in range(8):
                yield t * 8 + k, t, k

    def target(t, k):
        return p.dpeer(k) if t == 0 else far[k]

    def rows32(t):
        x = p.xh if t == 0 else 1 - p.xh
        return pl.ds(pl.multiple_of(x * 32, 32), 32), pl.ds(pl.multiple_of(x * 16, 16), 16)

    for s, t, k in slots():
        d = rem(p.dp + k, 8)
        r32, r16 = rows32(t)
        two, more, cond = down_pieces(d)
        if s == 0:
            r.r2F[0] = r.r1F[d, r32]
            for n in range(2):
                r.r2D[0, n] = r.r1D[two[n][1], r16]

            @pl.when(cond)
            def _():
                r.r2D[0, 2] = r.r1D[more[1], r16]

            continue
        m.send(r.r1F.at[d, r32], r.r2F.at[s], i_r2 + s, target(t, k))
        for n in range(2):
            m.copy(r.r1D.at[two[n][1], r16], r.r2D.at[s, n], i_r2d + s, target(t, k)).start()
        m.sent.append((r.r2D.at[0, pl.ds(0, 2)], i_r2d + s))

        @pl.when(cond)
        def _():
            m.copy(r.r1D.at[more[1], r16], r.r2D.at[s, 2], i_r2e + s, target(t, k)).start()

    r.dkv[...] = jnp.zeros_like(r.dkv)
    for dz in (0, 1, 3, 2):
        if dz:
            m.got(r.do_all.at[dz], i_do + dz)

    def backward_chunk(j, carry):
        dz = j
        i = 4 * z_of(dz) + p.g
        row4, qi4 = allowed_rows(i)
        do = r.do_all[dz].astype(F32)
        for hd, v in enumerate(spread_heads(do[:, 0:128], do[:, 128:256])):
            r.doz[pl.ds(hd * 128, 128), :] = v.astype(BF)
        prod = jnp.transpose(do) * r.oT[dz]
        drow = jnp.concatenate(
            [jnp.sum(prod[h * 64:(h + 1) * 64], axis=0, keepdims=True) for h in range(4)], axis=1
        )
        il = r.invl[dz, 0:1, :]
        qv = r.qz[dz]
        dov = r.doz[...]
        r.acc[...] = jnp.zeros_like(r.acc)

        def body(kb, inner):
            w = weights_of(kb, qv, row4, qi4) * il
            dp = dot(r.kv[kb, :, 128:256], dov, NT)
            ds = (w * (dp - drow)).astype(BF)
            r.acc[...] += dot(r.kt[kb], ds)
            r.dkv[kb, :, 0:128] += dot(ds, qv)
            r.dkv[kb, :, 128:256] += dot(w.astype(BF), dov)
            return inner

        lax.fori_loop(jnp.maximum(i - 8, 0), i + 1, body, 0)
        o = r.acc[...] * SCALE
        full = jnp.concatenate(
            [o[(h // 2) * 64:(h // 2) * 64 + 64, h * 128:(h + 1) * 128] for h in range(4)], axis=0
        )
        r.dqr[dz] = jnp.transpose(full)
        return carry

    lax.fori_loop(0, 4, backward_chunk, 0)

    lane = lax.broadcasted_iota(jnp.int32, (1, 256), 1)
    kscale = jnp.where(lane < 128, SCALE, 1.0)
    r.dkvb[...] = (r.dkv[...] * kscale.reshape(1, 1, 256)).astype(BF).reshape(4, 4, 128, 256)
    i_dkv = m.take(3)
    xs = (p.dp, p.z * 4 + gxs)
    m.send(r.dkvb.at[:, gx], r.dkvr.at[1], i_dkv + 1, p.xpeer())
    m.send(r.dkvb.at[:, gxs], r.dkvr.at[2], i_dkv + 2, xs)
    m.send(r.dkvb.at[:, gs], r.dkvr.at[0], i_dkv, p.sib())

    for dz in range(1, 4):
        m.got(r.o_full.at[dz], i_of + dz)
        m.got(r.da_c.at[dz], i_dc + dz)
        m.got(r.p3r.at[dz - 1], i_p3 + dz)
    r.gA[:, :, 512:768] = dot(
        r.o_full[...].reshape(512, 1024), r.da_c[...].reshape(512, 256), TN
    ).astype(BF).reshape(8, 128, 256)
    r.block_out[...] = (
        r.mid[...] + r.own3[...] + r.p3r[0].astype(F32) + r.p3r[1].astype(F32) + r.p3r[2].astype(F32)
    ).astype(BF)

    def got_ffn():
        for s, t, k in slots():
            if s == 0:
                continue
            m.got(r.r2F.at[s], i_r2 + s)
            m.got(r.r2D.at[s, pl.ds(0, 2)], i_r2d + s)
        mine = lax.div(p.dp, 2) == p.z

        @pl.when(mine)
        def _():
            for s, t, k in slots():
                if s:
                    m.got(r.r2D.at[s, 2], i_r2e + s)

        def add(s, total):
            return total + r.r2F[s].astype(F32)

        r.oF[...] = lax.fori_loop(1, 16, add, r.r2F[0].astype(F32)).astype(BF)

        def addd(s, total):
            return total + r.r2D[s, 0:2].astype(F32)

        r.oD[0:2] = lax.fori_loop(1, 16, addd, r.r2D[0, 0:2].astype(F32)).astype(BF)

        @pl.when(mine)
        def _():
            def adde(s, total):
                return total + r.r2D[s, 2].astype(F32)

            r.oD[2] = lax.fori_loop(1, 16, adde, r.r2D[0, 2].astype(F32)).astype(BF)

        @pl.when(jnp.logical_not(mine))
        def _():
            r.oD[2] = jnp.zeros((16, 1024), BF)

    got_ffn()

    def seq_at(z, g):
        return rem(z + 8, 4) * 4 + g

    class Gather:
        def __init__(self, own, buf):
            self.own, self.buf = own, buf
            self.il = m.take(1)
            self.ix, self.iz, self.izx, self.ic = m.take(1), m.take(4), m.take(4), m.take(8)

        def first(self):
            s = self.buf.at[p.sq]
            m.send(self.own, s, self.ix, p.xpeer())
            for dz in (2, 1, 3):
                m.send(self.own, s, self.iz + dz, p.zpeer(dz))
            m.send(self.own, s, self.ic, p.sib())
            m.local(self.own, s, self.il).start()

        def second(self):
            s = self.buf.at[seq_at(p.z, gx)]
            m.got(s, self.ix)
            for dz in (2, 1, 3):
                m.send(s, s, self.izx + dz, p.zpeer(dz))
            m.send(s, s, self.ic + 4, p.sib())

        def third(self):
            for dz in (1, 3, 2):
                s = self.buf.at[seq_at(p.z - dz, p.g)]
                m.got(s, self.iz + dz)
                m.send(s, s, self.ic + dz, p.sib())
            for dz in (1, 3, 2):
                s = self.buf.at[seq_at(p.z - dz, gx)]
                m.got(s, self.izx + dz)
                m.send(s, s, self.ic + 4 + dz, p.sib())

        def last(self):
            for dz in (0, 1, 3, 2):
                m.got(self.buf.at[seq_at(p.z - dz, gs)], self.ic + dz)
                m.got(self.buf.at[seq_at(p.z - dz, gxs)], self.ic + 4 + dz)
            m.local(self.own, self.buf.at[p.sq], self.il).wait()

    ag_f = Gather(r.oF, r.fF)
    ag_d = Gather(r.oD, r.fD)
    ag_a = Gather(r.oA, r.fA)

    for n in range(3):
        m.got(r.dkvr.at[n], i_dkv + n)
    sq_acc = jnp.zeros((1, 128), F32)
    sk_acc = jnp.zeros((1, 128), F32)
    for dz in range(4):
        zz = z_of(dz)
        i = 4 * zz + p.g
        dkv = r.dkv[i] * kscale
        for n in range(3):
            dkv = dkv + r.dkvr[n, zz].astype(F32)
        cs, sn = r.cosr[dz], r.sinr[dz]
        grads = (r.dqr[dz, :, 0:128], r.dqr[dz, :, 128:256], dkv[:, 0:128])
        for b, gr in enumerate(grads):
            gn = qg if b < 2 else kg
            v = r.qk_raw[dz, :, b * 128:(b + 1) * 128]
            f = lax.rsqrt(head_mean(v * v) + EPS)
            dn = gr * cs - swap_halves(gr) * sn
            add = jnp.sum(dn * v * f, axis=0, keepdims=True)
            if b < 2:
                sq_acc = sq_acc + add
            else:
                sk_acc = sk_acc + add
            wn = dn * gn
            r.dqkv[dz, :, b * 128:(b + 1) * 128] = (f * wn - v * (f * f * f) * head_mean(wn * v)).astype(BF)
        r.dqkv[dz, :, 384:512] = dkv[:, 128:256].astype(BF)
    i_p4 = m.take(4)
    for dz in (2, 1, 3):
        r.p4s[dz - 1] = dot(r.dqkv[dz], r.wqkv[...].reshape(1024, 512), NT).astype(BF)
        m.send(r.p4s.at[dz - 1], r.p4r.at[dz - 1], i_p4 + dz, p.zpeer(-dz))
    r.own[...] = dot(r.dqkv[0], r.wqkv[...].reshape(1024, 512), NT)
    r.gA[:, :, 0:512] = dot(
        r.h_all[...].reshape(512, 1024), r.dqkv[...].reshape(512, 512), TN
    ).astype(BF).reshape(8, 128, 512)
    m.send(r.gA.at[:, other], r.r1A, i_r1 + 2, p.sib())
    ag_f.first()
    ag_d.first()
    m.got(r.r1A, i_r1 + 2)
    r.r1A[...] = (r.r1A[...].astype(F32) + r.gA[:, half].astype(F32)).astype(BF)
    i_r2a = m.take(16)
    for s, t, k in slots():
        d = rem(p.dp + k, 8)
        r32, _ = rows32(t)
        if s == 0:
            r.r2A[0] = r.r1A[d, r32]
        else:
            m.send(r.r1A.at[d, r32], r.r2A.at[s], i_r2a + s, target(t, k))
    ag_f.second()
    ag_d.second()

    for dz in range(1, 4):
        m.got(r.p4r.at[dz - 1], i_p4 + dz)
    dh = r.own[...] + r.p4r[0].astype(F32) + r.p4r[1].astype(F32) + r.p4r[2].astype(F32)
    x0 = r.tok[...].astype(F32)
    r1 = lax.rsqrt(jnp.mean(x0 * x0, axis=1, keepdims=True) + EPS)
    small1 = jnp.sum(dh * x0 * r1, axis=0, keepdims=True)
    wdh = dh * gain1
    r.input_grad[...] = (
        r.dmid[...] + r1 * wdh - x0 * (r1 * r1 * r1) * jnp.mean(wdh * x0, axis=1, keepdims=True)
    ).astype(BF)

    both = lambda v: v + pltpu.roll(v, 64, 1)
    for d in range(8):
        cols = slice(d * 128, (d + 1) * 128)
        r.gsm[d] = jnp.concatenate(
            [small1[:, cols], small2[:, cols], both(sq_acc), both(sk_acc), jnp.zeros((4, 128), F32)], axis=0
        )
    i_s1 = m.take(8)
    i_s2 = m.take(16)
    for k in range(1, 8):
        m.send(r.gsm.at[rem(p.dp + k, 8)], r.gs1.at[k], i_s1 + k, p.dpeer(k))
    r.gs1[0] = r.gsm[p.dp]
    for k in range(1, 8):
        m.got(r.gs1.at[k], i_s1 + k)
    r.gs1s[...] = jnp.sum(r.gs1[...], axis=0)
    for k in range(1, 16):
        m.send(r.gs1s, r.gs2.at[k], i_s2 + k, p.speer(k))
    r.gs2[0] = r.gs1s[...]

    for s, t, k in slots():
        if s:
            m.got(r.r2A.at[s], i_r2a + s)

    def adda(s, total):
        return total + r.r2A[s].astype(F32)

    r.oA[...] = lax.fori_loop(1, 16, adda, r.r2A[0].astype(F32)).astype(BF)
    ag_a.first()
    ag_f.third()
    ag_d.third()
    ag_a.second()
    ag_a.third()
    for k in range(1, 16):
        m.got(r.gs2.at[k], i_s2 + k)
    r.g_small[...] = jnp.sum(r.gs2[...], axis=0)
    ag_f.last()
    ag_d.last()
    ag_a.last()

    m.finish()
    for k in range(1, 8):
        for n in range(2):
            down_copy(k, n, pieces[n]).wait_send()

    @pl.when(has_extra)
    def _():
        for k in range(1, 8):
            down_copy(k, 2, extra).wait_send()

    for s, t, k in slots():
        if s:
            _, more, cond = down_pieces(rem(p.dp + k, 8))

            @pl.when(cond)
            def _():
                m.copy(r.r1D.at[more[1], pl.ds(0, 16)], r.r2D.at[s, 2], i_r2e + s, p.sib()).wait_send()

    assert m.n <= NSEM, m.n


def block(args):
    vm = pl.BlockSpec(memory_space=pltpu.VMEM)
    hb = pl.BlockSpec(memory_space=pl.ANY)
    return pl.pallas_call(
        kernel,
        out_shape=tuple(jax.ShapeDtypeStruct(s, d) for s, d in OUTPUTS.values()),
        in_specs=[vm, vm] + [hb] * 7 + [vm],
        out_specs=tuple(hb if name[0] == "f" else vm for name in OUTPUTS),
        scratch_shapes=[pltpu.VMEM(s, d) for s, d in SCRATCH.values()]
        + [pltpu.SemaphoreType.DMA((NSEM,)), pltpu.SemaphoreType.DMA((NSEM,))],
        compiler_params=pltpu.CompilerParams(
            collective_id=0, has_side_effects=True, vmem_limit_bytes=63 * 2**20
        ),
        name="block",
    )(*args)


LAID = {
    "g_gate": (128, 4608),
    "g_up": (128, 4608),
    "g_down": (576, 1024),
    "g_q": (128, 1024),
    "g_k": (128, 512),
    "g_v": (128, 512),
    "g_out": (128, 1024),
}


def lay_kernel(f_f, f_d, f_a, g_gate, g_up, g_down, g_q, g_k, g_v, g_out):
    p = Place()

    def lay(s, carry):
        z = lax.div(s, 4)
        g = rem(s, 4)
        row = pl.ds(pl.multiple_of(rem(g, 2) * 64 + lax.div(g, 2) * 32, 32), 32)
        for t in range(9):
            cols = pl.ds(pl.multiple_of(t * 512 + z * 128, 128), 128)
            g_gate[row, cols] = f_f[s, :, t * 128:(t + 1) * 128].astype(F32)
            g_up[row, cols] = f_f[s, :, 1152 + t * 128:1152 + (t + 1) * 128].astype(F32)
        c256 = pl.ds(pl.multiple_of(z * 256, 256), 256)
        c128 = pl.ds(pl.multiple_of(z * 128, 128), 128)
        g_q[row, c256] = f_a[s, :, 0:256].astype(F32)
        g_k[row, c128] = f_a[s, :, 256:384].astype(F32)
        g_v[row, c128] = f_a[s, :, 384:512].astype(F32)
        g_out[row, c256] = f_a[s, :, 512:768].astype(F32)
        sub = rem(g, 2) * 32 + lax.div(g, 2) * 16
        for n in range(2):
            u = rem(2 * z + n - p.dp + 8, 8)
            g_down[pl.ds(pl.multiple_of(u * 64 + sub, 16), 16), :] = f_d[s, n].astype(F32)

        @pl.when(lax.div(p.dp, 2) == z)
        def _():
            g_down[pl.ds(pl.multiple_of(8 * 64 + sub, 16), 16), :] = f_d[s, 2].astype(F32)

        return carry

    lax.fori_loop(0, 16, lay, 0)


def lay_out(f_f, f_d, f_a):
    vm = pl.BlockSpec(memory_space=pltpu.VMEM)
    o = pl.pallas_call(
        lay_kernel,
        out_shape=tuple(jax.ShapeDtypeStruct(s, F32) for s in LAID.values()),
        in_specs=[vm] * 3,
        out_specs=tuple(vm for _ in LAID),
        compiler_params=pltpu.CompilerParams(vmem_limit_bytes=40 * 2**20),
        name="lay",
    )(f_f, f_d, f_a)
    return dict(zip(LAID, o))


def local(
    tokens, segment_ids, attn_gain, w_query, w_key, w_value, w_out, ffn_gain, w_gate, w_up, w_down,
    query_gain, key_gain, cotangent,
):
    inverse = ROPE_BASE ** (-(np.arange(32).astype(np.float32) * np.float32(2.0) / np.float32(64)))
    freq = jnp.asarray(np.tile(inverse.astype(np.float32), 4)[None])
    meta = jnp.concatenate(
        [
            attn_gain.astype(F32)[None],
            ffn_gain.astype(F32)[None],
            segment_ids.astype(F32),
            jnp.tile(query_gain.astype(F32), 2)[None],
            jnp.tile(key_gain.astype(F32), 2)[None],
            freq,
            jnp.zeros((2, 128), F32),
        ],
        axis=0,
    )
    o = block((tokens, meta, w_query, w_key, w_value, w_out, w_gate, w_up, w_down, cotangent))
    o = dict(zip(OUTPUTS, o))
    small = o["g_small"]
    w = lay_out(o["fF"], o["fD"], o["fA"])
    return (
        o["block_out"], o["input_grad"], small[0], w["g_q"], w["g_k"], w["g_v"], w["g_out"], small[1],
        w["g_gate"], w["g_up"], w["g_down"], small[2, :64], small[3, :64],
    )


def solution(mesh):
    both = ("dp", "seq")
    w = P("dp", None)
    return jax.shard_map(
        local,
        mesh=mesh,
        in_specs=(P(both, None), P("dp", "seq"), P("dp"), w, w, w, w, P("dp"), w, w, w, P(), P(), P(both, None)),
        out_specs=(P(both, None), P(both, None), P("dp"), w, w, w, w, P("dp"), w, w, w, P(), P()),
        check_vma=False,
    )
```

time: 1870 us -> 282 us (0.15)
  waiting for transfers between devices: 1430 us -> 0 us
  Pallas kernels: 0 us -> 269 us
  blocking collectives: 176 us -> 0 us
  matrix products: 139 us -> 0 us
  other arithmetic: 32 us -> 1.33 us
  starting transfers between devices: 24.4 us -> 0 us
    reduce_scatter x7 -> x0, waiting for transfers between devices: 734 us -> none  [the longest x1 192 us: local(): lax.psum_scatter(gradients[7].astype(jnp.bfloat16), 'dp', scatter_dimensi...]
    all_gather x7 -> x0, waiting for transfers between devices: 618 us -> none  [the longest x1 184 us: local(): lax.all_gather(w_down, 'dp', axis=0, tiled=True)]
    pallas_call x0 -> x2, Pallas kernels: none -> 269 us  [the longest x1 265 us: block(): pl.pallas_call(kernel, out_shape=tuple((jax.ShapeDtypeStruct(s, d) for s,...]
    dot_general x49 -> x0, matrix products: 139 us -> none  [the longest x7 23.9 us: over_cols(): lax.dot_general(left_side, right_side, (((1,), (1,)), ((), ())), preferre...]
    psum x2 -> x0, blocking collectives: 107 us -> none  [the longest x1 69.5 us: local(): gain_sums = lax.psum((grad_query_gain, grad_key_gain), ('dp', 'seq'))]
    all_gather x3 -> x0, blocking collectives: 57.1 us -> none  [the longest x1 29.1 us: local(): doc_all = lax.all_gather(segment_ids, 'seq', axis=1, tiled=True)[0]]
    all_to_all x4 -> x0, waiting for transfers between devices: 45.3 us -> none  [the longest x1 22.8 us: local(): lax.all_to_all(packed, 'seq', split_axis=1, concat_axis=0, tiled=True)[:, 0]]
    psum x1 -> x0, waiting for transfers between devices: 30.7 us -> none  [local(): lax.psum(shards[1].astype(jnp.bfloat16), 'seq').astype(jnp.float32)]
  transfers between devices with their start and end apart: 19 -> 0, of which waited for: 16 -> 0; matrix products, arithmetic and copies ran while one was open for 5% -> 0% of each run, Pallas kernels for 0% -> 0%
where the time goes in v1:
time: 282 us
  Pallas kernels  269 us (95%)
  local copies, waits for them, and re-layouts  10.9 us (4%)
    pallas_call x1, Pallas kernels, block(): pl.pallas_call(kernel, out_shape=tuple((jax.ShapeDtypeStruct(s, d) for s,...  265 us

profile of v1, /device:TPU:25, one launch (start us, length us, event | category | flops | bytes accessed | tf_op | source)
XLA Modules:
  0.0 282.0 jit_solution(10748416522118226413)
XLA Ops:
  0.6 0.7 convert_element_type.11
  1.3 0.7 tile.4
  2.0 0.1 broadcast_in_dim_tile.6
  2.0 0.7 tile.5
  2.7 0.1 broadcast_in_dim_tile.7
  2.8 0.7 bitcast_convert_fusion
  3.5 1.3 concatenate.3.refs_1_
  4.7 264.6 %block.1 = (bf16[128,1024]{1,0:T(8,128)(2,1)}, bf16[128,1024]{1,0:T(8,128)(2,1)}, bf16[16,32,2304]{2,1,0:T(8,128)(2,1)}, bf16[16,3,16,1024]{3,2,1,0:T(8,128)(2,1...) custom-call(bf16[128,1024]{1,0:T(8,128)(2,1)} %refs_0_.1, f32[8,128]{1,0:T(8,128)} %concatenate.3.refs_1_, ...), custom_call_target="tpu_custom_call" | custom-call | tf_op jit(solution)/shard_map/block/pallas_call | solution.py:893
  269.3 1.3 slice_bitcast_fusion.2
  270.6 1.3 slice_bitcast_fusion
  271.9 0.0 copy-start
  271.9 1.7 copy-done
  273.5 0.0 copy-start.1
  273.5 1.4 copy-done.1
  274.9 0.0 copy-start.2
  274.9 1.1 copy-done.2
  276.1 0.0 copy-start.4
  276.1 0.0 copy-start.3
  276.1 4.5 %lay.1 = (f32[128,4608]{1,0:T(8,128)}, f32[128,4608]{1,0:T(8,128)}, f32[576,1024]{1,0:T(8,128)}, f32[128,1024]{1,0:T(8,128)}, f32[128,512]{1,0:T(8,128)}, /*index=5*/f32[128,512]{1,0:T(8,128)}, f32[128,1024]{1,0:T(8,128)}) custom-call(bf16[16,32,2304]{2,1,0:T(8,128)(2,1)S(1)} %copy-done, bf16[16,3,16,1024]{3,2,1,0:T(8,128)(2,1)S(1)} %copy-done.1, ...), custom_call_target="tpu_custom_call" | custom-call | tf_op jit(solution)/shard_map/lay/pallas_call | solution.py:951
  280.6 0.0 copy-done.4
  280.6 0.7 copy.30
  281.3 0.0 copy-done.3
  281.3 0.7 copy.31
  (1 shorter events, 0.0 us)
Async XLA Ops:
  271.9 1.7 copy-start
  273.5 1.4 copy-start.1
  274.9 1.1 copy-start.2
  276.1 4.5 %copy-start.4 = (bf16[128,1024]{1,0:T(8,128)(2,1)S(1)}, bf16[128,1024]{1,0:T(8,128)(2,1)}, u32[]{:S(2)}) copy-start(bf16[128,1024]{1,0:T(8,128)(2,1)} %get-tuple-element.58) | copy-start | bytes 786436
  276.1 5.2 %copy-start.3 = (bf16[128,1024]{1,0:T(8,128)(2,1)S(1)}, bf16[128,1024]{1,0:T(8,128)(2,1)}, u32[]{:S(2)}) copy-start(bf16[128,1024]{1,0:T(8,128)(2,1)} %get-tuple-element.59) | copy-start | bytes 786436

commit v2 on v1

--- a/solution.py
+++ b/solution.py
@@ -54,9 +54,15 @@
     def speer(self, k):
         return (self.dp, rem(self.sq + k + 16, 16))
 
-    def tpeer(self, t):
-        xl = self.xl if t == 0 else 1 - self.xl
-        return (self.z * 2 + xl, self.y * 4 + self.g)
+    def ypeer(self, k):
+        return (rem(self.y + k + 4, 4) * 2 + self.xl, self.sq)
+
+    def xring(self, t):
+        xl = self.xl if t == 3 else 1 - self.xl
+        return (self.y * 2 + xl, self.sq if t == 1 else self.z * 4 + (1 - self.xh) * 2 + self.c)
+
+    def xplace(self, t):
+        return (self.xl if t in (0, 3) else 1 - self.xl), (self.xh if t in (0, 1) else 1 - self.xh)
 
 
 def seg_rows(ids):
@@ -92,7 +98,7 @@
     ]
 
 
-INPUTS = ["tok", "meta", "wq", "wk", "wv", "wo", "wg", "wu", "wd", "cot"]
+INPUTS = ["tok", "seg", "ga", "gf", "gqk", "freq", "wq", "wk", "wv", "wo", "wg", "wu", "wd", "cot"]
 OUTPUTS = {
     "block_out": ((128, 1024), BF),
     "input_grad": ((128, 1024), BF),
@@ -104,7 +110,7 @@
 SCRATCH = {
     "tok_all": ((4, 128, 1024), BF),
     "cot_all": ((4, 128, 1024), BF),
-    "h_all": ((4, 128, 1024), BF),
+    "meta": ((8, 128), F32),
     "mseq": ((16, 8, 128), F32),
     "mdp": ((8, 8, 128), F32),
     "wqkv": ((8, 128, 512), BF),
@@ -112,8 +118,6 @@
     "wg_v": ((8, 128, 1152), BF),
     "wu_v": ((8, 128, 1152), BF),
     "wd_v": ((18, 64, 1024), BF),
-    "wg_s": ((64, 1152), BF),
-    "wu_s": ((64, 1152), BF),
     "st": ((16, 128), F32),
     "qk_raw": ((4, 128, 384), F32),
     "qz": ((4, 512, 128), BF),
@@ -153,17 +157,36 @@
     "dkvr": ((3, 4, 128, 256), BF),
     "dqr": ((4, 128, 256), F32),
     "dqkv": ((4, 128, 512), BF),
-    "p4s": ((3, 128, 1024), BF),
     "p4r": ((3, 128, 1024), BF),
-    "gF": ((8, 128, 2304), BF),
+    "gF": ((4, 2, 128, 2304), BF),
     "gD": ((18, 64, 1024), BF),
-    "gA": ((8, 128, 768), BF),
-    "r1F": ((8, 64, 2304), BF),
+    "gA": ((4, 2, 128, 768), BF),
+    "r1F": ((4, 2, 64, 2304), BF),
     "r1D": ((18, 32, 1024), BF),
-    "r1A": ((8, 64, 768), BF),
-    "r2F": ((16, 32, 2304), BF),
-    "r2D": ((16, 3, 16, 1024), BF),
-    "r2A": ((16, 32, 768), BF),
+    "sD": ((4, 2, 2, 32, 1024), BF),
+    "sX": ((2, 32, 1024), BF),
+    "ax": ((3, 4, 32, 1152), BF),
+    "at": ((4, 32, 1152), BF),
+    "ay": ((3, 32, 1152), BF),
+    "by": ((3, 2, 64, 1152), BF),
+    "bt": ((2, 64, 1152), BF),
+    "bx": ((3, 32, 1152), BF),
+    "adx": ((3, 4, 2, 16, 512), BF),
+    "adt": ((4, 2, 16, 512), BF),
+    "ady": ((3, 2, 16, 512), BF),
+    "bdy": ((3, 2, 2, 32, 512), BF),
+    "bdt": ((2, 2, 32, 512), BF),
+    "bdx": ((3, 2, 16, 512), BF),
+    "xx": ((3, 16, 1024), BF),
+    "xt": ((16, 1024), BF),
+    "xy": ((3, 16, 1024), BF),
+    "qax": ((3, 4, 32, 384), BF),
+    "qat": ((4, 32, 384), BF),
+    "qay": ((3, 32, 384), BF),
+    "qby": ((3, 2, 64, 384), BF),
+    "qbt": ((2, 64, 384), BF),
+    "qbx": ((3, 32, 384), BF),
+    "r1A": ((4, 2, 64, 768), BF),
     "oF": ((32, 2304), BF),
     "oD": ((3, 16, 1024), BF),
     "oA": ((32, 768), BF),
@@ -172,7 +195,7 @@
     "gs1s": ((8, 128), F32),
     "gs2": ((16, 8, 128), F32),
 }
-NSEM = 320
+NSEM = 400
 
 
 class Refs:
@@ -205,6 +228,12 @@
 
     def got(self, dst, i):
         self.copy(dst, dst, i, self.p.sib()).wait_recv()
+
+    def flush(self, i):
+        for src, j in self.sent:
+            if j == i:
+                self.copy(src, src, i, self.p.sib()).wait_send()
+        self.sent = [e for e in self.sent if e[1] != i]
 
     def finish(self):
         for src, i in self.sent:
@@ -230,37 +259,151 @@
     zk = pl.ds(pl.multiple_of(p.z * 128, 128), 128)
     dps = [rem(p.dp + 8 - k, 8) for k in range(8)]
 
-    i_loc = m.take(3)
-    stage = []
-    for src, dst, i in ((r.wg, r.wg_s, i_loc), (r.wu, r.wu_s, i_loc + 1)):
+    i_loc = m.take(4)
+    parts = ((r.wq, zq, 0, 256), (r.wk, zk, 256, 128), (r.wv, zk, 384, 128))
+    for w, cols, at, wid in parts:
+        m.local(w.at[half, cols], r.wqkv.at[p.dp, half, pl.ds(at, wid)], i_loc).start()
+    m.local(r.wo.at[half], r.wo_v.at[p.dp, half], i_loc + 1).start()
+
+    def down_pieces(d):
+        out = []
+        for n in range(2):
+            u = rem(2 * p.z + n - d + 8, 8)
+            big = 9 * d + u
+            out.append((u, 2 * lax.div(big, 8) + rem(big, 2)))
+        big = 9 * d + 8
+        return out + [(8, 2 * lax.div(big, 8) + rem(big, 2))], lax.div(d, 2) == p.z
+
+    c32 = p.c * 32
+    h32 = pl.ds(pl.multiple_of(c32, 32), 32)
+    o32 = pl.ds(pl.multiple_of(32 - c32, 32), 32)
+    i_ld = m.take(3)
+    pieces, has_extra = down_pieces(p.dp)
+
+    def down_local(n):
+        u, hidx = pieces[n]
+        src = r.wd.at[pl.ds(pl.multiple_of(u * 64 + c32, 32), 32)]
+        return pltpu.make_async_copy(src, r.wd_v.at[hidx, h32], rsem.at[i_ld + n])
+
+    for n in range(2):
+        down_local(n).start()
+
+    @pl.when(has_extra)
+    def _():
+        down_local(2).start()
+
+    for src, dst, i in ((r.wg, r.wg_v, i_loc + 2), (r.wu, r.wu_v, i_loc + 3)):
         for t in range(9):
             cols = pl.ds(pl.multiple_of(t * 512 + p.z * 128, 128), 128)
-            m.local(src.at[half, cols], dst.at[:, pl.ds(t * 128, 128)], i).start()
-        stage.append((dst, i))
-    parts = ((r.wq, zq, 0, 256), (r.wk, zk, 256, 128), (r.wv, zk, 384, 128))
-    for w, cols, at, wid in parts:
-        m.local(w.at[half, cols], r.wqkv.at[p.dp, half, pl.ds(at, wid)], i_loc + 2).start()
+            m.local(src.at[half, cols], dst.at[p.dp, half, pl.ds(t * 128, 128)], i).start()
+
+    r.meta[0:1, :] = r.ga[...].astype(F32)
+    r.meta[1:2, :] = r.gf[...].astype(F32)
+    r.meta[2:3, :] = r.seg[...].astype(F32)
+    r.meta[3:8, :] = jnp.zeros((5, 128), F32)
 
     bar = pltpu.get_barrier_semaphore()
     for k in range(1, 16):
         pl.semaphore_signal(bar, inc=1, device_id=p.speer(k), device_id_type=MESH)
     for k in range(1, 8):
         pl.semaphore_signal(bar, inc=1, device_id=p.dpeer(k), device_id_type=MESH)
-    far = []
-    for k in range(8):
-        far.append((p.dpeer(k)[0], (p.z * 4 + (1 - p.xh) * 2 + p.c)))
-    for k in range(1, 8):
-        pl.semaphore_signal(bar, inc=1, device_id=far[k], device_id_type=MESH)
-    pl.semaphore_wait(bar, 29)
-
+    pl.semaphore_signal(bar, inc=1, device_id=p.xring(2), device_id_type=MESH)
+    pl.semaphore_wait(bar, 23)
+
+    class Shards:
+        def __init__(self, buf, i_share):
+            self.buf, self.share = buf, i_share
+            self.iy, self.ix = m.take(4), m.take(8)
+
+        def row(self, k, xl):
+            return rem(p.y - k + 4, 4) * 2 + xl
+
+        def quarter(self, t):
+            return pl.ds(pl.multiple_of(p.c * 64 + (t - 1) * 32, 32), 32)
+
+        def along_y(self):
+            s = self.buf.at[p.dp, half]
+            for k in (2, 1, 3):
+                m.send(s, s, self.iy + k, p.ypeer(k))
+
+        def along_x(self, k):
+            d = self.row(k, p.xl)
+            if k:
+                m.got(self.buf.at[d, half], self.iy + k)
+            for t in (1, 2):
+                s = self.buf.at[d, self.quarter(t)]
+                m.send(s, s, self.ix + 2 * k + t - 1, p.xring(t))
+
+        def to_core(self):
+            for k in range(4):
+                d = self.row(k, 1 - p.xl)
+                for t in (1, 2):
+                    m.got(self.buf.at[d, self.quarter(t)], self.ix + 2 * k + t - 1)
+            s = self.buf.at[:, half]
+            m.send(s, s, self.share, p.sib())
+
+        def done(self):
+            m.got(self.buf.at[:, other], self.share)
+
+    class Down:
+        def __init__(self, i_share):
+            self.share = i_share
+            self.iy, self.ix = m.take(12), m.take(24)
+
+        def move(self, d, t, i, dev, act):
+            where, more = down_pieces(d)
+            for n in range(3):
+                rows = h32 if t == 0 else pl.ds(pl.multiple_of(c32 + (t - 1) * 16, 16), 16)
+                s = r.wd_v.at[where[n][1], rows]
+                if n < 2:
+                    act(m.copy(s, s, i + n, dev))
+                else:
+
+                    @pl.when(more)
+                    def _():
+                        act(m.copy(s, s, i + n, dev))
+
+        def along_y(self):
+            for k in (2, 1, 3):
+                self.move(p.dp, 0, self.iy + 3 * k, p.ypeer(k), lambda q: q.start())
+
+        def along_x(self, k):
+            d = rem(p.y - k + 4, 4) * 2 + p.xl
+            if k:
+                self.move(d, 0, self.iy + 3 * k, p.sib(), lambda q: q.wait_recv())
+            for t in (1, 2):
+                self.move(d, t, self.ix + 6 * k + 3 * (t - 1), p.xring(t), lambda q: q.start())
+
+        def to_core(self):
+            for k in range(4):
+                d = rem(p.y - k + 4, 4) * 2 + 1 - p.xl
+                for t in (1, 2):
+                    self.move(d, t, self.ix + 6 * k + 3 * (t - 1), p.sib(), lambda q: q.wait_recv())
+            m.send(r.wd_v.at[:, h32], r.wd_v.at[:, h32], self.share, p.sib())
+
+        def done(self):
+            m.got(r.wd_v.at[:, o32], self.share)
+
+        def finish(self):
+            for k in (1, 2, 3):
+                self.move(p.dp, 0, self.iy + 3 * k, p.sib(), lambda q: q.wait_send())
+            for k in range(4):
+                d = rem(p.y - k + 4, 4) * 2 + p.xl
+                for t in (1, 2):
+                    self.move(d, t, self.ix + 6 * k + 3 * (t - 1), p.sib(), lambda q: q.wait_send())
+
+    i_share = m.take(5)
+    w_qkv = Shards(r.wqkv, i_share)
+    w_o = Shards(r.wo_v, i_share + 1)
+    w_d = Down(i_share + 2)
+    w_g = Shards(r.wg_v, i_share + 3)
+    w_u = Shards(r.wu_v, i_share + 4)
     i_tok = m.take(4)
-    for dz in (1, 3, 2):
+    for dz in (2, 1, 3):
         m.send(r.tok, r.tok_all.at[dz], i_tok + dz, p.zpeer(dz))
-    i_w = m.take(8)
-    for k in range(1, 8):
-        for w, cols, at, wid in parts:
-            m.copy(w.at[half, cols], r.wqkv.at[p.dp, half, pl.ds(at, wid)], i_w + k, p.dpeer(k)).start()
-        m.sent.append((r.wqkv.at[0, half], i_w + k))
+    m.local(r.wqkv.at[0, half], r.wqkv.at[0, half], i_loc).wait()
+    w_qkv.along_y()
+    w_qkv.along_x(0)
     i_mseq = m.take(16)
     for k in range(1, 16):
         m.send(r.meta, r.mseq.at[p.sq], i_mseq + k, p.speer(k))
@@ -269,12 +412,26 @@
         m.send(r.meta, r.mdp.at[p.dp], i_mdp + k, p.dpeer(k))
     r.mseq[p.sq] = r.meta[...]
     r.mdp[p.dp] = r.meta[...]
+    m.local(r.wo_v.at[0, half], r.wo_v.at[0, half], i_loc + 1).wait()
+    w_o.along_y()
+    for n in range(2):
+        down_local(n).wait()
+
+    @pl.when(has_extra)
+    def _():
+        down_local(2).wait()
+
+    w_d.along_y()
+    m.local(r.wg_v.at[0, half], r.wg_v.at[0, half], i_loc + 2).wait()
+    w_g.along_y()
+    m.local(r.wu_v.at[0, half], r.wu_v.at[0, half], i_loc + 3).wait()
+    w_u.along_y()
 
     for k in range(1, 16):
         m.got(r.mseq.at[rem(p.sq + 16 - k, 16)], i_mseq + k)
     r.st[...] = seg_rows(r.mseq[:, 2, :])
     lanesign = jnp.where(lane_half(), -1.0, 1.0)
-    freq = r.meta[5:6, :]
+    freq = r.freq[...]
     for dz in range(4):
         i = 4 * z_of(dz) + p.g
         row = r.st[pl.ds(i, 1), :]
@@ -287,64 +444,14 @@
     gain1 = jnp.concatenate([r.mdp[j, 0:1, :] for j in range(8)], axis=1)
     gain2 = jnp.concatenate([r.mdp[j, 1:2, :] for j in range(8)], axis=1)
 
-    m.local(r.wqkv.at[0, half], r.wqkv.at[0, half], i_loc + 2).wait()
-    for k in range(1, 8):
-        m.got(r.wqkv.at[dps[k], half], i_w + k)
-    i_share = m.take(5)
-    m.send(r.wqkv.at[:, half], r.wqkv.at[:, half], i_share, p.sib())
-
-    i_wo = m.take(8)
-    m.local(r.wo.at[half], r.wo_v.at[p.dp, half], i_wo).start()
-    for k in range(1, 8):
-        m.send(r.wo.at[half], r.wo_v.at[p.dp, half], i_wo + k, p.dpeer(k))
-    for dst, i in stage:
-        m.local(dst, dst, i).wait()
-    i_wd = m.take(1)
-    i_wds = m.take(24)
-    i_wg = m.take(8)
-    i_wu = m.take(8)
-
-    def down_pieces(d):
-        out = []
-        for n in range(2):
-            u = rem(2 * p.z + n - d + 8, 8)
-            big = 9 * d + u
-            out.append((u, 2 * lax.div(big, 8) + rem(big, 2)))
-        big = 9 * d + 8
-        return out, (8, 2 * lax.div(big, 8) + rem(big, 2)), lax.div(d, 2) == p.z
-
-    pieces, extra, has_extra = down_pieces(p.dp)
-    c32 = p.c * 32
-
-    def down_copy(k, n, piece):
-        u, hidx = piece
-        src = r.wd.at[pl.ds(pl.multiple_of(u * 64 + c32, 32), 32)]
-        dst = r.wd_v.at[hidx, pl.ds(pl.multiple_of(c32, 32), 32)]
-        if k == 0:
-            return pltpu.make_async_copy(src, dst, rsem.at[i_wd])
-        return pltpu.make_async_remote_copy(
-            src_ref=src, dst_ref=dst, send_sem=ssem.at[i_wds + 3 * k + n], recv_sem=rsem.at[i_wd],
-            device_id=p.dpeer(k), device_id_type=MESH,
-        )
-
-    for k in range(8):
-        for n in range(2):
-            down_copy(k, n, pieces[n]).start()
-
-    @pl.when(has_extra)
-    def _():
-        for k in range(8):
-            down_copy(k, 2, extra).start()
-
-    for src, dst, i in ((r.wg_s, r.wg_v, i_wg), (r.wu_s, r.wu_v, i_wu)):
-        for k in range(1, 8):
-            m.send(src, dst.at[p.dp, half], i + k, p.dpeer(k))
-        dst[p.dp, half] = src[...]
-    m.got(r.wqkv.at[:, other], i_share)
+    for k in (1, 3, 2):
+        w_qkv.along_x(k)
+    w_qkv.to_core()
+    w_qkv.done()
 
     wfull = r.wqkv[...].reshape(1024, 512)
-    qg = r.meta[3:4, :]
-    kg = r.meta[4:5, :]
+    qg = r.gqk[0:1, :].astype(F32)
+    kg = r.gqk[1:2, :].astype(F32)
     i_kv = m.take(4)
     i_kvx = m.take(4)
     i_kvf = m.take(4)
@@ -353,7 +460,7 @@
         x = x.astype(F32)
         r1 = lax.rsqrt(jnp.mean(x * x, axis=1, keepdims=True) + EPS)
         h = (x * r1 * gain1).astype(BF)
-        r.h_all[dz] = h
+        r.tok_all[dz] = h
         o = dot(h, wfull)
         cs, sn = r.cosr[dz], r.sinr[dz]
         r.qk_raw[dz] = o[:, 0:384]
@@ -396,6 +503,8 @@
         return carry
 
     lax.fori_loop(0, 16, turn, 0)
+    for k in (0, 1, 3, 2):
+        w_o.along_x(k)
 
     def allowed_rows(i):
         row = r.st[pl.ds(i, 1), :].astype(jnp.int32)
@@ -440,16 +549,17 @@
             m.send(r.o_s.at[dz], r.o_in.at[p.z], i_o + dz, p.zpeer(-dz))
         else:
             r.o_in[p.z] = r.o_s[0]
-
-    m.local(r.wo_v.at[0, half], r.wo_v.at[0, half], i_wo).wait()
-    for k in range(1, 8):
-        m.got(r.wo_v.at[dps[k], half], i_wo + k)
-    m.send(r.wo_v.at[:, half], r.wo_v.at[:, half], i_share + 1, p.sib())
+        if j < 3:
+            for k in (0, 1, 3, 2):
+                (w_d, w_g, w_u)[j].along_x(k)
+        if j == 1:
+            w_o.to_core()
+
     for dz in range(1, 4):
         m.got(r.o_in.at[rem(p.z + dz, 4)], i_o + dz)
     for j in range(4):
         r.o_own[:, j * 256:(j + 1) * 256] = r.o_in[j]
-    m.got(r.wo_v.at[:, other], i_share + 1)
+    w_o.done()
     x0 = r.tok[...].astype(F32)
     middle = x0 + dot(r.o_own[...], r.wo_v[...].reshape(1024, 1024))
     r.mid[...] = middle
@@ -459,17 +569,12 @@
     for dz in (2, 1, 3):
         m.send(r.h2.at[0], r.h2.at[dz], i_h2 + dz, p.zpeer(dz))
 
-    pltpu.make_async_copy(r.wd_v.at[:, pl.ds(0, 32)], r.wd_v.at[:, pl.ds(0, 32)], rsem.at[i_wd]).wait()
-    h32 = pl.ds(pl.multiple_of(c32, 32), 32)
-    o32 = pl.ds(pl.multiple_of(32 - c32, 32), 32)
-    m.send(r.wd_v.at[:, h32], r.wd_v.at[:, h32], i_share + 2, p.sib())
-    for n, (dst, i) in enumerate(((r.wg_v, i_wg), (r.wu_v, i_wu))):
-        for k in range(1, 8):
-            m.got(dst.at[dps[k], half], i + k)
-        m.send(dst.at[:, half], dst.at[:, half], i_share + 3 + n, p.sib())
+    w_d.to_core()
+    w_g.to_core()
+    w_u.to_core()
     for dz in range(1, 4):
         m.got(r.cot_all.at[dz], i_cot + dz)
-    m.got(r.wd_v.at[:, o32], i_share + 2)
+    w_d.done()
     wd = r.wd_v[...].reshape(1152, 1024)
     cots = r.cot_all[...].reshape(512, 1024)
 
@@ -482,8 +587,8 @@
         return carry
 
     lax.fori_loop(0, 3, dm_tile, 0)
-    m.got(r.wg_v.at[:, other], i_share + 3)
-    m.got(r.wu_v.at[:, other], i_share + 4)
+    w_g.done()
+    w_u.done()
 
     i_p2 = m.take(4)
     for pair in range(2):
@@ -522,12 +627,12 @@
 
     def gate_up_tile(t, carry):
         cols = cols384(t)
-        r.gF[:, :, cols] = dot(h2t, r.dg[:, :, cols].reshape(512, 384), TN).astype(BF).reshape(8, 128, 384)
-        r.gF[:, :, cols384(t + 3)] = dot(h2t, r.du[:, :, cols].reshape(512, 384), TN).astype(BF).reshape(8, 128, 384)
+        r.gF[:, :, :, cols] = dot(h2t, r.dg[:, :, cols].reshape(512, 384), TN).astype(BF).reshape(4, 2, 128, 384)
+        r.gF[:, :, :, cols384(t + 3)] = dot(h2t, r.du[:, :, cols].reshape(512, 384), TN).astype(BF).reshape(4, 2, 128, 384)
         return carry
 
     lax.fori_loop(0, 3, gate_up_tile, 0)
-    m.send(r.gF.at[:, other], r.r1F, i_r1, p.sib())
+    m.send(r.gF.at[:, :, other], r.r1F, i_r1, p.sib())
 
     def down_tile(t, carry):
         w = r.mixed[:, :, cols384(t)].reshape(512, 384)
@@ -578,54 +683,118 @@
     m.got(r.r1D, i_r1 + 1)
 
     def add_core(d, carry):
-        r.r1F[d] = (r.r1F[d].astype(F32) + r.gF[d, half].astype(F32)).astype(BF)
+        a, b = lax.div(d, 2), rem(d, 2)
+        r.r1F[a, b] = (r.r1F[a, b].astype(F32) + r.gF[a, b, half].astype(F32)).astype(BF)
+        where, more = down_pieces(d)
+        for n in range(2):
+            t = where[n][1]
+            r.sD[a, b, n] = (r.r1D[t].astype(F32) + r.gD[t, h32].astype(F32)).astype(BF)
+
+        @pl.when(more)
+        def _():
+            t = where[2][1]
+            r.sX[b] = (r.r1D[t].astype(F32) + r.gD[t, h32].astype(F32)).astype(BF)
+
         return carry
 
     lax.fori_loop(0, 8, add_core, 0)
 
-    def add_core_down(d, carry):
-        r.r1D[d] = (r.r1D[d].astype(F32) + r.gD[d, h32].astype(F32)).astype(BF)
-        return carry
-
-    lax.fori_loop(0, 18, add_core_down, 0)
-    i_r2 = m.take(16)
-    i_r2d = m.take(16)
-    i_r2e = m.take(16)
-
-    def slots():
-        for t in range(2):
-            for k in range(8):
-                yield t * 8 + k, t, k
-
-    def target(t, k):
-        return p.dpeer(k) if t == 0 else far[k]
-
-    def rows32(t):
-        x = p.xh if t == 0 else 1 - p.xh
-        return pl.ds(pl.multiple_of(x * 32, 32), 32), pl.ds(pl.multiple_of(x * 16, 16), 16)
-
-    for s, t, k in slots():
-        d = rem(p.dp + k, 8)
-        r32, r16 = rows32(t)
-        two, more, cond = down_pieces(d)
-        if s == 0:
-            r.r2F[0] = r.r1F[d, r32]
-            for n in range(2):
-                r.r2D[0, n] = r.r1D[two[n][1], r16]
-
-            @pl.when(cond)
-            def _():
-                r.r2D[0, 2] = r.r1D[more[1], r16]
-
-            continue
-        m.send(r.r1F.at[d, r32], r.r2F.at[s], i_r2 + s, target(t, k))
-        for n in range(2):
-            m.copy(r.r1D.at[two[n][1], r16], r.r2D.at[s, n], i_r2d + s, target(t, k)).start()
-        m.sent.append((r.r2D.at[0, pl.ds(0, 2)], i_r2d + s))
-
-        @pl.when(cond)
-        def _():
-            m.copy(r.r1D.at[more[1], r16], r.r2D.at[s, 2], i_r2e + s, target(t, k)).start()
+    def rows_of(x, n):
+        return pl.ds(pl.multiple_of(x * n, n), n)
+
+    class XFirst:
+        def __init__(self, src, mid1, tot, mid2):
+            self.src, self.mid1, self.tot, self.mid2 = src, mid1, tot, mid2
+            self.i1, self.i2 = m.take(4), m.take(4)
+
+        def one(self):
+            for t in (3, 1, 2):
+                m.send(self.src(t), self.mid1.at[t - 1], self.i1 + t, p.xring(t))
+
+        def two(self):
+            for t in (1, 2, 3):
+                m.got(self.mid1.at[t - 1], self.i1 + t)
+
+            def add(n, carry):
+                v = self.src(0).at[n][...].astype(F32)
+                for t in range(3):
+                    v = v + self.mid1[t, n].astype(F32)
+                self.tot[n] = v.astype(BF)
+                return carry
+
+            lax.fori_loop(0, 4, add, 0)
+            for k in (2, 1, 3):
+                m.send(self.tot.at[rem(p.y + k, 4)], self.mid2.at[k - 1], self.i2 + k, p.ypeer(k))
+
+        def sum(self):
+            for k in (1, 2, 3):
+                m.got(self.mid2.at[k - 1], self.i2 + k)
+            v = self.tot[p.y].astype(F32)
+            for k in range(3):
+                v = v + self.mid2[k].astype(F32)
+            return v.astype(BF)
+
+    class YFirst:
+        def __init__(self, src, part, mid1, tot, mid2):
+            self.src, self.part, self.mid1, self.tot, self.mid2 = src, part, mid1, tot, mid2
+            self.i1, self.i2 = m.take(4), m.take(4)
+
+        def one(self):
+            for k in (2, 1, 3):
+                m.send(self.src(rem(p.y + k, 4)), self.mid1.at[k - 1], self.i1 + k, p.ypeer(k))
+
+        def two(self):
+            for k in (1, 2, 3):
+                m.got(self.mid1.at[k - 1], self.i1 + k)
+
+            def add(n, carry):
+                v = self.src(p.y).at[n][...].astype(F32)
+                for k in range(3):
+                    v = v + self.mid1[k, n].astype(F32)
+                self.tot[n] = v.astype(BF)
+                return carry
+
+            lax.fori_loop(0, 2, add, 0)
+            for t in (3, 1, 2):
+                m.send(self.part(self.tot, t), self.mid2.at[t - 1], self.i2 + t, p.xring(t))
+
+        def sum(self):
+            for t in (1, 2, 3):
+                m.got(self.mid2.at[t - 1], self.i2 + t)
+            v = self.part(self.tot, 0)[...].astype(F32)
+            for t in range(3):
+                v = v + self.mid2[t].astype(F32)
+            return v.astype(BF)
+
+    def rows_x(buf, c0, c1):
+        return lambda t: buf.at[:, p.xplace(t)[0], rows_of(p.xplace(t)[1], 32), c0:c1]
+
+    def rows_y(buf, c0, c1):
+        return lambda y: buf.at[y, :, :, c0:c1]
+
+    def part_y(tot, t):
+        xl, xh = p.xplace(t)
+        return tot.at[xl, rows_of(xh, 32)]
+
+    def part_d(tot, t):
+        xl, xh = p.xplace(t)
+        return tot.at[xl, :, rows_of(xh, 16)]
+
+    sums = [
+        XFirst(rows_x(r.r1F, 0, 1152), r.ax, r.at, r.ay),
+        YFirst(rows_y(r.r1F, 1152, 2304), part_y, r.by, r.bt, r.bx),
+        XFirst(
+            lambda t: r.sD.at[:, p.xplace(t)[0], :, rows_of(p.xplace(t)[1], 16), 0:512], r.adx, r.adt, r.ady
+        ),
+        YFirst(lambda y: r.sD.at[y, :, :, :, 512:1024], part_d, r.bdy, r.bdt, r.bdx),
+    ]
+    for e in sums:
+        e.one()
+    i_x1 = m.take(4)
+    i_x2 = m.take(4)
+    for t in (3, 1, 2):
+        xl, xh = p.xplace(t)
+        m.send(r.sX.at[xl, rows_of(xh, 16)], r.xx.at[t - 1], i_x1 + t, p.xring(t))
 
     r.dkv[...] = jnp.zeros_like(r.dkv)
     for dz in (0, 1, 3, 2):
@@ -676,53 +845,47 @@
     m.send(r.dkvb.at[:, gxs], r.dkvr.at[2], i_dkv + 2, xs)
     m.send(r.dkvb.at[:, gs], r.dkvr.at[0], i_dkv, p.sib())
 
+    for e in sums:
+        e.two()
+    for t in (1, 2, 3):
+        m.got(r.xx.at[t - 1], i_x1 + t)
+    v = r.sX[p.xl, rows_of(p.xh, 16)].astype(F32)
+    for t in range(3):
+        v = v + r.xx[t].astype(F32)
+    r.xt[...] = v.astype(BF)
+    kz = rem(p.z - p.y + 4, 4)
+
+    @pl.when(kz != 0)
+    def _():
+        m.copy(r.xt, r.xy.at[kz - 1], i_x2 + kz, (p.z * 2 + p.xl, p.sq)).start()
+
     for dz in range(1, 4):
         m.got(r.o_full.at[dz], i_of + dz)
         m.got(r.da_c.at[dz], i_dc + dz)
         m.got(r.p3r.at[dz - 1], i_p3 + dz)
-    r.gA[:, :, 512:768] = dot(
+    r.gA[:, :, :, 512:768] = dot(
         r.o_full[...].reshape(512, 1024), r.da_c[...].reshape(512, 256), TN
-    ).astype(BF).reshape(8, 128, 256)
+    ).astype(BF).reshape(4, 2, 128, 256)
     r.block_out[...] = (
         r.mid[...] + r.own3[...] + r.p3r[0].astype(F32) + r.p3r[1].astype(F32) + r.p3r[2].astype(F32)
     ).astype(BF)
 
-    def got_ffn():
-        for s, t, k in slots():
-            if s == 0:
-                continue
-            m.got(r.r2F.at[s], i_r2 + s)
-            m.got(r.r2D.at[s, pl.ds(0, 2)], i_r2d + s)
-        mine = lax.div(p.dp, 2) == p.z
-
-        @pl.when(mine)
-        def _():
-            for s, t, k in slots():
-                if s:
-                    m.got(r.r2D.at[s, 2], i_r2e + s)
-
-        def add(s, total):
-            return total + r.r2F[s].astype(F32)
-
-        r.oF[...] = lax.fori_loop(1, 16, add, r.r2F[0].astype(F32)).astype(BF)
-
-        def addd(s, total):
-            return total + r.r2D[s, 0:2].astype(F32)
-
-        r.oD[0:2] = lax.fori_loop(1, 16, addd, r.r2D[0, 0:2].astype(F32)).astype(BF)
-
-        @pl.when(mine)
-        def _():
-            def adde(s, total):
-                return total + r.r2D[s, 2].astype(F32)
-
-            r.oD[2] = lax.fori_loop(1, 16, adde, r.r2D[0, 2].astype(F32)).astype(BF)
-
-        @pl.when(jnp.logical_not(mine))
-        def _():
-            r.oD[2] = jnp.zeros((16, 1024), BF)
-
-    got_ffn()
+    r.oF[:, 0:1152] = sums[0].sum()
+    r.oF[:, 1152:2304] = sums[1].sum()
+    r.oD[0:2, :, 0:512] = sums[2].sum()
+    r.oD[0:2, :, 512:1024] = sums[3].sum()
+
+    @pl.when(kz == 0)
+    def _():
+        v = r.xt[...].astype(F32)
+        for k in (1, 2, 3):
+            m.got(r.xy.at[k - 1], i_x2 + k)
+            v = v + r.xy[k - 1].astype(F32)
+        r.oD[2] = v.astype(BF)
+
+    @pl.when(kz != 0)
+    def _():
+        r.oD[2] = jnp.zeros((16, 1024), BF)
 
     def seq_at(z, g):
         return rem(z + 8, 4) * 4 + g
@@ -794,28 +957,31 @@
             r.dqkv[dz, :, b * 128:(b + 1) * 128] = (f * wn - v * (f * f * f) * head_mean(wn * v)).astype(BF)
         r.dqkv[dz, :, 384:512] = dkv[:, 128:256].astype(BF)
     i_p4 = m.take(4)
+    for dz in range(1, 4):
+        m.flush(i_p2 + dz)
     for dz in (2, 1, 3):
-        r.p4s[dz - 1] = dot(r.dqkv[dz], r.wqkv[...].reshape(1024, 512), NT).astype(BF)
-        m.send(r.p4s.at[dz - 1], r.p4r.at[dz - 1], i_p4 + dz, p.zpeer(-dz))
+        r.p2s[dz - 1] = dot(r.dqkv[dz], r.wqkv[...].reshape(1024, 512), NT).astype(BF)
+        m.send(r.p2s.at[dz - 1], r.p4r.at[dz - 1], i_p4 + dz, p.zpeer(-dz))
     r.own[...] = dot(r.dqkv[0], r.wqkv[...].reshape(1024, 512), NT)
-    r.gA[:, :, 0:512] = dot(
-        r.h_all[...].reshape(512, 1024), r.dqkv[...].reshape(512, 512), TN
-    ).astype(BF).reshape(8, 128, 512)
-    m.send(r.gA.at[:, other], r.r1A, i_r1 + 2, p.sib())
+    r.gA[:, :, :, 0:512] = dot(
+        r.tok_all[...].reshape(512, 1024), r.dqkv[...].reshape(512, 512), TN
+    ).astype(BF).reshape(4, 2, 128, 512)
+    m.send(r.gA.at[:, :, other], r.r1A, i_r1 + 2, p.sib())
     ag_f.first()
     ag_d.first()
     m.got(r.r1A, i_r1 + 2)
-    r.r1A[...] = (r.r1A[...].astype(F32) + r.gA[:, half].astype(F32)).astype(BF)
-    i_r2a = m.take(16)
-    for s, t, k in slots():
-        d = rem(p.dp + k, 8)
-        r32, _ = rows32(t)
-        if s == 0:
-            r.r2A[0] = r.r1A[d, r32]
-        else:
-            m.send(r.r1A.at[d, r32], r.r2A.at[s], i_r2a + s, target(t, k))
+    r.r1A[...] = (r.r1A[...].astype(F32) + r.gA[:, :, half].astype(F32)).astype(BF)
+    sums_a = [
+        XFirst(rows_x(r.r1A, 0, 384), r.qax, r.qat, r.qay),
+        YFirst(rows_y(r.r1A, 384, 768), part_y, r.qby, r.qbt, r.qbx),
+    ]
+    for e in sums_a:
+        e.one()
     ag_f.second()
     ag_d.second()
+
+    for e in sums_a:
+        e.two()
 
     for dz in range(1, 4):
         m.got(r.p4r.at[dz - 1], i_p4 + dz)
@@ -846,14 +1012,8 @@
         m.send(r.gs1s, r.gs2.at[k], i_s2 + k, p.speer(k))
     r.gs2[0] = r.gs1s[...]
 
-    for s, t, k in slots():
-        if s:
-            m.got(r.r2A.at[s], i_r2a + s)
-
-    def adda(s, total):
-        return total + r.r2A[s].astype(F32)
-
-    r.oA[...] = lax.fori_loop(1, 16, adda, r.r2A[0].astype(F32)).astype(BF)
+    r.oA[:, 0:384] = sums_a[0].sum()
+    r.oA[:, 384:768] = sums_a[1].sum()
     ag_a.first()
     ag_f.third()
     ag_d.third()
@@ -867,22 +1027,11 @@
     ag_a.last()
 
     m.finish()
-    for k in range(1, 8):
-        for n in range(2):
-            down_copy(k, n, pieces[n]).wait_send()
-
-    @pl.when(has_extra)
+    w_d.finish()
+
+    @pl.when(kz != 0)
     def _():
-        for k in range(1, 8):
-            down_copy(k, 2, extra).wait_send()
-
-    for s, t, k in slots():
-        if s:
-            _, more, cond = down_pieces(rem(p.dp + k, 8))
-
-            @pl.when(cond)
-            def _():
-                m.copy(r.r1D.at[more[1], pl.ds(0, 16)], r.r2D.at[s, 2], i_r2e + s, p.sib()).wait_send()
+        m.copy(r.xt, r.xt, i_x2 + kz, p.sib()).wait_send()
 
     assert m.n <= NSEM, m.n
 
@@ -893,7 +1042,7 @@
     return pl.pallas_call(
         kernel,
         out_shape=tuple(jax.ShapeDtypeStruct(s, d) for s, d in OUTPUTS.values()),
-        in_specs=[vm, vm] + [hb] * 7 + [vm],
+        in_specs=[vm] * 6 + [hb] * 7 + [vm],
         out_specs=tuple(hb if name[0] == "f" else vm for name in OUTPUTS),
         scratch_shapes=[pltpu.VMEM(s, d) for s, d in SCRATCH.values()]
         + [pltpu.SemaphoreType.DMA((NSEM,)), pltpu.SemaphoreType.DMA((NSEM,))],
@@ -965,19 +1114,13 @@
 ):
     inverse = ROPE_BASE ** (-(np.arange(32).astype(np.float32) * np.float32(2.0) / np.float32(64)))
     freq = jnp.asarray(np.tile(inverse.astype(np.float32), 4)[None])
-    meta = jnp.concatenate(
-        [
-            attn_gain.astype(F32)[None],
-            ffn_gain.astype(F32)[None],
-            segment_ids.astype(F32),
-            jnp.tile(query_gain.astype(F32), 2)[None],
-            jnp.tile(key_gain.astype(F32), 2)[None],
-            freq,
-            jnp.zeros((2, 128), F32),
-        ],
-        axis=0,
+    gqk = jnp.stack([jnp.tile(query_gain, 2), jnp.tile(key_gain, 2)])
+    o = block(
+        (
+            tokens, segment_ids, attn_gain[None], ffn_gain[None], gqk, freq, w_query, w_key, w_value,
+            w_out, w_gate, w_up, w_down, cotangent,
+        )
     )
-    o = block((tokens, meta, w_query, w_key, w_value, w_out, w_gate, w_up, w_down, cotangent))
     o = dict(zip(OUTPUTS, o))
     small = o["g_small"]
     w = lay_out(o["fF"], o["fD"], o["fA"])

time: 282 us -> 202 us (0.72)
  Pallas kernels: 269 us -> 190 us
    pallas_call x1, Pallas kernels: 265 us -> 185 us  [block(): pl.pallas_call(kernel, out_shape=tuple((jax.ShapeDtypeStruct(s, d) for s,...]
where the time goes in v2:
time: 202 us; the launch traced here: 201 us
  Pallas kernels  190 us (94%)
  local copies, waits for them, and re-layouts  9.66 us (5%)
    pallas_call x1, Pallas kernels, block(): pl.pallas_call(kernel, out_shape=tuple((jax.ShapeDtypeStruct(s, d) for s,...  185 us
    unnamed x12, local copies, waits for them, and re-layouts  5.62 us
    pallas_call x1, Pallas kernels, lay_out(): pl.pallas_call(lay_kernel, out_shape=tuple((jax.ShapeDtypeStruct(s, F32)...  4.52 us

profile of v2, /device:TPU:25, one launch (start us, length us, event | category | flops | bytes accessed | tf_op | source)
XLA Modules:
  0.0 200.7 jit_solution(4516167549413271793)
XLA Ops:
  0.6 0.7 tile.4
  1.3 0.1 stack_tile.6
  1.4 0.7 tile.5
  2.0 0.1 stack_tile.7
  2.1 0.5 pad_maximum_fusion.refs_4_
  2.7 185.3 %block.1 = (bf16[128,1024]{1,0:T(8,128)(2,1)}, bf16[128,1024]{1,0:T(8,128)(2,1)}, bf16[16,32,2304]{2,1,0:T(8,128)(2,1)}, bf16[16,3,16,1024]{3,2,1,0:T(8,128)(2,1...) custom-call(bf16[128,1024]{1,0:T(8,128)(2,1)} %refs_0_.1, s32[1,128]{1,0:T(1,128)} %refs_1_.1, ...), custom_call_target="tpu_custom_call" | custom-call | tf_op jit(solution)/shard_map/block/pallas_call | solution.py:1042
  188.0 1.3 slice_bitcast_fusion.2
  189.2 1.3 slice_bitcast_fusion
  190.5 0.0 copy-start
  190.5 1.7 copy-done
  192.2 0.0 copy-start.1
  192.2 1.4 copy-done.1
  193.6 0.0 copy-start.2
  193.6 1.1 copy-done.2
  194.7 0.0 copy-start.4
  194.7 0.0 copy-start.3
  194.7 4.5 %lay.1 = (f32[128,4608]{1,0:T(8,128)}, f32[128,4608]{1,0:T(8,128)}, f32[576,1024]{1,0:T(8,128)}, f32[128,1024]{1,0:T(8,128)}, f32[128,512]{1,0:T(8,128)}, /*index=5*/f32[128,512]{1,0:T(8,128)}, f32[128,1024]{1,0:T(8,128)}) custom-call(bf16[16,32,2304]{2,1,0:T(8,128)(2,1)S(1)} %copy-done, bf16[16,3,16,1024]{3,2,1,0:T(8,128)(2,1)S(1)} %copy-done.1, ...), custom_call_target="tpu_custom_call" | custom-call | tf_op jit(solution)/shard_map/lay/pallas_call | solution.py:1100
  199.3 0.0 copy-done.4
  199.3 0.7 copy.30
  200.0 0.0 copy-done.3
  200.0 0.7 copy.31
Async XLA Ops:
  190.5 1.7 copy-start
  192.2 1.4 copy-start.1
  193.6 1.1 copy-start.2
  194.7 4.5 %copy-start.4 = (bf16[128,1024]{1,0:T(8,128)(2,1)S(1)}, bf16[128,1024]{1,0:T(8,128)(2,1)}, u32[]{:S(2)}) copy-start(bf16[128,1024]{1,0:T(8,128)(2,1)} %get-tuple-element.56) | copy-start | bytes 786436
  194.7 5.2 %copy-start.3 = (bf16[128,1024]{1,0:T(8,128)(2,1)S(1)}, bf16[128,1024]{1,0:T(8,128)(2,1)}, u32[]{:S(2)}) copy-start(bf16[128,1024]{1,0:T(8,128)(2,1)} %get-tuple-element.57) | copy-start | bytes 786436

commit v3 on v2

--- a/solution.py
+++ b/solution.py
@@ -122,21 +122,20 @@
     "qk_raw": ((4, 128, 384), F32),
     "qz": ((4, 512, 128), BF),
     "kv": ((16, 128, 256), BF),
-    "kt": ((16, 128, 128), BF),
-    "vt": ((16, 128, 128), BF),
+    "kvt": ((128, 2048), BF),
+    "pT": ((1152, 512), BF),
+    "dsT": ((1152, 512), BF),
     "cosr": ((4, 128, 128), F32),
     "sinr": ((4, 128, 128), F32),
     "invl": ((4, 8, 512), F32),
     "oT": ((4, 256, 128), F32),
-    "acc": ((128, 512), F32),
-    "lacc": ((8, 512), F32),
     "o_s": ((4, 128, 256), BF),
     "o_in": ((4, 128, 256), BF),
     "o_own": ((128, 1024), BF),
     "o_full": ((4, 128, 1024), BF),
     "mid": ((128, 1024), F32),
     "h2": ((4, 128, 1024), BF),
-    "dm": ((4, 128, 1152), F32),
+    "dm": ((4, 128, 1152), BF),
     "mixed": ((4, 128, 1152), BF),
     "dg": ((4, 128, 1152), BF),
     "du": ((4, 128, 1152), BF),
@@ -195,7 +194,7 @@
     "gs1s": ((8, 128), F32),
     "gs2": ((16, 8, 128), F32),
 }
-NSEM = 400
+NSEM = 112
 
 
 class Refs:
@@ -222,6 +221,12 @@
     def send(self, src, dst, i, dev):
         self.copy(src, dst, i, dev).start()
         self.sent.append((src, i))
+
+    def part(self, src, dst, i, dev):
+        self.copy(src, dst, i, dev).start()
+
+    def whole(self, ref, i):
+        self.sent.append((ref, i))
 
     def local(self, src, dst, i):
         return pltpu.make_async_copy(src, dst, self.rsem.at[i])
@@ -313,7 +318,7 @@
     class Shards:
         def __init__(self, buf, i_share):
             self.buf, self.share = buf, i_share
-            self.iy, self.ix = m.take(4), m.take(8)
+            self.iy, self.ix = m.take(3) - 1, m.take(1)
 
         def row(self, k, xl):
             return rem(p.y - k + 4, 4) * 2 + xl
@@ -332,13 +337,11 @@
                 m.got(self.buf.at[d, half], self.iy + k)
             for t in (1, 2):
                 s = self.buf.at[d, self.quarter(t)]
-                m.send(s, s, self.ix + 2 * k + t - 1, p.xring(t))
+                m.part(s, s, self.ix, p.xring(t))
 
         def to_core(self):
-            for k in range(4):
-                d = self.row(k, 1 - p.xl)
-                for t in (1, 2):
-                    m.got(self.buf.at[d, self.quarter(t)], self.ix + 2 * k + t - 1)
+            m.whole(self.buf.at[0:4, half], self.ix)
+            m.got(self.buf.at[0:4, half], self.ix)
             s = self.buf.at[:, half]
             m.send(s, s, self.share, p.sib())
 
@@ -348,37 +351,46 @@
     class Down:
         def __init__(self, i_share):
             self.share = i_share
-            self.iy, self.ix = m.take(12), m.take(24)
-
-        def move(self, d, t, i, dev, act):
+            self.iy, self.ix = m.take(3) - 1, m.take(1)
+
+        def start(self, d, t, i, dev):
             where, more = down_pieces(d)
             for n in range(3):
                 rows = h32 if t == 0 else pl.ds(pl.multiple_of(c32 + (t - 1) * 16, 16), 16)
                 s = r.wd_v.at[where[n][1], rows]
                 if n < 2:
-                    act(m.copy(s, s, i + n, dev))
+                    m.part(s, s, i, dev)
                 else:
 
                     @pl.when(more)
                     def _():
-                        act(m.copy(s, s, i + n, dev))
+                        m.part(s, s, i, dev)
+
+        def wait(self, d, act):
+            _, more = down_pieces(d)
+
+            @pl.when(more)
+            def _():
+                act(r.wd_v.at[0:3, h32])
+
+            @pl.when(jnp.logical_not(more))
+            def _():
+                act(r.wd_v.at[0:2, h32])
 
         def along_y(self):
             for k in (2, 1, 3):
-                self.move(p.dp, 0, self.iy + 3 * k, p.ypeer(k), lambda q: q.start())
+                self.start(p.dp, 0, self.iy + k, p.ypeer(k))
 
         def along_x(self, k):
             d = rem(p.y - k + 4, 4) * 2 + p.xl
             if k:
-                self.move(d, 0, self.iy + 3 * k, p.sib(), lambda q: q.wait_recv())
+                self.wait(d, lambda ref: m.got(ref, self.iy + k))
             for t in (1, 2):
-                self.move(d, t, self.ix + 6 * k + 3 * (t - 1), p.xring(t), lambda q: q.start())
+                self.start(d, t, self.ix, p.xring(t))
 
         def to_core(self):
-            for k in range(4):
-                d = rem(p.y - k + 4, 4) * 2 + 1 - p.xl
-                for t in (1, 2):
-                    self.move(d, t, self.ix + 6 * k + 3 * (t - 1), p.sib(), lambda q: q.wait_recv())
+            m.whole(r.wd_v.at[0:9, h32], self.ix)
+            m.got(r.wd_v.at[0:9, h32], self.ix)
             m.send(r.wd_v.at[:, h32], r.wd_v.at[:, h32], self.share, p.sib())
 
         def done(self):
@@ -386,11 +398,7 @@
 
         def finish(self):
             for k in (1, 2, 3):
-                self.move(p.dp, 0, self.iy + 3 * k, p.sib(), lambda q: q.wait_send())
-            for k in range(4):
-                d = rem(p.y - k + 4, 4) * 2 + p.xl
-                for t in (1, 2):
-                    self.move(d, t, self.ix + 6 * k + 3 * (t - 1), p.sib(), lambda q: q.wait_send())
+                self.wait(p.dp, lambda ref: m.copy(ref, ref, self.iy + k, p.sib()).wait_send())
 
     i_share = m.take(5)
     w_qkv = Shards(r.wqkv, i_share)
@@ -398,20 +406,24 @@
     w_d = Down(i_share + 2)
     w_g = Shards(r.wg_v, i_share + 3)
     w_u = Shards(r.wu_v, i_share + 4)
-    i_tok = m.take(4)
+    i_tok = m.take(3) - 1
     for dz in (2, 1, 3):
         m.send(r.tok, r.tok_all.at[dz], i_tok + dz, p.zpeer(dz))
     m.local(r.wqkv.at[0, half], r.wqkv.at[0, half], i_loc).wait()
     w_qkv.along_y()
     w_qkv.along_x(0)
-    i_mseq = m.take(16)
+    i_mseq = m.take()
     for k in range(1, 16):
-        m.send(r.meta, r.mseq.at[p.sq], i_mseq + k, p.speer(k))
-    i_mdp = m.take(8)
+        m.part(r.meta, r.mseq.at[p.sq], i_mseq, p.speer(k))
+    m.whole(r.mseq.at[0:15], i_mseq)
+    i_mdp = m.take()
     for k in range(1, 8):
-        m.send(r.meta, r.mdp.at[p.dp], i_mdp + k, p.dpeer(k))
+        m.part(r.meta, r.mdp.at[p.dp], i_mdp, p.dpeer(k))
+    m.whole(r.mdp.at[0:7], i_mdp)
     r.mseq[p.sq] = r.meta[...]
     r.mdp[p.dp] = r.meta[...]
+    for k in (1, 3, 2):
+        w_qkv.along_x(k)
     m.local(r.wo_v.at[0, half], r.wo_v.at[0, half], i_loc + 1).wait()
     w_o.along_y()
     for n in range(2):
@@ -422,14 +434,18 @@
         down_local(2).wait()
 
     w_d.along_y()
+
+    m.got(r.mseq.at[0:15], i_mseq)
+    r.st[...] = seg_rows(r.mseq[:, 2, :])
+    m.got(r.mdp.at[0:7], i_mdp)
+    gain1 = jnp.concatenate([r.mdp[j, 0:1, :] for j in range(8)], axis=1)
+    gain2 = jnp.concatenate([r.mdp[j, 1:2, :] for j in range(8)], axis=1)
+    w_qkv.to_core()
     m.local(r.wg_v.at[0, half], r.wg_v.at[0, half], i_loc + 2).wait()
     w_g.along_y()
     m.local(r.wu_v.at[0, half], r.wu_v.at[0, half], i_loc + 3).wait()
     w_u.along_y()
 
-    for k in range(1, 16):
-        m.got(r.mseq.at[rem(p.sq + 16 - k, 16)], i_mseq + k)
-    r.st[...] = seg_rows(r.mseq[:, 2, :])
     lanesign = jnp.where(lane_half(), -1.0, 1.0)
     freq = r.freq[...]
     for dz in range(4):
@@ -439,22 +455,14 @@
         ang = jnp.transpose(jnp.broadcast_to(pos, (128, 128))) * freq
         r.cosr[dz] = jnp.cos(ang)
         r.sinr[dz] = jnp.sin(ang) * lanesign
-    for k in range(1, 8):
-        m.got(r.mdp.at[dps[k]], i_mdp + k)
-    gain1 = jnp.concatenate([r.mdp[j, 0:1, :] for j in range(8)], axis=1)
-    gain2 = jnp.concatenate([r.mdp[j, 1:2, :] for j in range(8)], axis=1)
-
-    for k in (1, 3, 2):
-        w_qkv.along_x(k)
-    w_qkv.to_core()
     w_qkv.done()
 
     wfull = r.wqkv[...].reshape(1024, 512)
     qg = r.gqk[0:1, :].astype(F32)
     kg = r.gqk[1:2, :].astype(F32)
-    i_kv = m.take(4)
+    i_kv = m.take()
     i_kvx = m.take(4)
-    i_kvf = m.take(4)
+    i_kvf = m.take()
 
     def project(dz, x):
         x = x.astype(F32)
@@ -475,88 +483,96 @@
         r.kv[i, :, 0:128] = rot[2].astype(BF)
         r.kv[i, :, 128:256] = o[:, 384:512].astype(BF)
         m.send(r.kv.at[i], r.kv.at[i], i_kvx + dz, p.xpeer())
-        m.send(r.kv.at[i], r.kv.at[i], i_kv + dz, p.sib())
+        m.part(r.kv.at[i], r.kv.at[i], i_kv, p.sib())
 
     project(0, r.tok[...])
     for dz in (1, 3, 2):
         m.got(r.tok_all.at[dz], i_tok + dz)
         project(dz, r.tok_all[dz])
-    i_cot = m.take(4)
+    i_cot = m.take()
     for dz in (1, 3, 2):
-        m.send(r.cot, r.cot_all.at[dz], i_cot + dz, p.zpeer(dz))
+        m.part(r.cot, r.cot_all.at[dz], i_cot, p.zpeer(dz))
+    m.whole(r.cot_all.at[1:4], i_cot)
     r.cot_all[0] = r.cot[...]
+    for w in (w_o, w_d):
+        for k in (0, 1, 3, 2):
+            w.along_x(k)
     gs = p.g + 1 - 2 * p.c
     gx = (1 - p.xh) * 2 + p.c
     gxs = (1 - p.xh) * 2 + 1 - p.c
     for dz in (0, 1, 3, 2):
         zz = 4 * z_of(dz)
         m.got(r.kv.at[zz + gx], i_kvx + dz)
-        m.send(r.kv.at[zz + gx], r.kv.at[zz + gx], i_kvf + dz, p.sib())
-    for dz in (0, 1, 3, 2):
-        zz = 4 * z_of(dz)
-        m.got(r.kv.at[zz + gs], i_kv + dz)
-        m.got(r.kv.at[zz + gxs], i_kvf + dz)
-
-    def turn(j, carry):
-        r.kt[j] = jnp.transpose(r.kv[j, :, 0:128].astype(F32)).astype(BF)
-        r.vt[j] = jnp.transpose(r.kv[j, :, 128:256].astype(F32)).astype(BF)
-        return carry
-
-    lax.fori_loop(0, 16, turn, 0)
-    for k in (0, 1, 3, 2):
-        w_o.along_x(k)
+        m.part(r.kv.at[zz + gx], r.kv.at[zz + gx], i_kvf, p.sib())
+    four = r.kv.at[0:4]
+    for i in (i_kv, i_kvf):
+        m.whole(four, i)
+        m.got(four, i)
+
+    def turn(first):
+        def one(j, carry):
+            t = jnp.transpose(r.kv[j, :, first:first + 128].astype(F32))
+            r.kvt[:, pl.ds(pl.multiple_of(j * 128, 128), 128)] = t.astype(BF)
+            return carry
+
+        lax.fori_loop(0, 16, one, 0)
+
+    turn(128)
 
     def allowed_rows(i):
         row = r.st[pl.ds(i, 1), :].astype(jnp.int32)
         qi = lax.broadcasted_iota(jnp.int32, (1, 128), 1) + i * 128
         return jnp.concatenate([row] * 4, axis=1), jnp.concatenate([qi] * 4, axis=1)
 
+    def window(i):
+        return jnp.minimum(jnp.maximum(i - 8, 0), 7)
+
     def weights_of(kb, qv, row4, qi4):
-        s = dot(r.kv[kb, :, 0:128], qv, NT)
-        ki = lax.broadcasted_iota(jnp.int32, (128, 512), 0) + kb * 128
+        s = dot(r.kv[pl.ds(kb, 3), :, 0:128].reshape(384, 128), qv, NT)
+        ki = lax.broadcasted_iota(jnp.int32, (384, 512), 0) + kb * 128
         return jnp.where((ki >= row4) & (ki <= qi4), jnp.exp2(s * (SCALE * LOG2E)), 0.0)
 
-    def forward_chunk(j, carry):
-        dz = rem(j + 1, 4)
-        i = 4 * z_of(dz) + p.g
-        row4, qi4 = allowed_rows(i)
-        r.acc[...] = jnp.zeros_like(r.acc)
-        r.lacc[...] = jnp.zeros_like(r.lacc)
-        qv = r.qz[dz]
-
-        def body(kb, inner):
-            w = weights_of(kb, qv, row4, qi4)
-            r.lacc[...] += jnp.sum(w.reshape(16, 8, 512), axis=0)
-            r.acc[...] += dot(r.vt[kb], w.astype(BF))
-            return inner
-
-        lax.fori_loop(jnp.maximum(i - 8, 0), i + 1, body, 0)
-        il = 1.0 / jnp.sum(r.lacc[...], axis=0, keepdims=True)
-        r.invl[dz] = jnp.broadcast_to(il, (8, 512))
-        o = r.acc[...] * il
-        full = jnp.concatenate(
+    def keys_turned(k0):
+        return r.kvt[:, pl.ds(pl.multiple_of(k0 * 128, 128), 1152)]
+
+    def heads_down(o):
+        return jnp.concatenate(
             [o[(h // 2) * 64:(h // 2) * 64 + 64, h * 128:(h + 1) * 128] for h in range(4)], axis=0
         )
+
+    def forward_chunk(dz):
+        i = 4 * z_of(dz) + p.g
+        k0 = window(i)
+        row4, qi4 = allowed_rows(i)
+        qv = r.qz[dz]
+        total = jnp.zeros((8, 512), F32)
+        for t in range(3):
+            w = weights_of(k0 + 3 * t, qv, row4, qi4)
+            total = total + jnp.sum(w.reshape(48, 8, 512), axis=0)
+            r.pT[t * 384:(t + 1) * 384] = w.astype(BF)
+        il = 1.0 / jnp.sum(total, axis=0, keepdims=True)
+        r.invl[dz] = jnp.broadcast_to(il, (8, 512))
+        full = heads_down(dot(keys_turned(k0), r.pT[...]) * il)
         r.oT[dz] = full
         r.o_s[dz] = jnp.transpose(full).astype(BF)
-        return carry
-
-    i_o = m.take(4)
+
+    i_o = m.take()
     for j in range(4):
-        forward_chunk(j, 0)
         dz = (j + 1) % 4
+        forward_chunk(dz)
         if dz:
-            m.send(r.o_s.at[dz], r.o_in.at[p.z], i_o + dz, p.zpeer(-dz))
+            m.part(r.o_s.at[dz], r.o_in.at[p.z], i_o, p.zpeer(-dz))
         else:
             r.o_in[p.z] = r.o_s[0]
-        if j < 3:
+        if j in (0, 2):
             for k in (0, 1, 3, 2):
-                (w_d, w_g, w_u)[j].along_x(k)
+                (w_g, None, w_u)[j].along_x(k)
         if j == 1:
             w_o.to_core()
-
-    for dz in range(1, 4):
-        m.got(r.o_in.at[rem(p.z + dz, 4)], i_o + dz)
+    m.whole(r.o_in.at[0:3], i_o)
+
+    w_d.to_core()
+    m.got(r.o_in.at[0:3], i_o)
     for j in range(4):
         r.o_own[:, j * 256:(j + 1) * 256] = r.o_in[j]
     w_o.done()
@@ -565,15 +581,19 @@
     r.mid[...] = middle
     r2 = lax.rsqrt(jnp.mean(middle * middle, axis=1, keepdims=True) + EPS)
     r.h2[0] = (middle * r2 * gain2).astype(BF)
-    i_h2 = m.take(4)
+    i_h2 = m.take(3) - 1
     for dz in (2, 1, 3):
         m.send(r.h2.at[0], r.h2.at[dz], i_h2 + dz, p.zpeer(dz))
-
-    w_d.to_core()
+    i_of = m.take()
+    for dz in (2, 1, 3):
+        m.part(r.o_own, r.o_full.at[dz], i_of, p.zpeer(dz))
+    m.whole(r.o_full.at[1:4], i_of)
+    r.o_full[0] = r.o_own[...]
+
+    turn(0)
     w_g.to_core()
     w_u.to_core()
-    for dz in range(1, 4):
-        m.got(r.cot_all.at[dz], i_cot + dz)
+    m.got(r.cot_all.at[1:4], i_cot)
     w_d.done()
     wd = r.wd_v[...].reshape(1152, 1024)
     cots = r.cot_all[...].reshape(512, 1024)
@@ -583,14 +603,14 @@
 
     def dm_tile(t, carry):
         w = r.wd_v[pl.ds(t * 6, 6)].reshape(384, 1024)
-        r.dm[:, :, cols384(t)] = dot(cots, w, NT).reshape(4, 128, 384)
+        r.dm[:, :, cols384(t)] = dot(cots, w, NT).astype(BF).reshape(4, 128, 384)
         return carry
 
     lax.fori_loop(0, 3, dm_tile, 0)
     w_g.done()
     w_u.done()
 
-    i_p2 = m.take(4)
+    i_p2 = m.take()
     for pair in range(2):
         two = slice(2 * pair, 2 * pair + 2)
         for dz in ((1,), (2, 3))[pair]:
@@ -603,7 +623,7 @@
             up = dot(hh, r.wu_v[:, :, cols].reshape(1024, 384))
             sig = 1.0 / (1.0 + jnp.exp(-gate))
             act = gate * sig
-            dmt = r.dm[two, :, cols].reshape(256, 384)
+            dmt = r.dm[two, :, cols].astype(F32).reshape(256, 384)
             r.mixed[two, :, cols] = (act * up).astype(BF).reshape(2, 128, 384)
             r.dg[two, :, cols] = (dmt * up * sig * (1.0 + gate * (1.0 - sig))).astype(BF).reshape(2, 128, 384)
             r.du[two, :, cols] = (dmt * act).astype(BF).reshape(2, 128, 384)
@@ -615,12 +635,12 @@
         if pair == 0:
             r.own[...] = part[0:128]
             r.p2s[0] = part[128:256].astype(BF)
-            m.send(r.p2s.at[0], r.p2r.at[0], i_p2 + 1, p.zpeer(-1))
+            m.part(r.p2s.at[0], r.p2r.at[0], i_p2, p.zpeer(-1))
         else:
             r.p2s[1] = part[0:128].astype(BF)
-            m.send(r.p2s.at[1], r.p2r.at[1], i_p2 + 2, p.zpeer(-2))
+            m.part(r.p2s.at[1], r.p2r.at[1], i_p2, p.zpeer(-2))
             r.p2s[2] = part[128:256].astype(BF)
-            m.send(r.p2s.at[2], r.p2r.at[2], i_p2 + 3, p.zpeer(-3))
+            m.part(r.p2s.at[2], r.p2r.at[2], i_p2, p.zpeer(-3))
 
     i_r1 = m.take(3)
     h2t = r.h2[...].reshape(512, 1024)
@@ -649,8 +669,8 @@
 
     lax.fori_loop(1, 4, out_chunk, 0)
 
-    for dz in range(1, 4):
-        m.got(r.p2r.at[dz - 1], i_p2 + dz)
+    m.whole(r.p2s, i_p2)
+    m.got(r.p2r, i_p2)
     dh2 = r.own[...] + r.p2r[0].astype(F32) + r.p2r[1].astype(F32) + r.p2r[2].astype(F32)
     middle = r.mid[...]
     r2 = lax.rsqrt(jnp.mean(middle * middle, axis=1, keepdims=True) + EPS)
@@ -660,23 +680,23 @@
     r.dmid[...] = dmid
     r.da[...] = dmid.astype(BF)
     r.dob[...] = dot(r.da[...], r.wo_v[...].reshape(1024, 1024), NT).astype(BF)
-    i_do = m.take(4)
+    i_do = m.take()
 
     def zcols(z):
         return pl.ds(pl.multiple_of(z * 256, 256), 256)
 
     for dz in (2, 1, 3):
-        m.send(r.dob.at[:, zcols(rem(p.z + dz, 4))], r.do_all.at[dz], i_do + dz, p.zpeer(dz))
+        m.part(r.dob.at[:, zcols(rem(p.z + dz, 4))], r.do_all.at[dz], i_do, p.zpeer(dz))
+    m.whole(r.do_all.at[1:4], i_do)
     r.do_all[0] = r.dob[:, zq]
-    i_p3 = m.take(4)
-    i_of = m.take(4)
-    i_dc = m.take(4)
+    i_p3 = m.take()
+    i_dc = m.take()
     for dz in (2, 1, 3):
-        m.send(r.o_own, r.o_full.at[dz], i_of + dz, p.zpeer(dz))
-        m.send(r.da.at[:, zcols(rem(p.z + dz, 4))], r.da_c.at[dz], i_dc + dz, p.zpeer(dz))
+        m.part(r.da.at[:, zcols(rem(p.z + dz, 4))], r.da_c.at[dz], i_dc, p.zpeer(dz))
+    m.whole(r.da_c.at[1:4], i_dc)
     for dz in (2, 1, 3):
-        m.send(r.p3s.at[dz - 1], r.p3r.at[dz - 1], i_p3 + dz, p.zpeer(-dz))
-    r.o_full[0] = r.o_own[...]
+        m.part(r.p3s.at[dz - 1], r.p3r.at[dz - 1], i_p3, p.zpeer(-dz))
+    m.whole(r.p3s, i_p3)
     r.da_c[0] = r.da[:, zq]
 
     m.got(r.r1F, i_r1)
@@ -705,15 +725,15 @@
     class XFirst:
         def __init__(self, src, mid1, tot, mid2):
             self.src, self.mid1, self.tot, self.mid2 = src, mid1, tot, mid2
-            self.i1, self.i2 = m.take(4), m.take(4)
+            self.i1, self.i2 = m.take(), m.take()
 
         def one(self):
             for t in (3, 1, 2):
-                m.send(self.src(t), self.mid1.at[t - 1], self.i1 + t, p.xring(t))
+                m.part(self.src(t), self.mid1.at[t - 1], self.i1, p.xring(t))
+            m.whole(self.mid1, self.i1)
 
         def two(self):
-            for t in (1, 2, 3):
-                m.got(self.mid1.at[t - 1], self.i1 + t)
+            m.got(self.mid1, self.i1)
 
             def add(n, carry):
                 v = self.src(0).at[n][...].astype(F32)
@@ -724,11 +744,11 @@
 
             lax.fori_loop(0, 4, add, 0)
             for k in (2, 1, 3):
-                m.send(self.tot.at[rem(p.y + k, 4)], self.mid2.at[k - 1], self.i2 + k, p.ypeer(k))
+                m.part(self.tot.at[rem(p.y + k, 4)], self.mid2.at[k - 1], self.i2, p.ypeer(k))
+            m.whole(self.mid2, self.i2)
 
         def sum(self):
-            for k in (1, 2, 3):
-                m.got(self.mid2.at[k - 1], self.i2 + k)
+            m.got(self.mid2, self.i2)
             v = self.tot[p.y].astype(F32)
             for k in range(3):
                 v = v + self.mid2[k].astype(F32)
@@ -737,15 +757,15 @@
     class YFirst:
         def __init__(self, src, part, mid1, tot, mid2):
             self.src, self.part, self.mid1, self.tot, self.mid2 = src, part, mid1, tot, mid2
-            self.i1, self.i2 = m.take(4), m.take(4)
+            self.i1, self.i2 = m.take(), m.take()
 
         def one(self):
             for k in (2, 1, 3):
-                m.send(self.src(rem(p.y + k, 4)), self.mid1.at[k - 1], self.i1 + k, p.ypeer(k))
+                m.part(self.src(rem(p.y + k, 4)), self.mid1.at[k - 1], self.i1, p.ypeer(k))
+            m.whole(self.mid1, self.i1)
 
         def two(self):
-            for k in (1, 2, 3):
-                m.got(self.mid1.at[k - 1], self.i1 + k)
+            m.got(self.mid1, self.i1)
 
             def add(n, carry):
                 v = self.src(p.y).at[n][...].astype(F32)
@@ -756,11 +776,11 @@
 
             lax.fori_loop(0, 2, add, 0)
             for t in (3, 1, 2):
-                m.send(self.part(self.tot, t), self.mid2.at[t - 1], self.i2 + t, p.xring(t))
+                m.part(self.part(self.tot, t), self.mid2.at[t - 1], self.i2, p.xring(t))
+            m.whole(self.mid2, self.i2)
 
         def sum(self):
-            for t in (1, 2, 3):
-                m.got(self.mid2.at[t - 1], self.i2 + t)
+            m.got(self.mid2, self.i2)
             v = self.part(self.tot, 0)[...].astype(F32)
             for t in range(3):
                 v = v + self.mid2[t].astype(F32)
@@ -790,16 +810,15 @@
     ]
     for e in sums:
         e.one()
-    i_x1 = m.take(4)
-    i_x2 = m.take(4)
+    i_x1 = m.take()
+    i_x2 = m.take()
     for t in (3, 1, 2):
         xl, xh = p.xplace(t)
-        m.send(r.sX.at[xl, rows_of(xh, 16)], r.xx.at[t - 1], i_x1 + t, p.xring(t))
+        m.part(r.sX.at[xl, rows_of(xh, 16)], r.xx.at[t - 1], i_x1, p.xring(t))
+    m.whole(r.xx, i_x1)
 
     r.dkv[...] = jnp.zeros_like(r.dkv)
-    for dz in (0, 1, 3, 2):
-        if dz:
-            m.got(r.do_all.at[dz], i_do + dz)
+    m.got(r.do_all.at[1:4], i_do)
 
     def backward_chunk(j, carry):
         dz = j
@@ -815,23 +834,17 @@
         il = r.invl[dz, 0:1, :]
         qv = r.qz[dz]
         dov = r.doz[...]
-        r.acc[...] = jnp.zeros_like(r.acc)
-
-        def body(kb, inner):
-            w = weights_of(kb, qv, row4, qi4) * il
-            dp = dot(r.kv[kb, :, 128:256], dov, NT)
-            ds = (w * (dp - drow)).astype(BF)
-            r.acc[...] += dot(r.kt[kb], ds)
-            r.dkv[kb, :, 0:128] += dot(ds, qv)
-            r.dkv[kb, :, 128:256] += dot(w.astype(BF), dov)
-            return inner
-
-        lax.fori_loop(jnp.maximum(i - 8, 0), i + 1, body, 0)
-        o = r.acc[...] * SCALE
-        full = jnp.concatenate(
-            [o[(h // 2) * 64:(h // 2) * 64 + 64, h * 128:(h + 1) * 128] for h in range(4)], axis=0
-        )
-        r.dqr[dz] = jnp.transpose(full)
+        k0 = window(i)
+        for t in range(3):
+            rows = slice(t * 384, (t + 1) * 384)
+            w = weights_of(k0 + 3 * t, qv, row4, qi4) * il
+            r.pT[rows] = w.astype(BF)
+            dp = dot(r.kv[pl.ds(k0 + 3 * t, 3), :, 128:256].reshape(384, 128), dov, NT)
+            r.dsT[rows] = (w * (dp - drow)).astype(BF)
+        nine = pl.ds(k0, 9)
+        r.dkv[nine, :, 0:128] += dot(r.dsT[...], qv).reshape(9, 128, 128)
+        r.dkv[nine, :, 128:256] += dot(r.pT[...], dov).reshape(9, 128, 128)
+        r.dqr[dz] = jnp.transpose(heads_down(dot(keys_turned(k0), r.dsT[...]) * SCALE))
         return carry
 
     lax.fori_loop(0, 4, backward_chunk, 0)
@@ -839,16 +852,16 @@
     lane = lax.broadcasted_iota(jnp.int32, (1, 256), 1)
     kscale = jnp.where(lane < 128, SCALE, 1.0)
     r.dkvb[...] = (r.dkv[...] * kscale.reshape(1, 1, 256)).astype(BF).reshape(4, 4, 128, 256)
-    i_dkv = m.take(3)
+    i_dkv = m.take()
     xs = (p.dp, p.z * 4 + gxs)
-    m.send(r.dkvb.at[:, gx], r.dkvr.at[1], i_dkv + 1, p.xpeer())
-    m.send(r.dkvb.at[:, gxs], r.dkvr.at[2], i_dkv + 2, xs)
-    m.send(r.dkvb.at[:, gs], r.dkvr.at[0], i_dkv, p.sib())
+    m.part(r.dkvb.at[:, gx], r.dkvr.at[1], i_dkv, p.xpeer())
+    m.part(r.dkvb.at[:, gxs], r.dkvr.at[2], i_dkv, xs)
+    m.part(r.dkvb.at[:, gs], r.dkvr.at[0], i_dkv, p.sib())
+    m.whole(r.dkvr, i_dkv)
 
     for e in sums:
         e.two()
-    for t in (1, 2, 3):
-        m.got(r.xx.at[t - 1], i_x1 + t)
+    m.got(r.xx, i_x1)
     v = r.sX[p.xl, rows_of(p.xh, 16)].astype(F32)
     for t in range(3):
         v = v + r.xx[t].astype(F32)
@@ -857,12 +870,11 @@
 
     @pl.when(kz != 0)
     def _():
-        m.copy(r.xt, r.xy.at[kz - 1], i_x2 + kz, (p.z * 2 + p.xl, p.sq)).start()
-
-    for dz in range(1, 4):
-        m.got(r.o_full.at[dz], i_of + dz)
-        m.got(r.da_c.at[dz], i_dc + dz)
-        m.got(r.p3r.at[dz - 1], i_p3 + dz)
+        m.part(r.xt, r.xy.at[kz - 1], i_x2, (p.z * 2 + p.xl, p.sq))
+
+    m.got(r.o_full.at[1:4], i_of)
+    m.got(r.da_c.at[1:4], i_dc)
+    m.got(r.p3r, i_p3)
     r.gA[:, :, :, 512:768] = dot(
         r.o_full[...].reshape(512, 1024), r.da_c[...].reshape(512, 256), TN
     ).astype(BF).reshape(4, 2, 128, 256)
@@ -878,9 +890,9 @@
     @pl.when(kz == 0)
     def _():
         v = r.xt[...].astype(F32)
-        for k in (1, 2, 3):
-            m.got(r.xy.at[k - 1], i_x2 + k)
-            v = v + r.xy[k - 1].astype(F32)
+        m.got(r.xy, i_x2)
+        for k in range(3):
+            v = v + r.xy[k].astype(F32)
         r.oD[2] = v.astype(BF)
 
     @pl.when(kz != 0)
@@ -891,48 +903,78 @@
         return rem(z + 8, 4) * 4 + g
 
     class Gather:
-        def __init__(self, own, buf):
-            self.own, self.buf = own, buf
-            self.il = m.take(1)
-            self.ix, self.iz, self.izx, self.ic = m.take(1), m.take(4), m.take(4), m.take(8)
+        def __init__(self, own, buf, order):
+            self.own, self.buf, self.order = own, buf, order
+            self.il, self.ix, self.iz, self.ic = m.take(), m.take(), m.take(), m.take()
+
+        def on(self, src, s, where):
+            if "x" in where:
+                m.part(src, s, self.ix, p.xpeer())
+            if "z" in where:
+                for dz in (2, 1, 3):
+                    m.part(src, s, self.iz, p.zpeer(dz))
+            if "b" in where:
+                for dz in (2, 1, 3):
+                    m.part(src, s, self.iz, (p.dp, seq_at(p.z + dz, gx)))
+            if "c" in where:
+                m.part(src, s, self.ic, p.sib())
+
+        def got(self, n, i):
+            m.got(self.buf.at[0:n], i)
+
+        def slot(self, dz, g):
+            return self.buf.at[seq_at(p.z - dz, g)]
 
         def first(self):
-            s = self.buf.at[p.sq]
-            m.send(self.own, s, self.ix, p.xpeer())
-            for dz in (2, 1, 3):
-                m.send(self.own, s, self.iz + dz, p.zpeer(dz))
-            m.send(self.own, s, self.ic, p.sib())
-            m.local(self.own, s, self.il).start()
+            m.local(self.own, self.slot(0, p.g), self.il).start()
+            self.on(self.own, self.slot(0, p.g), "zxcb" if self.order == "zx" else "zxc")
 
         def second(self):
-            s = self.buf.at[seq_at(p.z, gx)]
-            m.got(s, self.ix)
-            for dz in (2, 1, 3):
-                m.send(s, s, self.izx + dz, p.zpeer(dz))
-            m.send(s, s, self.ic + 4, p.sib())
+            if self.order == "x":
+                self.got(1, self.ix)
+                s = self.slot(0, gx)
+                self.on(s, s, "zc")
+            elif self.order == "z":
+                self.got(3, self.iz)
+                for dz in (1, 2, 3):
+                    s = self.slot(dz, p.g)
+                    self.on(s, s, "xc")
+            else:
+                self.got(1, self.ix)
+                self.got(6, self.iz)
+                for dz in range(4):
+                    for g in (p.g, gx)[dz == 0:]:
+                        s = self.slot(dz, g)
+                        self.on(s, s, "c")
 
         def third(self):
-            for dz in (1, 3, 2):
-                s = self.buf.at[seq_at(p.z - dz, p.g)]
-                m.got(s, self.iz + dz)
-                m.send(s, s, self.ic + dz, p.sib())
-            for dz in (1, 3, 2):
-                s = self.buf.at[seq_at(p.z - dz, gx)]
-                m.got(s, self.izx + dz)
-                m.send(s, s, self.ic + 4 + dz, p.sib())
+            if self.order == "x":
+                self.got(6, self.iz)
+                for dz in (1, 2, 3):
+                    for g in (p.g, gx):
+                        s = self.slot(dz, g)
+                        self.on(s, s, "c")
+            elif self.order == "z":
+                self.got(4, self.ix)
+                for dz in range(4):
+                    s = self.slot(dz, gx)
+                    self.on(s, s, "c")
 
         def last(self):
-            for dz in (0, 1, 3, 2):
-                m.got(self.buf.at[seq_at(p.z - dz, gs)], self.ic + dz)
-                m.got(self.buf.at[seq_at(p.z - dz, gxs)], self.ic + 4 + dz)
-            m.local(self.own, self.buf.at[p.sq], self.il).wait()
-
-    ag_f = Gather(r.oF, r.fF)
-    ag_d = Gather(r.oD, r.fD)
-    ag_a = Gather(r.oA, r.fA)
-
-    for n in range(3):
-        m.got(r.dkvr.at[n], i_dkv + n)
+            n = {"x": (1, 6), "z": (4, 3), "zx": (1, 6)}[self.order]
+            m.whole(self.buf.at[0:n[0]], self.ix)
+            m.whole(self.buf.at[0:n[1]], self.iz)
+            m.whole(self.buf.at[0:8], self.ic)
+            self.got(8, self.ic)
+            m.local(self.own, self.slot(0, p.g), self.il).wait()
+
+    ag_f = Gather(r.oF, r.fF, "z")
+    ag_d = Gather(r.oD, r.fD, "x")
+    ag_a = Gather(r.oA, r.fA, "zx")
+    ag_f.first()
+    ag_d.first()
+
+    m.got(r.dkvr, i_dkv)
     sq_acc = jnp.zeros((1, 128), F32)
     sk_acc = jnp.zeros((1, 128), F32)
     for dz in range(4):
@@ -956,19 +998,17 @@
             wn = dn * gn
             r.dqkv[dz, :, b * 128:(b + 1) * 128] = (f * wn - v * (f * f * f) * head_mean(wn * v)).astype(BF)
         r.dqkv[dz, :, 384:512] = dkv[:, 128:256].astype(BF)
-    i_p4 = m.take(4)
-    for dz in range(1, 4):
-        m.flush(i_p2 + dz)
-    for dz in (2, 1, 3):
-        r.p2s[dz - 1] = dot(r.dqkv[dz], r.wqkv[...].reshape(1024, 512), NT).astype(BF)
-        m.send(r.p2s.at[dz - 1], r.p4r.at[dz - 1], i_p4 + dz, p.zpeer(-dz))
-    r.own[...] = dot(r.dqkv[0], r.wqkv[...].reshape(1024, 512), NT)
     r.gA[:, :, :, 0:512] = dot(
         r.tok_all[...].reshape(512, 1024), r.dqkv[...].reshape(512, 512), TN
     ).astype(BF).reshape(4, 2, 128, 512)
     m.send(r.gA.at[:, :, other], r.r1A, i_r1 + 2, p.sib())
-    ag_f.first()
-    ag_d.first()
+    i_p4 = m.take()
+    m.flush(i_p2)
+    for dz in (2, 1, 3):
+        r.p2s[dz - 1] = dot(r.dqkv[dz], r.wqkv[...].reshape(1024, 512), NT).astype(BF)
+        m.part(r.p2s.at[dz - 1], r.p4r.at[dz - 1], i_p4, p.zpeer(-dz))
+    m.whole(r.p2s, i_p4)
+    r.own[...] = dot(r.dqkv[0], r.wqkv[...].reshape(1024, 512), NT)
     m.got(r.r1A, i_r1 + 2)
     r.r1A[...] = (r.r1A[...].astype(F32) + r.gA[:, :, half].astype(F32)).astype(BF)
     sums_a = [
@@ -983,8 +1023,7 @@
     for e in sums_a:
         e.two()
 
-    for dz in range(1, 4):
-        m.got(r.p4r.at[dz - 1], i_p4 + dz)
+    m.got(r.p4r, i_p4)
     dh = r.own[...] + r.p4r[0].astype(F32) + r.p4r[1].astype(F32) + r.p4r[2].astype(F32)
     x0 = r.tok[...].astype(F32)
     r1 = lax.rsqrt(jnp.mean(x0 * x0, axis=1, keepdims=True) + EPS)
@@ -1000,16 +1039,17 @@
         r.gsm[d] = jnp.concatenate(
             [small1[:, cols], small2[:, cols], both(sq_acc), both(sk_acc), jnp.zeros((4, 128), F32)], axis=0
         )
-    i_s1 = m.take(8)
-    i_s2 = m.take(16)
+    i_s1 = m.take()
+    i_s2 = m.take()
     for k in range(1, 8):
-        m.send(r.gsm.at[rem(p.dp + k, 8)], r.gs1.at[k], i_s1 + k, p.dpeer(k))
+        m.part(r.gsm.at[rem(p.dp + k, 8)], r.gs1.at[k], i_s1, p.dpeer(k))
+    m.whole(r.gs1.at[1:8], i_s1)
     r.gs1[0] = r.gsm[p.dp]
-    for k in range(1, 8):
-        m.got(r.gs1.at[k], i_s1 + k)
+    m.got(r.gs1.at[1:8], i_s1)
     r.gs1s[...] = jnp.sum(r.gs1[...], axis=0)
     for k in range(1, 16):
-        m.send(r.gs1s, r.gs2.at[k], i_s2 + k, p.speer(k))
+        m.part(r.gs1s, r.gs2.at[k], i_s2, p.speer(k))
+    m.whole(r.gs2.at[1:16], i_s2)
     r.gs2[0] = r.gs1s[...]
 
     r.oA[:, 0:384] = sums_a[0].sum()
@@ -1018,9 +1058,7 @@
     ag_f.third()
     ag_d.third()
     ag_a.second()
-    ag_a.third()
-    for k in range(1, 16):
-        m.got(r.gs2.at[k], i_s2 + k)
+    m.got(r.gs2.at[1:16], i_s2)
     r.g_small[...] = jnp.sum(r.gs2[...], axis=0)
     ag_f.last()
     ag_d.last()
@@ -1031,7 +1069,7 @@
 
     @pl.when(kz != 0)
     def _():
-        m.copy(r.xt, r.xt, i_x2 + kz, p.sib()).wait_send()
+        m.copy(r.xt, r.xt, i_x2, p.sib()).wait_send()
 
     assert m.n <= NSEM, m.n
 
@@ -1053,7 +1091,7 @@
     )(*args)
 
 
-LAID = {
+PLACED = {
     "g_gate": (128, 4608),
     "g_up": (128, 4608),
     "g_down": (576, 1024),
@@ -1063,49 +1101,107 @@
     "g_out": (128, 1024),
 }
 
-
-def lay_kernel(f_f, f_d, f_a, g_gate, g_up, g_down, g_q, g_k, g_v, g_out):
+LAID = {
+    "g_attn": ((1, 128), F32),
+    "g_ffn": ((1, 128), F32),
+    "g_qg": ((1, 64), F32),
+    "g_kg": ((1, 64), F32),
+    **{name: (shape, F32) for name, shape in PLACED.items()},
+}
+
+
+def lay_kernel(f_f, f_d, f_a, sm, *refs):
+    outs = dict(zip(LAID, refs[:len(LAID)]))
+    v_f, v_d, v_a = refs[len(LAID):len(LAID) + 3]
+    stage = dict(zip(PLACED, refs[len(LAID) + 3:len(LAID) + 3 + len(PLACED)]))
+    isem, osem = refs[len(LAID) + 3 + len(PLACED):]
     p = Place()
-
-    def lay(s, carry):
+    ins = [
+        pltpu.make_async_copy(f_f, v_f, isem.at[0]),
+        pltpu.make_async_copy(f_d, v_d, isem.at[1]),
+        pltpu.make_async_copy(f_a, v_a, isem.at[2]),
+    ]
+    for q in ins:
+        q.start()
+    outs["g_attn"][...] = sm[0:1, :]
+    outs["g_ffn"][...] = sm[1:2, :]
+    outs["g_qg"][...] = sm[2:3, 0:64]
+    outs["g_kg"][...] = sm[3:4, 0:64]
+
+    def place(name):
+        n = list(PLACED).index(name)
+        return pltpu.make_async_copy(stage[name], outs[name], osem.at[n])
+
+    def row_of(s):
+        g = rem(s, 4)
+        return pl.ds(pl.multiple_of(rem(g, 2) * 64 + lax.div(g, 2) * 32, 32), 32)
+
+    ins[0].wait()
+    for name, base in (("g_gate", 0), ("g_up", 1152)):
+
+        def lay(s, carry):
+            z = lax.div(s, 4)
+            for t in range(9):
+                cols = pl.ds(pl.multiple_of(t * 512 + z * 128, 128), 128)
+                stage[name][row_of(s), cols] = v_f[s, :, base + t * 128:base + (t + 1) * 128].astype(F32)
+            return carry
+
+        lax.fori_loop(0, 16, lay, 0)
+        place(name).start()
+    ins[1].wait()
+
+    def lay_down(s, carry):
         z = lax.div(s, 4)
         g = rem(s, 4)
-        row = pl.ds(pl.multiple_of(rem(g, 2) * 64 + lax.div(g, 2) * 32, 32), 32)
-        for t in range(9):
-            cols = pl.ds(pl.multiple_of(t * 512 + z * 128, 128), 128)
-            g_gate[row, cols] = f_f[s, :, t * 128:(t + 1) * 128].astype(F32)
-            g_up[row, cols] = f_f[s, :, 1152 + t * 128:1152 + (t + 1) * 128].astype(F32)
-        c256 = pl.ds(pl.multiple_of(z * 256, 256), 256)
-        c128 = pl.ds(pl.multiple_of(z * 128, 128), 128)
-        g_q[row, c256] = f_a[s, :, 0:256].astype(F32)
-        g_k[row, c128] = f_a[s, :, 256:384].astype(F32)
-        g_v[row, c128] = f_a[s, :, 384:512].astype(F32)
-        g_out[row, c256] = f_a[s, :, 512:768].astype(F32)
         sub = rem(g, 2) * 32 + lax.div(g, 2) * 16
         for n in range(2):
             u = rem(2 * z + n - p.dp + 8, 8)
-            g_down[pl.ds(pl.multiple_of(u * 64 + sub, 16), 16), :] = f_d[s, n].astype(F32)
+            stage["g_down"][pl.ds(pl.multiple_of(u * 64 + sub, 16), 16), :] = v_d[s, n].astype(F32)
 
         @pl.when(lax.div(p.dp, 2) == z)
         def _():
-            g_down[pl.ds(pl.multiple_of(8 * 64 + sub, 16), 16), :] = f_d[s, 2].astype(F32)
+            stage["g_down"][pl.ds(pl.multiple_of(8 * 64 + sub, 16), 16), :] = v_d[s, 2].astype(F32)
 
         return carry
 
-    lax.fori_loop(0, 16, lay, 0)
-
-
-def lay_out(f_f, f_d, f_a):
+    lax.fori_loop(0, 16, lay_down, 0)
+    place("g_down").start()
+    ins[2].wait()
+
+    def lay_attn(s, carry):
+        z = lax.div(s, 4)
+        row = row_of(s)
+        c256 = pl.ds(pl.multiple_of(z * 256, 256), 256)
+        c128 = pl.ds(pl.multiple_of(z * 128, 128), 128)
+        stage["g_q"][row, c256] = v_a[s, :, 0:256].astype(F32)
+        stage["g_k"][row, c128] = v_a[s, :, 256:384].astype(F32)
+        stage["g_v"][row, c128] = v_a[s, :, 384:512].astype(F32)
+        stage["g_out"][row, c256] = v_a[s, :, 512:768].astype(F32)
+        return carry
+
+    lax.fori_loop(0, 16, lay_attn, 0)
+    for name in ("g_q", "g_k", "g_v", "g_out"):
+        place(name).start()
+    for name in PLACED:
+        place(name).wait()
+
+
+def lay_out(o):
+    hb = pl.BlockSpec(memory_space=pl.ANY)
     vm = pl.BlockSpec(memory_space=pltpu.VMEM)
-    o = pl.pallas_call(
+    small = ("g_attn", "g_ffn", "g_qg", "g_kg")
+    got = pl.pallas_call(
         lay_kernel,
-        out_shape=tuple(jax.ShapeDtypeStruct(s, F32) for s in LAID.values()),
-        in_specs=[vm] * 3,
-        out_specs=tuple(vm for _ in LAID),
-        compiler_params=pltpu.CompilerParams(vmem_limit_bytes=40 * 2**20),
+        out_shape=tuple(jax.ShapeDtypeStruct(s, d) for s, d in LAID.values()),
+        in_specs=[hb] * 3 + [vm],
+        out_specs=tuple(vm if n in small else hb for n in LAID),
+        scratch_shapes=[pltpu.VMEM(*OUTPUTS[n]) for n in ("fF", "fD", "fA")]
+        + [pltpu.VMEM(s, F32) for s in PLACED.values()]
+        + [pltpu.SemaphoreType.DMA((3,)), pltpu.SemaphoreType.DMA((len(PLACED),))],
+        compiler_params=pltpu.CompilerParams(vmem_limit_bytes=62 * 2**20),
         name="lay",
-    )(f_f, f_d, f_a)
-    return dict(zip(LAID, o))
+    )(o["fF"], o["fD"], o["fA"], o["g_small"])
+    return dict(zip(LAID, got))
 
 
 def local(
@@ -1122,11 +1218,11 @@
         )
     )
     o = dict(zip(OUTPUTS, o))
-    small = o["g_small"]
-    w = lay_out(o["fF"], o["fD"], o["fA"])
+    w = lay_out(o)
     return (
-        o["block_out"], o["input_grad"], small[0], w["g_q"], w["g_k"], w["g_v"], w["g_out"], small[1],
-        w["g_gate"], w["g_up"], w["g_down"], small[2, :64], small[3, :64],
+        o["block_out"], o["input_grad"], w["g_attn"].reshape(128), w["g_q"], w["g_k"], w["g_v"], w["g_out"],
+        w["g_ffn"].reshape(128), w["g_gate"], w["g_up"], w["g_down"], w["g_qg"].reshape(64),
+        w["g_kg"].reshape(64),
     )
 
 

time: 202 us -> 176 us (0.87)
  Pallas kernels: 190 us -> 170 us
  local copies, waits for them, and re-layouts: 9.66 us -> 2.9 us
    pallas_call x1, Pallas kernels: 185 us -> 163 us  [block(): pl.pallas_call(kernel, out_shape=tuple((jax.ShapeDtypeStruct(s, d) for s,...]
    unnamed x12 -> x6, local copies, waits for them, and re-layouts: 5.62 us -> 1.42 us
    squeeze x2 -> x0, local copies, waits for them, and re-layouts: 2.56 us -> none  [the longest x1 1.28 us: local(): small[1]]
    pallas_call x1, Pallas kernels: 4.52 us -> 6.76 us  [lay_out(): pl.pallas_call(lay_kernel, out_shape=tuple((jax.ShapeDtypeStruct(s, d) fo...]
where the time goes in v3:
time: 176 us; the launch traced here: 174 us
  Pallas kernels  170 us (97%)
  local copies, waits for them, and re-layouts  2.9 us (2%)
    pallas_call x1, Pallas kernels, block(): pl.pallas_call(kernel, out_shape=tuple((jax.ShapeDtypeStruct(s, d) for s,...  163 us
    pallas_call x1, Pallas kernels, lay_out(): pl.pallas_call(lay_kernel, out_shape=tuple((jax.ShapeDtypeStruct(s, d) fo...  6.76 us

profile of v3, /device:TPU:25, one launch (start us, length us, event | category | flops | bytes accessed | tf_op | source)
XLA Modules:
  0.0 174.0 jit_solution(15120856488348909142)
XLA Ops:
  0.6 0.7 tile.4
  1.3 0.1 stack_tile.6
  1.4 0.7 tile.5
  2.0 0.1 stack_tile.7
  2.1 0.5 pad_maximum_fusion.refs_4_
  2.7 163.1 %block.1 = (bf16[128,1024]{1,0:T(8,128)(2,1)}, bf16[128,1024]{1,0:T(8,128)(2,1)}, bf16[16,32,2304]{2,1,0:T(8,128)(2,1)}, bf16[16,3,16,1024]{3,2,1,0:T(8,128)(2,1...) custom-call(bf16[128,1024]{1,0:T(8,128)(2,1)} %refs_0_.1, s32[1,128]{1,0:T(1,128)} %refs_1_.1, bf16[1,128]{1,0:T(2,128)(2,1)} %bitcast.6, ...), custom_call_target="tpu_custom_call" | custom-call | tf_op jit(solution)/shard_map/block/pallas_call | solution.py:1080
  165.8 0.0 copy-start.1
  165.8 0.0 copy-start
  165.8 6.8 %lay.1 = (f32[1,128]{1,0:T(1,128)}, f32[1,128]{1,0:T(1,128)}, f32[1,64]{1,0:T(1,128)}, f32[1,64]{1,0:T(1,128)}, f32[128,4608]{1,0:T(8,128)}, /*index=5*/f32[128,...) custom-call(bf16[16,32,2304]{2,1,0:T(8,128)(2,1)} %get-tuple-element, ...), custom_call_target="tpu_custom_call" | custom-call | tf_op jit(solution)/shard_map/lay/pallas_call | solution.py:1193
  172.6 0.0 copy-done.1
  172.6 0.7 copy.30
  173.3 0.0 copy-done
  173.3 0.7 copy.31
Async XLA Ops:
  165.8 6.8 %copy-start.1 = (bf16[128,1024]{1,0:T(8,128)(2,1)S(1)}, bf16[128,1024]{1,0:T(8,128)(2,1)}, u32[]{:S(2)}) copy-start(bf16[128,1024]{1,0:T(8,128)(2,1)} %get-tuple-element.60) | copy-start | bytes 786436
  165.8 7.5 %copy-start = (bf16[128,1024]{1,0:T(8,128)(2,1)S(1)}, bf16[128,1024]{1,0:T(8,128)(2,1)}, u32[]{:S(2)}) copy-start(bf16[128,1024]{1,0:T(8,128)(2,1)} %get-tuple-element.61) | copy-start | bytes 786436

commit v4 on v3

--- a/solution.py
+++ b/solution.py
@@ -98,7 +98,7 @@
     ]
 
 
-INPUTS = ["tok", "seg", "ga", "gf", "gqk", "freq", "wq", "wk", "wv", "wo", "wg", "wu", "wd", "cot"]
+INPUTS = ["tok", "seg", "ga", "gf", "gq", "gk", "freq", "wq", "wk", "wv", "wo", "wg", "wu", "wd", "cot"]
 OUTPUTS = {
     "block_out": ((128, 1024), BF),
     "input_grad": ((128, 1024), BF),
@@ -458,8 +458,8 @@
     w_qkv.done()
 
     wfull = r.wqkv[...].reshape(1024, 512)
-    qg = r.gqk[0:1, :].astype(F32)
-    kg = r.gqk[1:2, :].astype(F32)
+    qg = jnp.concatenate([r.gq[...].astype(F32)] * 2, axis=1)
+    kg = jnp.concatenate([r.gk[...].astype(F32)] * 2, axis=1)
     i_kv = m.take()
     i_kvx = m.take(4)
     i_kvf = m.take()
@@ -486,6 +486,8 @@
         m.part(r.kv.at[i], r.kv.at[i], i_kv, p.sib())
 
     project(0, r.tok[...])
+    for k in (0, 1, 3, 2):
+        w_o.along_x(k)
     for dz in (1, 3, 2):
         m.got(r.tok_all.at[dz], i_tok + dz)
         project(dz, r.tok_all[dz])
@@ -494,9 +496,8 @@
         m.part(r.cot, r.cot_all.at[dz], i_cot, p.zpeer(dz))
     m.whole(r.cot_all.at[1:4], i_cot)
     r.cot_all[0] = r.cot[...]
-    for w in (w_o, w_d):
-        for k in (0, 1, 3, 2):
-            w.along_x(k)
+    for k in (0, 1, 3, 2):
+        w_d.along_x(k)
     gs = p.g + 1 - 2 * p.c
     gx = (1 - p.xh) * 2 + p.c
     gxs = (1 - p.xh) * 2 + 1 - p.c
@@ -504,6 +505,8 @@
         zz = 4 * z_of(dz)
         m.got(r.kv.at[zz + gx], i_kvx + dz)
         m.part(r.kv.at[zz + gx], r.kv.at[zz + gx], i_kvf, p.sib())
+    for k in (0, 1, 3, 2):
+        w_g.along_x(k)
     four = r.kv.at[0:4]
     for i in (i_kv, i_kvf):
         m.whole(four, i)
@@ -518,6 +521,9 @@
         lax.fori_loop(0, 16, one, 0)
 
     turn(128)
+    w_o.to_core()
+    for k in (0, 1, 3, 2):
+        w_u.along_x(k)
 
     def allowed_rows(i):
         row = r.st[pl.ds(i, 1), :].astype(jnp.int32)
@@ -564,14 +570,11 @@
             m.part(r.o_s.at[dz], r.o_in.at[p.z], i_o, p.zpeer(-dz))
         else:
             r.o_in[p.z] = r.o_s[0]
-        if j in (0, 2):
-            for k in (0, 1, 3, 2):
-                (w_g, None, w_u)[j].along_x(k)
         if j == 1:
-            w_o.to_core()
+            w_d.to_core()
     m.whole(r.o_in.at[0:3], i_o)
 
-    w_d.to_core()
+    w_g.to_core()
     m.got(r.o_in.at[0:3], i_o)
     for j in range(4):
         r.o_own[:, j * 256:(j + 1) * 256] = r.o_in[j]
@@ -591,7 +594,6 @@
     r.o_full[0] = r.o_own[...]
 
     turn(0)
-    w_g.to_core()
     w_u.to_core()
     m.got(r.cot_all.at[1:4], i_cot)
     w_d.done()
@@ -630,29 +632,37 @@
             return carry
 
         lax.fori_loop(0, 3, ffn_tile, 0)
+
+    i_r1 = m.take(4)
+    h2t = r.h2[...].reshape(512, 1024)
+
+    def gate_tile(t, carry):
+        w = r.dg[:, :, cols384(t)].reshape(512, 384)
+        r.gF[:, :, :, cols384(t)] = dot(h2t, w, TN).astype(BF).reshape(4, 2, 128, 384)
+        return carry
+
+    def up_tile(t, carry):
+        w = r.du[:, :, cols384(t)].reshape(512, 384)
+        r.gF[:, :, :, cols384(t + 3)] = dot(h2t, w, TN).astype(BF).reshape(4, 2, 128, 384)
+        return carry
+
+    lax.fori_loop(0, 3, gate_tile, 0)
+    m.send(r.gF.at[:, :, other, 0:1152], r.r1F.at[:, :, :, 0:1152], i_r1, p.sib())
+    lax.fori_loop(0, 3, up_tile, 0)
+    m.send(r.gF.at[:, :, other, 1152:2304], r.r1F.at[:, :, :, 1152:2304], i_r1 + 3, p.sib())
+    for pair in (1, 0):
+        two = slice(2 * pair, 2 * pair + 2)
         part = dot(r.dg[two].reshape(256, 1152), r.wg_v[...].reshape(1024, 1152), NT)
         part += dot(r.du[two].reshape(256, 1152), r.wu_v[...].reshape(1024, 1152), NT)
-        if pair == 0:
-            r.own[...] = part[0:128]
-            r.p2s[0] = part[128:256].astype(BF)
-            m.part(r.p2s.at[0], r.p2r.at[0], i_p2, p.zpeer(-1))
-        else:
+        if pair:
             r.p2s[1] = part[0:128].astype(BF)
             m.part(r.p2s.at[1], r.p2r.at[1], i_p2, p.zpeer(-2))
             r.p2s[2] = part[128:256].astype(BF)
             m.part(r.p2s.at[2], r.p2r.at[2], i_p2, p.zpeer(-3))
-
-    i_r1 = m.take(3)
-    h2t = r.h2[...].reshape(512, 1024)
-
-    def gate_up_tile(t, carry):
-        cols = cols384(t)
-        r.gF[:, :, :, cols] = dot(h2t, r.dg[:, :, cols].reshape(512, 384), TN).astype(BF).reshape(4, 2, 128, 384)
-        r.gF[:, :, :, cols384(t + 3)] = dot(h2t, r.du[:, :, cols].reshape(512, 384), TN).astype(BF).reshape(4, 2, 128, 384)
-        return carry
-
-    lax.fori_loop(0, 3, gate_up_tile, 0)
-    m.send(r.gF.at[:, :, other], r.r1F, i_r1, p.sib())
+        else:
+            r.p2s[0] = part[128:256].astype(BF)
+            m.part(r.p2s.at[0], r.p2r.at[0], i_p2, p.zpeer(-1))
+            r.own[...] = part[0:128]
 
     def down_tile(t, carry):
         w = r.mixed[:, :, cols384(t)].reshape(512, 384)
@@ -661,6 +671,108 @@
 
     lax.fori_loop(0, 3, down_tile, 0)
     m.send(r.gD.at[:, o32], r.r1D, i_r1 + 1, p.sib())
+
+    m.got(r.r1F.at[:, :, :, 0:1152], i_r1)
+    m.got(r.r1F.at[:, :, :, 1152:2304], i_r1 + 3)
+
+    def add_core(d, carry):
+        a, b = lax.div(d, 2), rem(d, 2)
+        r.r1F[a, b] = (r.r1F[a, b].astype(F32) + r.gF[a, b, half].astype(F32)).astype(BF)
+        return carry
+
+    lax.fori_loop(0, 8, add_core, 0)
+
+    def rows_of(x, n):
+        return pl.ds(pl.multiple_of(x * n, n), n)
+
+    class XFirst:
+        def __init__(self, src, mid1, tot, mid2):
+            self.src, self.mid1, self.tot, self.mid2 = src, mid1, tot, mid2
+            self.i1, self.i2 = m.take(), m.take()
+
+        def one(self):
+            for t in (3, 1, 2):
+                m.part(self.src(t), self.mid1.at[t - 1], self.i1, p.xring(t))
+            m.whole(self.mid1, self.i1)
+
+        def two(self):
+            m.got(self.mid1, self.i1)
+
+            def add(n, carry):
+                v = self.src(0).at[n][...].astype(F32)
+                for t in range(3):
+                    v = v + self.mid1[t, n].astype(F32)
+                self.tot[n] = v.astype(BF)
+                return carry
+
+            lax.fori_loop(0, 4, add, 0)
+            for k in (2, 1, 3):
+                m.part(self.tot.at[rem(p.y + k, 4)], self.mid2.at[k - 1], self.i2, p.ypeer(k))
+            m.whole(self.mid2, self.i2)
+
+        def sum(self):
+            m.got(self.mid2, self.i2)
+            v = self.tot[p.y].astype(F32)
+            for k in range(3):
+                v = v + self.mid2[k].astype(F32)
+            return v.astype(BF)
+
+    class YFirst:
+        def __init__(self, src, part, mid1, tot, mid2):
+            self.src, self.part, self.mid1, self.tot, self.mid2 = src, part, mid1, tot, mid2
+            self.i1, self.i2 = m.take(), m.take()
+
+        def one(self):
+            for k in (2, 1, 3):
+                m.part(self.src(rem(p.y + k, 4)), self.mid1.at[k - 1], self.i1, p.ypeer(k))
+            m.whole(self.mid1, self.i1)
+
+        def two(self):
+            m.got(self.mid1, self.i1)
+
+            def add(n, carry):
+                v = self.src(p.y).at[n][...].astype(F32)
+                for k in range(3):
+                    v = v + self.mid1[k, n].astype(F32)
+                self.tot[n] = v.astype(BF)
+                return carry
+
+            lax.fori_loop(0, 2, add, 0)
+            for t in (3, 1, 2):
+                m.part(self.part(self.tot, t), self.mid2.at[t - 1], self.i2, p.xring(t))
+            m.whole(self.mid2, self.i2)
+
+        def sum(self):
+            m.got(self.mid2, self.i2)
+            v = self.part(self.tot, 0)[...].astype(F32)
+            for t in range(3):
+                v = v + self.mid2[t].astype(F32)
+            return v.astype(BF)
+
+    def rows_x(buf, c0, c1):
+        return lambda t: buf.at[:, p.xplace(t)[0], rows_of(p.xplace(t)[1], 32), c0:c1]
+
+    def rows_y(buf, c0, c1):
+        return lambda y: buf.at[y, :, :, c0:c1]
+
+    def part_y(tot, t):
+        xl, xh = p.xplace(t)
+        return tot.at[xl, rows_of(xh, 32)]
+
+    def part_d(tot, t):
+        xl, xh = p.xplace(t)
+        return tot.at[xl, :, rows_of(xh, 16)]
+
+    sums = [
+        XFirst(rows_x(r.r1F, 0, 1152), r.ax, r.at, r.ay),
+        YFirst(rows_y(r.r1F, 1152, 2304), part_y, r.by, r.bt, r.bx),
+        XFirst(
+            lambda t: r.sD.at[:, p.xplace(t)[0], :, rows_of(p.xplace(t)[1], 16), 0:512], r.adx, r.adt, r.ady
+        ),
+        YFirst(lambda y: r.sD.at[y, :, :, :, 512:1024], part_d, r.bdy, r.bdt, r.bdx),
+    ]
+    for e in sums[0:2]:
+        e.one()
     r.own3[...] = dot(r.mixed[0], wd)
 
     def out_chunk(dz, carry):
@@ -668,6 +780,31 @@
         return carry
 
     lax.fori_loop(1, 4, out_chunk, 0)
+    m.got(r.r1D, i_r1 + 1)
+
+    def add_core_down(d, carry):
+        a, b = lax.div(d, 2), rem(d, 2)
+        where, more = down_pieces(d)
+        for n in range(2):
+            t = where[n][1]
+            r.sD[a, b, n] = (r.r1D[t].astype(F32) + r.gD[t, h32].astype(F32)).astype(BF)
+
+        @pl.when(more)
+        def _():
+            t = where[2][1]
+            r.sX[b] = (r.r1D[t].astype(F32) + r.gD[t, h32].astype(F32)).astype(BF)
+
+        return carry
+
+    lax.fori_loop(0, 8, add_core_down, 0)
+    for e in sums[2:4]:
+        e.one()
+    i_x1 = m.take()
+    i_x2 = m.take()
+    for t in (3, 1, 2):
+        xl, xh = p.xplace(t)
+        m.part(r.sX.at[xl, rows_of(xh, 16)], r.xx.at[t - 1], i_x1, p.xring(t))
+    m.whole(r.xx, i_x1)
 
     m.whole(r.p2s, i_p2)
     m.got(r.p2r, i_p2)
@@ -679,14 +816,17 @@
     dmid = r.cot[...].astype(F32) + r2 * wdh - middle * (r2 * r2 * r2) * jnp.mean(wdh * middle, axis=1, keepdims=True)
     r.dmid[...] = dmid
     r.da[...] = dmid.astype(BF)
-    r.dob[...] = dot(r.da[...], r.wo_v[...].reshape(1024, 1024), NT).astype(BF)
     i_do = m.take()
 
     def zcols(z):
         return pl.ds(pl.multiple_of(z * 256, 256), 256)
 
-    for dz in (2, 1, 3):
-        m.part(r.dob.at[:, zcols(rem(p.z + dz, 4))], r.do_all.at[dz], i_do, p.zpeer(dz))
+    for dz in (2, 1, 3, 0):
+        zz = rem(p.z + dz, 4)
+        w = r.wo_v[pl.ds(2 * zz, 2)].reshape(256, 1024)
+        r.dob[:, zcols(zz)] = dot(r.da[...], w, NT).astype(BF)
+        if dz:
+            m.part(r.dob.at[:, zcols(zz)], r.do_all.at[dz], i_do, p.zpeer(dz))
     m.whole(r.do_all.at[1:4], i_do)
     r.do_all[0] = r.dob[:, zq]
     i_p3 = m.take()
@@ -699,130 +839,20 @@
     m.whole(r.p3s, i_p3)
     r.da_c[0] = r.da[:, zq]
 
-    m.got(r.r1F, i_r1)
-    m.got(r.r1D, i_r1 + 1)
-
-    def add_core(d, carry):
-        a, b = lax.div(d, 2), rem(d, 2)
-        r.r1F[a, b] = (r.r1F[a, b].astype(F32) + r.gF[a, b, half].astype(F32)).astype(BF)
-        where, more = down_pieces(d)
-        for n in range(2):
-            t = where[n][1]
-            r.sD[a, b, n] = (r.r1D[t].astype(F32) + r.gD[t, h32].astype(F32)).astype(BF)
-
-        @pl.when(more)
-        def _():
-            t = where[2][1]
-            r.sX[b] = (r.r1D[t].astype(F32) + r.gD[t, h32].astype(F32)).astype(BF)
-
-        return carry
-
-    lax.fori_loop(0, 8, add_core, 0)
-
-    def rows_of(x, n):
-        return pl.ds(pl.multiple_of(x * n, n), n)
-
-    class XFirst:
-        def __init__(self, src, mid1, tot, mid2):
-            self.src, self.mid1, self.tot, self.mid2 = src, mid1, tot, mid2
-            self.i1, self.i2 = m.take(), m.take()
-
-        def one(self):
-            for t in (3, 1, 2):
-                m.part(self.src(t), self.mid1.at[t - 1], self.i1, p.xring(t))
-            m.whole(self.mid1, self.i1)
-
-        def two(self):
-            m.got(self.mid1, self.i1)
-
-            def add(n, carry):
-                v = self.src(0).at[n][...].astype(F32)
-                for t in range(3):
-                    v = v + self.mid1[t, n].astype(F32)
-                self.tot[n] = v.astype(BF)
-                return carry
-
-            lax.fori_loop(0, 4, add, 0)
-            for k in (2, 1, 3):
-                m.part(self.tot.at[rem(p.y + k, 4)], self.mid2.at[k - 1], self.i2, p.ypeer(k))
-            m.whole(self.mid2, self.i2)
-
-        def sum(self):
-            m.got(self.mid2, self.i2)
-            v = self.tot[p.y].astype(F32)
-            for k in range(3):
-                v = v + self.mid2[k].astype(F32)
-            return v.astype(BF)
-
-    class YFirst:
-        def __init__(self, src, part, mid1, tot, mid2):
-            self.src, self.part, self.mid1, self.tot, self.mid2 = src, part, mid1, tot, mid2
-            self.i1, self.i2 = m.take(), m.take()
-
-        def one(self):
-            for k in (2, 1, 3):
-                m.part(self.src(rem(p.y + k, 4)), self.mid1.at[k - 1], self.i1, p.ypeer(k))
-            m.whole(self.mid1, self.i1)
-
-        def two(self):
-            m.got(self.mid1, self.i1)
-
-            def add(n, carry):
-                v = self.src(p.y).at[n][...].astype(F32)
-                for k in range(3):
-                    v = v + self.mid1[k, n].astype(F32)
-                self.tot[n] = v.astype(BF)
-                return carry
-
-            lax.fori_loop(0, 2, add, 0)
-            for t in (3, 1, 2):
-                m.part(self.part(self.tot, t), self.mid2.at[t - 1], self.i2, p.xring(t))
-            m.whole(self.mid2, self.i2)
-
-        def sum(self):
-            m.got(self.mid2, self.i2)
-            v = self.part(self.tot, 0)[...].astype(F32)
-            for t in range(3):
-                v = v + self.mid2[t].astype(F32)
-            return v.astype(BF)
-
-    def rows_x(buf, c0, c1):
-        return lambda t: buf.at[:, p.xplace(t)[0], rows_of(p.xplace(t)[1], 32), c0:c1]
-
-    def rows_y(buf, c0, c1):
-        return lambda y: buf.at[y, :, :, c0:c1]
-
-    def part_y(tot, t):
-        xl, xh = p.xplace(t)
-        return tot.at[xl, rows_of(xh, 32)]
-
-    def part_d(tot, t):
-        xl, xh = p.xplace(t)
-        return tot.at[xl, :, rows_of(xh, 16)]
-
-    sums = [
-        XFirst(rows_x(r.r1F, 0, 1152), r.ax, r.at, r.ay),
-        YFirst(rows_y(r.r1F, 1152, 2304), part_y, r.by, r.bt, r.bx),
-        XFirst(
-            lambda t: r.sD.at[:, p.xplace(t)[0], :, rows_of(p.xplace(t)[1], 16), 0:512], r.adx, r.adt, r.ady
-        ),
-        YFirst(lambda y: r.sD.at[y, :, :, :, 512:1024], part_d, r.bdy, r.bdt, r.bdx),
-    ]
-    for e in sums:
-        e.one()
-    i_x1 = m.take()
-    i_x2 = m.take()
-    for t in (3, 1, 2):
-        xl, xh = p.xplace(t)
-        m.part(r.sX.at[xl, rows_of(xh, 16)], r.xx.at[t - 1], i_x1, p.xring(t))
-    m.whole(r.xx, i_x1)
-
     r.dkv[...] = jnp.zeros_like(r.dkv)
     m.got(r.do_all.at[1:4], i_do)
+    for e in sums[0:2]:
+        e.two()
+
+    lane = lax.broadcasted_iota(jnp.int32, (1, 256), 1)
+    kscale = jnp.where(lane < 128, SCALE, 1.0)
+    i_dkv = m.take()
+    xs = (p.dp, p.z * 4 + gxs)
 
     def backward_chunk(j, carry):
-        dz = j
-        i = 4 * z_of(dz) + p.g
+        zz = 3 - j
+        dz = rem(p.z - zz + 4, 4)
+        i = 4 * zz + p.g
         row4, qi4 = allowed_rows(i)
         do = r.do_all[dz].astype(F32)
         for hd, v in enumerate(spread_heads(do[:, 0:128], do[:, 128:256])):
@@ -844,22 +874,18 @@
         nine = pl.ds(k0, 9)
         r.dkv[nine, :, 0:128] += dot(r.dsT[...], qv).reshape(9, 128, 128)
         r.dkv[nine, :, 128:256] += dot(r.pT[...], dov).reshape(9, 128, 128)
+        r.dkvb[zz] = (r.dkv[pl.ds(4 * zz, 4)] * kscale.reshape(1, 1, 256)).astype(BF)
+        m.part(r.dkvb.at[zz, gx], r.dkvr.at[1, zz], i_dkv, p.xpeer())
+        m.part(r.dkvb.at[zz, gxs], r.dkvr.at[2, zz], i_dkv, xs)
+        m.part(r.dkvb.at[zz, gs], r.dkvr.at[0, zz], i_dkv, p.sib())
         r.dqr[dz] = jnp.transpose(heads_down(dot(keys_turned(k0), r.dsT[...]) * SCALE))
         return carry
 
     lax.fori_loop(0, 4, backward_chunk, 0)
 
-    lane = lax.broadcasted_iota(jnp.int32, (1, 256), 1)
-    kscale = jnp.where(lane < 128, SCALE, 1.0)
-    r.dkvb[...] = (r.dkv[...] * kscale.reshape(1, 1, 256)).astype(BF).reshape(4, 4, 128, 256)
-    i_dkv = m.take()
-    xs = (p.dp, p.z * 4 + gxs)
-    m.part(r.dkvb.at[:, gx], r.dkvr.at[1], i_dkv, p.xpeer())
-    m.part(r.dkvb.at[:, gxs], r.dkvr.at[2], i_dkv, xs)
-    m.part(r.dkvb.at[:, gs], r.dkvr.at[0], i_dkv, p.sib())
     m.whole(r.dkvr, i_dkv)
 
-    for e in sums:
+    for e in sums[2:4]:
         e.two()
     m.got(r.xx, i_x1)
     v = r.sX[p.xl, rows_of(p.xh, 16)].astype(F32)
@@ -872,32 +898,8 @@
     def _():
         m.part(r.xt, r.xy.at[kz - 1], i_x2, (p.z * 2 + p.xl, p.sq))
 
-    m.got(r.o_full.at[1:4], i_of)
-    m.got(r.da_c.at[1:4], i_dc)
-    m.got(r.p3r, i_p3)
-    r.gA[:, :, :, 512:768] = dot(
-        r.o_full[...].reshape(512, 1024), r.da_c[...].reshape(512, 256), TN
-    ).astype(BF).reshape(4, 2, 128, 256)
-    r.block_out[...] = (
-        r.mid[...] + r.own3[...] + r.p3r[0].astype(F32) + r.p3r[1].astype(F32) + r.p3r[2].astype(F32)
-    ).astype(BF)
-
     r.oF[:, 0:1152] = sums[0].sum()
     r.oF[:, 1152:2304] = sums[1].sum()
-    r.oD[0:2, :, 0:512] = sums[2].sum()
-    r.oD[0:2, :, 512:1024] = sums[3].sum()
-
-    @pl.when(kz == 0)
-    def _():
-        v = r.xt[...].astype(F32)
-        m.got(r.xy, i_x2)
-        for k in range(3):
-            v = v + r.xy[k].astype(F32)
-        r.oD[2] = v.astype(BF)
-
-    @pl.when(kz != 0)
-    def _():
-        r.oD[2] = jnp.zeros((16, 1024), BF)
 
     def seq_at(z, g):
         return rem(z + 8, 4) * 4 + g
@@ -972,7 +974,16 @@
     ag_d = Gather(r.oD, r.fD, "x")
     ag_a = Gather(r.oA, r.fA, "zx")
     ag_f.first()
-    ag_d.first()
+
+    m.got(r.o_full.at[1:4], i_of)
+    m.got(r.da_c.at[1:4], i_dc)
+    m.got(r.p3r, i_p3)
+    r.gA[:, :, :, 512:768] = dot(
+        r.o_full[...].reshape(512, 1024), r.da_c[...].reshape(512, 256), TN
+    ).astype(BF).reshape(4, 2, 128, 256)
+    r.block_out[...] = (
+        r.mid[...] + r.own3[...] + r.p3r[0].astype(F32) + r.p3r[1].astype(F32) + r.p3r[2].astype(F32)
+    ).astype(BF)
 
     m.got(r.dkvr, i_dkv)
     sq_acc = jnp.zeros((1, 128), F32)
@@ -1009,6 +1020,22 @@
         m.part(r.p2s.at[dz - 1], r.p4r.at[dz - 1], i_p4, p.zpeer(-dz))
     m.whole(r.p2s, i_p4)
     r.own[...] = dot(r.dqkv[0], r.wqkv[...].reshape(1024, 512), NT)
+    r.oD[0:2, :, 0:512] = sums[2].sum()
+    r.oD[0:2, :, 512:1024] = sums[3].sum()
+
+    @pl.when(kz == 0)
+    def _():
+        v = r.xt[...].astype(F32)
+        m.got(r.xy, i_x2)
+        for k in range(3):
+            v = v + r.xy[k].astype(F32)
+        r.oD[2] = v.astype(BF)
+
+    @pl.when(kz != 0)
+    def _():
+        r.oD[2] = jnp.zeros((16, 1024), BF)
+
+    ag_d.first()
     m.got(r.r1A, i_r1 + 2)
     r.r1A[...] = (r.r1A[...].astype(F32) + r.gA[:, :, half].astype(F32)).astype(BF)
     sums_a = [
@@ -1080,7 +1107,7 @@
     return pl.pallas_call(
         kernel,
         out_shape=tuple(jax.ShapeDtypeStruct(s, d) for s, d in OUTPUTS.values()),
-        in_specs=[vm] * 6 + [hb] * 7 + [vm],
+        in_specs=[vm] * 7 + [hb] * 7 + [vm],
         out_specs=tuple(hb if name[0] == "f" else vm for name in OUTPUTS),
         scratch_shapes=[pltpu.VMEM(s, d) for s, d in SCRATCH.values()]
         + [pltpu.SemaphoreType.DMA((NSEM,)), pltpu.SemaphoreType.DMA((NSEM,))],
@@ -1102,6 +1129,8 @@
 }
 
 LAID = {
+    "block_out": ((128, 1024), BF),
+    "input_grad": ((128, 1024), BF),
     "g_attn": ((1, 128), F32),
     "g_ffn": ((1, 128), F32),
     "g_qg": ((1, 64), F32),
@@ -1110,7 +1139,7 @@
 }
 
 
-def lay_kernel(f_f, f_d, f_a, sm, *refs):
+def lay_kernel(f_f, f_d, f_a, b_o, i_g, sm, *refs):
     outs = dict(zip(LAID, refs[:len(LAID)]))
     v_f, v_d, v_a = refs[len(LAID):len(LAID) + 3]
     stage = dict(zip(PLACED, refs[len(LAID) + 3:len(LAID) + 3 + len(PLACED)]))
@@ -1123,6 +1152,8 @@
     ]
     for q in ins:
         q.start()
+    outs["block_out"][...] = b_o[...]
+    outs["input_grad"][...] = i_g[...]
     outs["g_attn"][...] = sm[0:1, :]
     outs["g_ffn"][...] = sm[1:2, :]
     outs["g_qg"][...] = sm[2:3, 0:64]
@@ -1189,18 +1220,18 @@
 def lay_out(o):
     hb = pl.BlockSpec(memory_space=pl.ANY)
     vm = pl.BlockSpec(memory_space=pltpu.VMEM)
-    small = ("g_attn", "g_ffn", "g_qg", "g_kg")
+    small = ("block_out", "input_grad", "g_attn", "g_ffn", "g_qg", "g_kg")
     got = pl.pallas_call(
         lay_kernel,
         out_shape=tuple(jax.ShapeDtypeStruct(s, d) for s, d in LAID.values()),
-        in_specs=[hb] * 3 + [vm],
+        in_specs=[hb] * 3 + [vm] * 3,
         out_specs=tuple(vm if n in small else hb for n in LAID),
         scratch_shapes=[pltpu.VMEM(*OUTPUTS[n]) for n in ("fF", "fD", "fA")]
         + [pltpu.VMEM(s, F32) for s in PLACED.values()]
         + [pltpu.SemaphoreType.DMA((3,)), pltpu.SemaphoreType.DMA((len(PLACED),))],
         compiler_params=pltpu.CompilerParams(vmem_limit_bytes=62 * 2**20),
         name="lay",
-    )(o["fF"], o["fD"], o["fA"], o["g_small"])
+    )(o["fF"], o["fD"], o["fA"], o["block_out"], o["input_grad"], o["g_small"])
     return dict(zip(LAID, got))
 
 
@@ -1210,17 +1241,16 @@
 ):
     inverse = ROPE_BASE ** (-(np.arange(32).astype(np.float32) * np.float32(2.0) / np.float32(64)))
     freq = jnp.asarray(np.tile(inverse.astype(np.float32), 4)[None])
-    gqk = jnp.stack([jnp.tile(query_gain, 2), jnp.tile(key_gain, 2)])
     o = block(
         (
-            tokens, segment_ids, attn_gain[None], ffn_gain[None], gqk, freq, w_query, w_key, w_value,
+            tokens, segment_ids, attn_gain[None], ffn_gain[None], query_gain[None], key_gain[None], freq, w_query, w_key, w_value,
             w_out, w_gate, w_up, w_down, cotangent,
         )
     )
     o = dict(zip(OUTPUTS, o))
     w = lay_out(o)
     return (
-        o["block_out"], o["input_grad"], w["g_attn"].reshape(128), w["g_q"], w["g_k"], w["g_v"], w["g_out"],
+        w["block_out"], w["input_grad"], w["g_attn"].reshape(128), w["g_q"], w["g_k"], w["g_v"], w["g_out"],
         w["g_ffn"].reshape(128), w["g_gate"], w["g_up"], w["g_down"], w["g_qg"].reshape(64),
         w["g_kg"].reshape(64),
     )

time: 176 us -> 166 us (0.943)
  Pallas kernels: 170 us -> 162 us
  local copies, waits for them, and re-layouts: 2.9 us -> 0 us
    pallas_call x1, Pallas kernels: 163 us -> 155 us  [block(): pl.pallas_call(kernel, out_shape=tuple((jax.ShapeDtypeStruct(s, d) for s,...]
where the time goes in v4:
time: 166 us; the launch traced here: 163 us
  Pallas kernels  162 us (98%)
    pallas_call x1, Pallas kernels, block(): pl.pallas_call(kernel, out_shape=tuple((jax.ShapeDtypeStruct(s, d) for s,...  155 us
    pallas_call x1, Pallas kernels, lay_out(): pl.pallas_call(lay_kernel, out_shape=tuple((jax.ShapeDtypeStruct(s, d) fo...  7.35 us

profile of v4, /device:TPU:25, one launch (start us, length us, event | category | flops | bytes accessed | tf_op | source)
XLA Modules:
  0.0 163.3 jit_solution(11366021849774023969)
XLA Ops:
  0.7 155.1 %block.1 = (bf16[128,1024]{1,0:T(8,128)(2,1)}, bf16[128,1024]{1,0:T(8,128)(2,1)}, bf16[16,32,2304]{2,1,0:T(8,128)(2,1)}, bf16[16,3,16,1024]{3,2,1,0:T(8,128)(2,1...) custom-call(bf16[128,1024]{1,0:T(8,128)(2,1)} %refs_0_.1, s32[1,128]{1,0:T(1,128)} %refs_1_.1, bf16[1,128]{1,0:T(2,128)(2,1)} %bitcast.8, ...), custom_call_target="tpu_custom_call" | custom-call | tf_op jit(solution)/shard_map/block/pallas_call | solution.py:1107
  155.8 7.3 %lay.1 = (bf16[128,1024]{1,0:T(8,128)(2,1)}, bf16[128,1024]{1,0:T(8,128)(2,1)}, f32[1,128]{1,0:T(1,128)}, f32[1,128]{1,0:T(1,128)}, f32[1,64]{1,0:T(1,128)}, /*i...) custom-call(bf16[16,32,2304]{2,1,0:T(8,128)(2,1)} %get-tuple-element, ...), custom_call_target="tpu_custom_call" | custom-call | tf_op jit(solution)/shard_map/lay/pallas_call | solution.py:1224

commit v5 on v4

--- a/solution.py
+++ b/solution.py
@@ -505,8 +505,6 @@
         zz = 4 * z_of(dz)
         m.got(r.kv.at[zz + gx], i_kvx + dz)
         m.part(r.kv.at[zz + gx], r.kv.at[zz + gx], i_kvf, p.sib())
-    for k in (0, 1, 3, 2):
-        w_g.along_x(k)
     four = r.kv.at[0:4]
     for i in (i_kv, i_kvf):
         m.whole(four, i)
@@ -521,9 +519,9 @@
         lax.fori_loop(0, 16, one, 0)
 
     turn(128)
+    for k in (0, 1, 3, 2):
+        w_g.along_x(k)
     w_o.to_core()
-    for k in (0, 1, 3, 2):
-        w_u.along_x(k)
 
     def allowed_rows(i):
         row = r.st[pl.ds(i, 1), :].astype(jnp.int32)
@@ -571,6 +569,8 @@
         else:
             r.o_in[p.z] = r.o_s[0]
         if j == 1:
+            for k in (0, 1, 3, 2):
+                w_u.along_x(k)
             w_d.to_core()
     m.whole(r.o_in.at[0:3], i_o)
 
@@ -1046,7 +1046,6 @@
         e.one()
     ag_f.second()
     ag_d.second()
-
     for e in sums_a:
         e.two()
 
@@ -1072,17 +1071,16 @@
         m.part(r.gsm.at[rem(p.dp + k, 8)], r.gs1.at[k], i_s1, p.dpeer(k))
     m.whole(r.gs1.at[1:8], i_s1)
     r.gs1[0] = r.gsm[p.dp]
+    r.oA[:, 0:384] = sums_a[0].sum()
+    r.oA[:, 384:768] = sums_a[1].sum()
+    ag_a.first()
+    ag_f.third()
     m.got(r.gs1.at[1:8], i_s1)
     r.gs1s[...] = jnp.sum(r.gs1[...], axis=0)
     for k in range(1, 16):
         m.part(r.gs1s, r.gs2.at[k], i_s2, p.speer(k))
     m.whole(r.gs2.at[1:16], i_s2)
     r.gs2[0] = r.gs1s[...]
-
-    r.oA[:, 0:384] = sums_a[0].sum()
-    r.oA[:, 384:768] = sums_a[1].sum()
-    ag_a.first()
-    ag_f.third()
     ag_d.third()
     ag_a.second()
     m.got(r.gs2.at[1:16], i_s2)
@@ -1146,7 +1144,8 @@
     isem, osem = refs[len(LAID) + 3 + len(PLACED):]
     p = Place()
     ins = [
-        pltpu.make_async_copy(f_f, v_f, isem.at[0]),
+        pltpu.make_async_copy(f_f.at[:, :, 0:1152], v_f.at[:, :, 0:1152], isem.at[0]),
+        pltpu.make_async_copy(f_f.at[:, :, 1152:2304], v_f.at[:, :, 1152:2304], isem.at[3]),
         pltpu.make_async_copy(f_d, v_d, isem.at[1]),
         pltpu.make_async_copy(f_a, v_a, isem.at[2]),
     ]
@@ -1167,19 +1166,22 @@
         g = rem(s, 4)
         return pl.ds(pl.multiple_of(rem(g, 2) * 64 + lax.div(g, 2) * 32, 32), 32)
 
-    ins[0].wait()
-    for name, base in (("g_gate", 0), ("g_up", 1152)):
-
-        def lay(s, carry):
-            z = lax.div(s, 4)
-            for t in range(9):
-                cols = pl.ds(pl.multiple_of(t * 512 + z * 128, 128), 128)
-                stage[name][row_of(s), cols] = v_f[s, :, base + t * 128:base + (t + 1) * 128].astype(F32)
+    for name, base, q in (("g_gate", 0, ins[0]), ("g_up", 1152, ins[1])):
+        q.wait()
+
+        def lay(g, carry):
+            row = row_of(g)
+            for z in range(4):
+                for t in range(9):
+                    cols = slice(t * 512 + z * 128, t * 512 + z * 128 + 128)
+                    v = v_f[4 * z + g, :, base + t * 128:base + (t + 1) * 128]
+                    stage[name][row, cols] = v.astype(F32)
+            n = list(PLACED).index(name)
+            pltpu.make_async_copy(stage[name].at[row], outs[name].at[row], osem.at[n]).start()
             return carry
 
-        lax.fori_loop(0, 16, lay, 0)
-        place(name).start()
-    ins[1].wait()
+        lax.fori_loop(0, 4, lay, 0)
+    ins[2].wait()
 
     def lay_down(s, carry):
         z = lax.div(s, 4)
@@ -1197,7 +1199,7 @@
 
     lax.fori_loop(0, 16, lay_down, 0)
     place("g_down").start()
-    ins[2].wait()
+    ins[3].wait()
 
     def lay_attn(s, carry):
         z = lax.div(s, 4)
@@ -1228,7 +1230,7 @@
         out_specs=tuple(vm if n in small else hb for n in LAID),
         scratch_shapes=[pltpu.VMEM(*OUTPUTS[n]) for n in ("fF", "fD", "fA")]
         + [pltpu.VMEM(s, F32) for s in PLACED.values()]
-        + [pltpu.SemaphoreType.DMA((3,)), pltpu.SemaphoreType.DMA((len(PLACED),))],
+        + [pltpu.SemaphoreType.DMA((4,)), pltpu.SemaphoreType.DMA((len(PLACED),))],
         compiler_params=pltpu.CompilerParams(vmem_limit_bytes=62 * 2**20),
         name="lay",
     )(o["fF"], o["fD"], o["fA"], o["block_out"], o["input_grad"], o["g_small"])

time: 166 us -> 162 us (0.976); the launches traced: 163 us -> 162 us
  no operation moved by 1% of the time
where the time goes in v5:
time: 162 us
  Pallas kernels  161 us (99%)
    pallas_call x1, Pallas kernels, block(): pl.pallas_call(kernel, out_shape=tuple((jax.ShapeDtypeStruct(s, d) for s,...  154 us
    pallas_call x1, Pallas kernels, lay_out(): pl.pallas_call(lay_kernel, out_shape=tuple((jax.ShapeDtypeStruct(s, d) fo...  6.65 us

profile of v5, /device:TPU:25, one launch (start us, length us, event | category | flops | bytes accessed | tf_op | source)
XLA Modules:
  0.0 161.5 jit_solution(8035650870454271235)
XLA Ops:
  0.7 154.1 %block.1 = (bf16[128,1024]{1,0:T(8,128)(2,1)}, bf16[128,1024]{1,0:T(8,128)(2,1)}, bf16[16,32,2304]{2,1,0:T(8,128)(2,1)}, bf16[16,3,16,1024]{3,2,1,0:T(8,128)(2,1...) custom-call(bf16[128,1024]{1,0:T(8,128)(2,1)} %refs_0_.1, s32[1,128]{1,0:T(1,128)} %refs_1_.1, bf16[1,128]{1,0:T(2,128)(2,1)} %bitcast.8, ...), custom_call_target="tpu_custom_call" | custom-call | tf_op jit(solution)/shard_map/block/pallas_call | solution.py:1105
  154.7 6.7 %lay.1 = (bf16[128,1024]{1,0:T(8,128)(2,1)}, bf16[128,1024]{1,0:T(8,128)(2,1)}, f32[1,128]{1,0:T(1,128)}, f32[1,128]{1,0:T(1,128)}, f32[1,64]{1,0:T(1,128)}, /*i...) custom-call(bf16[16,32,2304]{2,1,0:T(8,128)(2,1)} %get-tuple-element, ...), custom_call_target="tpu_custom_call" | custom-call | tf_op jit(solution)/shard_map/lay/pallas_call | solution.py:1226

commit v6 on v5

--- a/solution.py
+++ b/solution.py
@@ -1009,10 +1009,6 @@
             wn = dn * gn
             r.dqkv[dz, :, b * 128:(b + 1) * 128] = (f * wn - v * (f * f * f) * head_mean(wn * v)).astype(BF)
         r.dqkv[dz, :, 384:512] = dkv[:, 128:256].astype(BF)
-    r.gA[:, :, :, 0:512] = dot(
-        r.tok_all[...].reshape(512, 1024), r.dqkv[...].reshape(512, 512), TN
-    ).astype(BF).reshape(4, 2, 128, 512)
-    m.send(r.gA.at[:, :, other], r.r1A, i_r1 + 2, p.sib())
     i_p4 = m.take()
     m.flush(i_p2)
     for dz in (2, 1, 3):
@@ -1020,6 +1016,10 @@
         m.part(r.p2s.at[dz - 1], r.p4r.at[dz - 1], i_p4, p.zpeer(-dz))
     m.whole(r.p2s, i_p4)
     r.own[...] = dot(r.dqkv[0], r.wqkv[...].reshape(1024, 512), NT)
+    r.gA[:, :, :, 0:512] = dot(
+        r.tok_all[...].reshape(512, 1024), r.dqkv[...].reshape(512, 512), TN
+    ).astype(BF).reshape(4, 2, 128, 512)
+    m.send(r.gA.at[:, :, other], r.r1A, i_r1 + 2, p.sib())
     r.oD[0:2, :, 0:512] = sums[2].sum()
     r.oD[0:2, :, 512:1024] = sums[3].sum()
 

time: 162 us -> 164 us (1.012)
  no operation moved by 1% of the time
where the time goes in v6:
time: 164 us; the launch traced here: 163 us
  Pallas kernels  162 us (99%)
    pallas_call x1, Pallas kernels, block(): pl.pallas_call(kernel, out_shape=tuple((jax.ShapeDtypeStruct(s, d) for s,...  155 us
    pallas_call x1, Pallas kernels, lay_out(): pl.pallas_call(lay_kernel, out_shape=tuple((jax.ShapeDtypeStruct(s, d) fo...  6.65 us

profile of v6, /device:TPU:25, one launch (start us, length us, event | category | flops | bytes accessed | tf_op | source)
XLA Modules:
  0.0 162.6 jit_solution(12399309131265233485)
XLA Ops:
  0.7 155.1 %block.1 = (bf16[128,1024]{1,0:T(8,128)(2,1)}, bf16[128,1024]{1,0:T(8,128)(2,1)}, bf16[16,32,2304]{2,1,0:T(8,128)(2,1)}, bf16[16,3,16,1024]{3,2,1,0:T(8,128)(2,1...) custom-call(bf16[128,1024]{1,0:T(8,128)(2,1)} %refs_0_.1, s32[1,128]{1,0:T(1,128)} %refs_1_.1, bf16[1,128]{1,0:T(2,128)(2,1)} %bitcast.8, ...), custom_call_target="tpu_custom_call" | custom-call | tf_op jit(solution)/shard_map/block/pallas_call | solution.py:1105
  155.8 6.7 %lay.1 = (bf16[128,1024]{1,0:T(8,128)(2,1)}, bf16[128,1024]{1,0:T(8,128)(2,1)}, f32[1,128]{1,0:T(1,128)}, f32[1,128]{1,0:T(1,128)}, f32[1,64]{1,0:T(1,128)}, /*i...) custom-call(bf16[16,32,2304]{2,1,0:T(8,128)(2,1)} %get-tuple-element, ...), custom_call_target="tpu_custom_call" | custom-call | tf_op jit(solution)/shard_map/lay/pallas_call | solution.py:1226
